TPU v7x, 32 devices: a whole 2x2x4 slice. The times are simulated.
32 devices in a mesh: lm: 8 (over y, x, core), cam: 4 (over z).
Axes of the slice: x: 2, y: 2, z: 4, core: 2. Of those that a mesh axis runs over, the one named last changes fastest.
Arguments:
- panels: bfloat16 [64, 16, 64, 384], P(('lm', 'cam')), may hold values from -0.59765625 to 0.59765625
- curvature: float32 [3, 3, 8192], P(None, None, ('lm', 'cam')), as said below
- visible_blocks: int32 [64, 16], P(('lm', 'cam')), may hold values from 0 to 31, as said below
- counts: int32 [64], P(('lm', 'cam')), may hold values from 2 to 16
- camera_hessian: float32 [32, 64, 64], P('lm'), may hold values from -6 to 6
Outputs:
- reduced_system: float32 [2048, 2048], P('lm', 'cam')
Inputs may be any that keep to these rules, and one draw needn't show every extreme that they name: `visible_blocks`: the 16 ids of a tile are distinct and lie in a window of 16 consecutive camera blocks, counted cyclically. `curvature`: each landmark's block is symmetric and strictly diagonally dominant.
All inputs are finite; a program needn't handle non-finite values.
Results may differ from a plain program's by a relative error of at most 0.0003.
Values may be sent and summed in bfloat16 or wider, within the bound.
No kernel may reach another device: no remote copies, remote signals or barrier semaphores. Data moves between devices by JAX's collectives and lax.ppermute only.
A program may use at most 128 MiB of HBM per device.

v0:
```python
import functools
import math

import jax
import jax.numpy as jnp
from jax import lax
from jax.experimental import pallas as pl
from jax.experimental.pallas import tpu as pltpu
from jax.sharding import PartitionSpec as P

CB = 64
LMB = 128
K = 16
WIDTH = 3 * LMB
STRIP = 16
LANES = 128
CHUNK = 512
VMEM = pl.BlockSpec(memory_space=pltpu.VMEM)
SMEM = pl.BlockSpec(memory_space=pltpu.SMEM)
PARAMS = pltpu.CompilerParams(vmem_limit_bytes=32 * 1024 * 1024)


def invert_rows(cur_ref, start):
    lanes = pl.ds(start, LMB)
    entry = [[cur_ref[row, col : col + 1, lanes] for col in range(3)] for row in range(3)]
    cofactor = [
        [
            entry[(row + 1) % 3][(col + 1) % 3] * entry[(row + 2) % 3][(col + 2) % 3]
            - entry[(row + 1) % 3][(col + 2) % 3] * entry[(row + 2) % 3][(col + 1) % 3]
            for col in range(3)
        ]
        for row in range(3)
    ]
    determ = (
        entry[0][0] * cofactor[0][0] + entry[0][1] * cofactor[0][1] + entry[0][2] * cofactor[0][2]
    )
    return [[cofactor[col][row] / determ for col in range(3)] for row in range(3)]


def encode(dst, lanes, parts):
    blocks = len(parts)
    row = lax.broadcasted_iota(jnp.int32, (8, LANES), 0)
    tops = jnp.full((8, LANES), 2.0**-100, jnp.float32)
    for block, part in enumerate(parts):
        top = jnp.max(jnp.abs(part), axis=0, keepdims=True)
        tops = jnp.where(row == block, jnp.maximum(top, tops), tops)
    power = jnp.ceil(jnp.log2(tops) - 14.99)
    inverse = jnp.exp2(-power)
    for block, part in enumerate(parts):
        coded = jnp.round(part * inverse[block : block + 1])
        dst[pl.ds(block * CB, CB), lanes] = coded.astype(jnp.int32).astype(jnp.int16)
    strip = jnp.concatenate([power, power], axis=0).astype(jnp.int32)
    dst[pl.ds(blocks * CB, STRIP), lanes] = strip.astype(jnp.int16)


def decode(src, lanes, blocks):
    strip = src[pl.ds(blocks * CB, STRIP), lanes].astype(jnp.int32).astype(jnp.float32)
    scale = jnp.exp2(strip)
    return [
        src[pl.ds(block * CB, CB), lanes].astype(jnp.int32).astype(jnp.float32)
        * scale[block : block + 1]
        for block in range(blocks)
    ]


def gathered(keep, came, lanes, blocks):
    parts = [keep[pl.ds(block * CB, CB), lanes] for block in range(blocks)]
    for src in came:
        parts = [part + other for part, other in zip(parts, decode(src, lanes, blocks))]
    return parts


def spot_of(index, order):
    bits = len(order)
    return sum(((index >> (bits - 1 - pos)) & 1) << bit for pos, bit in enumerate(order))


def form_kernel(total, table, pan, cur, rows):
    tiles, height, _ = rows.shape

    def one_tile(tile, carry):
        inverse = invert_rows(cur, pl.multiple_of(tile * LMB, LMB))

        def one_place(place, carry):
            slot = table[tile, total + place]
            lines = pl.ds(pl.multiple_of(place * CB, CB), CB)

            @pl.when(slot >= 0)
            def form():
                wide = pan[tile, slot].astype(jnp.float32)
                split = [wide[:, c * LMB : (c + 1) * LMB] for c in range(3)]
                for q in range(3):
                    formed = (
                        split[0] * inverse[0][q]
                        + split[1] * inverse[1][q]
                        + split[2] * inverse[2][q]
                    )
                    high = formed.astype(jnp.bfloat16)
                    low = (formed - high.astype(jnp.float32)).astype(jnp.bfloat16)
                    at = q * LMB
                    rows[tile, lines, at : at + LMB] = high
                    rows[tile, lines, WIDTH + at : WIDTH + at + LMB] = low

            @pl.when(slot < 0)
            def blank():
                rows[tile, lines, :] = jnp.zeros((CB, 2 * WIDTH), jnp.bfloat16)

            return carry

        return lax.fori_loop(0, height // CB, one_place, carry)

    lax.fori_loop(0, tiles, one_tile, 0)


def piece_kernel(plan, table_a, table_b, pan_a, pan_b, rows_a, rows_b, out, right, *scratch):
    sending, base, order, total, row_blocks, halves, tiles, chunks = plan
    acc = scratch[0] if sending else out
    acc[...] = jnp.zeros_like(acc)
    spots = [spot_of(half + (halves if sending else 0), order) for half in range(halves)]
    extent = row_blocks * CB
    for table, pan, rows in ((table_a, pan_a, rows_a), (table_b, pan_b, rows_b)):

        def one_tile(tile, carry):
            used = [
                functools.reduce(
                    jnp.maximum,
                    [table[tile, total + spot * row_blocks + block] for block in range(row_blocks)],
                )
                for spot in spots
            ]

            @pl.when(functools.reduce(jnp.maximum, used) >= 0)
            def some():
                def one_chunk(chunk, carry):
                    def one_place(place, carry):
                        slot = table[tile, base + chunk * (CHUNK // CB) + place]
                        lines = pl.ds(pl.multiple_of(place * CB, CB), CB)

                        @pl.when(slot >= 0)
                        def fill():
                            panel = pan[tile, slot]
                            right[lines, :WIDTH] = panel
                            right[lines, WIDTH:] = panel

                        @pl.when(slot < 0)
                        def blank():
                            right[lines, :] = jnp.zeros((CB, 2 * WIDTH), jnp.bfloat16)

                        return carry

                    lax.fori_loop(0, CHUNK // CB, one_place, 0)
                    lanes = pl.ds(pl.multiple_of(chunk * CHUNK, CHUNK), CHUNK)
                    for half, spot in enumerate(spots):

                        @pl.when(used[half] >= 0)
                        def add():
                            acc[half, :, lanes] += lax.dot_general(
                                rows[tile, spot * extent : (spot + 1) * extent, :],
                                right[...],
                                (((1,), (1,)), ((), ())),
                                preferred_element_type=jnp.float32,
                            )

                    return carry

                lax.fori_loop(0, chunks, one_chunk, 0)

            return carry

        lax.fori_loop(0, tiles, one_tile, 0)

    if sending:

        def code(start, carry):
            lanes = pl.ds(pl.multiple_of(start * LANES, LANES), LANES)
            for half in range(halves):
                parts = [acc[half, pl.ds(block * CB, CB), lanes] for block in range(row_blocks)]
                encode(out.at[half], lanes, parts)
            return carry

        lax.fori_loop(0, out.shape[2] // LANES, code, 0)


def relay_kernel(row_blocks, keep_ref, *rest):
    dst = rest[-1].at[0]

    def code(start, carry):
        lanes = pl.ds(pl.multiple_of(start * LANES, LANES), LANES)
        came = [ref.at[0] for ref in rest[:-1]]
        encode(dst, lanes, gathered(keep_ref.at[0], came, lanes, row_blocks))
        return carry

    lax.fori_loop(0, dst.shape[1] // LANES, code, 0)


def cross_kernel(row_blocks, group, arrays, *rest):
    dsts = rest[2 * arrays :]
    for piece in range(2):
        keep = rest[piece * arrays].at[0]
        came = [ref.at[0] for ref in rest[piece * arrays + 1 : (piece + 1) * arrays]]
        for other, dst in enumerate(dsts):
            for start in range(0, group, LANES):
                lanes = pl.ds((other + 1) * group + start, LANES)
                parts = gathered(keep, came, lanes, row_blocks)
                encode(dst.at[piece], pl.ds(start, LANES), parts)


def base_kernel(plan, me_ref, wide_ref, *rest):
    turn, row_blocks, col_blocks, arrays = plan
    out_ref = rest[-1]
    group = out_ref.shape[1] // 2
    first_row = (me_ref[0] * 2 + me_ref[1]) * row_blocks
    first_col = me_ref[2] * col_blocks
    lane = lax.broadcasted_iota(jnp.int32, (CB, LANES), 1) // CB
    for piece in range(2):
        keep = rest[piece * arrays].at[0]
        came = [ref.at[0] for ref in rest[piece * arrays + 1 : (piece + 1) * arrays]]
        for start in range(0, group, LANES):
            parts = gathered(keep, came, pl.ds(start, LANES), row_blocks)
            base = first_col + ((2 * turn + piece) * group + start) // CB
            for block in range(row_blocks):
                wide = jnp.where(base + lane == first_row + block, wide_ref[block], 0.0)
                out_ref[pl.ds(block * CB, CB), pl.ds(piece * group + start, LANES)] = (
                    wide - parts[block]
                )


def finish_kernel(row_blocks, far, base_ref, *rest):
    out_ref = rest[-1]
    group = out_ref.shape[1] // 2
    for piece in range(2):
        came = [ref.at[piece] for ref in rest[:far]]
        for start in range(0, group, LANES):
            total = [0.0] * row_blocks
            for src in came:
                parts = decode(src, pl.ds(start, LANES), row_blocks)
                total = [left + right for left, right in zip(total, parts)]
            lanes = pl.ds(piece * group + start, LANES)
            for block in range(row_blocks):
                lines = pl.ds(block * CB, CB)
                out_ref[lines, lanes] = base_ref[lines, lanes] - total[block]


def body(panels, curvature, visible_blocks, counts, camera_hessian):
    tiles = panels.shape[0]
    n_lm, n_cam = lax.axis_size("lm"), lax.axis_size("cam")
    chips = n_lm // 2
    bits = int(math.log2(chips))
    row_blocks = camera_hessian.shape[0]
    extent = row_blocks * CB
    col_blocks = row_blocks * n_lm // n_cam
    turns = col_blocks * CB // (2 * LANES)
    pieces = 2 * turns
    group = col_blocks * CB // pieces
    columns = group * n_cam
    total = row_blocks * n_lm
    coded = extent + STRIP
    orders = [list(range(bits)), list(reversed(range(bits)))]
    lm, cam = lax.axis_index("lm"), lax.axis_index("cam")
    me = jnp.stack([lm // 2, lm % 2, cam]).astype(jnp.int32)

    live = jnp.arange(K, dtype=jnp.int32)[None, :] < counts[:, None]
    ids = jnp.where(live, visible_blocks, -1)

    def swap(value, bit):
        return lax.ppermute(value, "lm", [(i, i ^ (1 << bit)) for i in range(n_lm)])

    pan_other, cur_other, ids_other = swap(panels, 0), swap(curvature, 0), swap(ids, 0)
    wide = jnp.concatenate([camera_hessian, camera_hessian], axis=-1)
    per = group // CB
    slots = jnp.arange(K, dtype=jnp.int32)[None, :, None]
    places = jnp.arange(total + chips * row_blocks, dtype=jnp.int32)

    def table_of(ids):
        inner = ids % col_blocks
        spot = ((inner // per) * n_cam + ((ids // col_blocks) ^ cam)) * per + inner % per
        owner = ids // row_blocks
        line = total + ((owner // 2) ^ (lm // 2)) * row_blocks + ids % row_blocks
        spot = jnp.where(ids >= 0, spot, -1)
        line = jnp.where((ids >= 0) & (owner % 2 == lm % 2), line, -1)
        found = (spot[:, :, None] == places) | (line[:, :, None] == places)
        return jnp.max(jnp.where(found, slots, -1), axis=1)

    def form_call(table, panels, curvature):
        return pl.pallas_call(
            functools.partial(form_kernel, total),
            in_specs=[SMEM, VMEM, VMEM],
            out_specs=VMEM,
            out_shape=jax.ShapeDtypeStruct((tiles, chips * extent, 2 * WIDTH), jnp.bfloat16),
            compiler_params=PARAMS,
            name="form",
        )(table, panels, curvature)

    tables = (table_of(ids), table_of(ids_other))
    rows = (
        form_call(tables[0], panels, curvature),
        form_call(tables[1], pan_other, cur_other),
    )

    def piece_call(sending, turn, which, tables):
        height, kind = (coded, jnp.int16) if sending else (extent, jnp.float32)
        plan = (
            sending,
            (2 * turn + which) * n_cam * per,
            orders[which],
            total,
            row_blocks,
            chips // 2,
            tiles,
            columns // CHUNK,
        )
        return pl.pallas_call(
            functools.partial(piece_kernel, plan),
            in_specs=[SMEM] * 2 + [VMEM] * 4,
            out_specs=VMEM,
            out_shape=jax.ShapeDtypeStruct((chips // 2, height, columns), kind),
            scratch_shapes=[pltpu.VMEM((CHUNK, 2 * WIDTH), jnp.bfloat16)]
            + [pltpu.VMEM((chips // 2, extent, columns), jnp.float32)] * sending,
            compiler_params=PARAMS,
            name="send" if sending else "keep",
        )(*tables, panels, pan_other, *rows)

    sends, keeps = [], []
    for turn in range(turns):
        for sending, made in ((True, sends), (False, keeps)):
            made.append([piece_call(sending, turn, which, tables) for which in range(2)])
            tables = lax.optimization_barrier((tables, made[-1]))[0]

    came = [[[], []] for _ in range(turns)]
    result = None
    for turn in range(turns):
        if turn:
            first_came = [arrays[0] for arrays in came[turn - 1]]
            sends[turn] = lax.optimization_barrier((sends[turn], first_came))[0]
        for stage in range(bits):
            for piece in range(2):
                came[turn][piece].append(swap(sends[turn][piece], orders[piece][stage] + 1))
            size = chips >> (stage + 1)
            if size == 1:
                break
            for piece in range(2):
                arrays = [keeps[turn][piece]] + came[turn][piece]

                def later(half, block, size=size):
                    return (size // 2 + half, 0, block)

                sends[turn][piece] = pl.pallas_call(
                    functools.partial(relay_kernel, row_blocks),
                    grid=(size // 2, columns // CHUNK),
                    in_specs=[pl.BlockSpec((1, extent, CHUNK), later)]
                    + [pl.BlockSpec((1, coded, CHUNK), later)] * (len(arrays) - 1),
                    out_specs=pl.BlockSpec((1, coded, CHUNK), lambda half, block: (half, 0, block)),
                    out_shape=jax.ShapeDtypeStruct((size // 2, coded, columns), jnp.int16),
                    compiler_params=PARAMS,
                    name="relay",
                )(*arrays)

        near = [array for piece in range(2) for array in [keeps[turn][piece]] + came[turn][piece]]
        arrays = len(near) // 2

        def first(width):
            return [
                pl.BlockSpec((1, coded if pos % arrays else extent, width), lambda step: (0, 0, 0))
                for pos in range(2 * arrays)
            ]

        crossed = pl.pallas_call(
            functools.partial(cross_kernel, row_blocks, group, arrays),
            grid=(1,),
            in_specs=first(columns),
            out_specs=[pl.BlockSpec((2, coded, group), lambda step: (0, 0, 0))] * (n_cam - 1),
            out_shape=[jax.ShapeDtypeStruct((2, coded, group), jnp.int16)] * (n_cam - 1),
            compiler_params=PARAMS,
            name="cross",
        )(*near)
        far = [
            lax.ppermute(value, "cam", [(i, i ^ (pos + 1)) for i in range(n_cam)])
            for pos, value in enumerate(crossed)
        ]
        base = pl.pallas_call(
            functools.partial(base_kernel, (turn, row_blocks, col_blocks, arrays)),
            grid=(1,),
            in_specs=[SMEM, VMEM] + first(group),
            out_specs=pl.BlockSpec((extent, 2 * group), lambda step: (0, 0)),
            out_shape=jax.ShapeDtypeStruct((extent, 2 * group), jnp.float32),
            compiler_params=PARAMS,
            name="base",
        )(me, wide, *near)
        before = [] if result is None else [result]
        result = pl.pallas_call(
            functools.partial(finish_kernel, row_blocks, n_cam - 1),
            grid=(1,),
            in_specs=[VMEM] * n_cam + [pl.BlockSpec(memory_space=pl.ANY)] * len(before),
            out_specs=pl.BlockSpec((extent, 2 * group), lambda step, turn=turn: (0, turn)),
            out_shape=jax.ShapeDtypeStruct((extent, col_blocks * CB), jnp.float32),
            input_output_aliases={n_cam: 0} if before else {},
            compiler_params=PARAMS,
            name="finish",
        )(base, *far, *before)
    return result


def solution(mesh):
    return jax.shard_map(
        body,
        mesh=mesh,
        in_specs=(
            P(("lm", "cam"), None, None, None),
            P(None, None, ("lm", "cam")),
            P(("lm", "cam"), None),
            P(("lm", "cam")),
            P("lm", None, None),
        ),
        out_specs=P("lm", "cam"),
        check_vma=False,
    )
```

profile of v0, /device:TPU:0, one launch (start us, length us, event | category | flops | bytes accessed | tf_op | source)
XLA Modules:
  0.0 82.9 jit_solution(11671889145873314668)
XLA Ops:
  0.0 0.5 collective-permute-start.1
  0.5 0.8 fusion.3
  1.2 0.1 collective-permute-start
  1.3 0.5 collective-permute-start.2
  1.8 0.1 select_reduce_fusion.1.table.table_a
  1.9 0.0 copy-start
  1.9 1.4 %copy-done = bf16[2,16,64,384]{3,2,1,0:T(8,128)(2,1)S(1)} copy-done((bf16[2,16,64,384]{3,2,1,0:T(8,128)(2,1)S(1)}, bf16[2,16,64,384]{3,2,1,0:T(8,128)(2,1)}, u32[]{:S(2)}) %copy-start) | copy-done | bytes 1572888
  3.3 0.7 copy-done.2
  4.0 1.9 %form.2.rows_a = bf16[2,1024,768]{2,1,0:T(8,128)(2,1)S(1)} custom-call(s32[2,48]{1,0:T(2,128)S(1)} %select_reduce_fusion.1.table.table_a, bf16[2,16,64,384]{3,2,1,0:T(8,128)(2,1)S(1)} %copy-done, f32[3,3,256]{2,1,0:T(4,128)S(1)} %copy-done.2), custom_call_target="tpu_custom_call" | custom-call | tf_op jit(solution)/shard_map/form/pallas_call | solution.py:285
  5.9 0.0 copy-start.1
  5.9 0.0 collective-permute-done
  6.0 0.1 select_reduce_fusion.table.table_b
  6.0 0.0 collective-permute-done.2.cur
  6.1 0.0 collective-permute-done.1.pan.pan_b
  6.1 1.8 %form.3.rows_b = bf16[2,1024,768]{2,1,0:T(8,128)(2,1)S(1)} custom-call(s32[2,48]{1,0:T(2,128)S(1)} %select_reduce_fusion.table.table_b, bf16[2,16,64,384]{3,2,1,0:T(8,128)(2,1)S(1)} %collective-permute-done.1.pan.pan_b, f32[3,3,256]{2,1,0:T(4,128)S(1)} %collective-permute-done.2.cur), custom_call_target="tpu_custom_call" | custom-call | tf_op jit(solution)/shard_map/form/pallas_call | solution.py:285
  7.8 3.7 %send.5 = s16[2,272,512]{2,1,0:T(8,128)(2,1)S(1)} custom-call(s32[2,48]{1,0:T(2,128)S(1)} %select_reduce_fusion.1.table.table_a, s32[2,48]{1,0:T(2,128)S(1)} %select_reduce_fusion.table.table_b, bf16[2,16,64,384]{3,2,1,0:T(8,128)(2,1)S(1)} %copy-done.1, bf16[2,16,64,384]{3,2,1,0:T(8,128)(2,1)S(1)} %collective-permute-done.1.pan.pan_b, ...), custom_call_target="tpu_custom_call" | custom-call | tf_op jit(solution)/shard_map/send/pallas_call | solution.py:312
  11.6 2.8 %collective-permute-start.4 = (s16[2,272,512]{2,1,0:T(8,128)(2,1)S(1)}, s16[2,272,512]{2,1,0:T(8,128)(2,1)S(1)}, u32[]{:S(2)}, u32[]{:S(2)}) collective-permute-start(s16[2,272,512]{2,1,0:T(8,128)(2,1)S(1)} %send.5), channel_id=1, source_target_pairs={{0,16},{4,20},{8,24},{12,28},{16,0},{20,4},{24,8},{28,12},{1,17},{... | collective-permute-start | bytes 1671176 | tf_op jit(solution)/shard_map/ppermute | solution.py:266
  14.4 3.9 %send.4 = s16[2,272,512]{2,1,0:T(8,128)(2,1)S(1)} custom-call(s32[2,48]{1,0:T(2,128)S(1)} %select_reduce_fusion.1.table.table_a, s32[2,48]{1,0:T(2,128)S(1)} %select_reduce_fusion.table.table_b, bf16[2,16,64,384]{3,2,1,0:T(8,128)(2,1)S(1)} %copy-done.1, bf16[2,16,64,384]{3,2,1,0:T(8,128)(2,1)S(1)} %collective-permute-done.1.pan.pan_b, ...), custom_call_target="tpu_custom_call" | custom-call | tf_op jit(solution)/shard_map/send/pallas_call | solution.py:312
  18.3 0.6 collective-permute-start.3
  18.9 3.0 %keep.5.keep_ref.rest_3_ = f32[2,256,512]{2,1,0:T(8,128)S(1)} custom-call(s32[2,48]{1,0:T(2,128)S(1)} %select_reduce_fusion.1.table.table_a, s32[2,48]{1,0:T(2,128)S(1)} %select_reduce_fusion.table.table_b, bf16[2,16,64,384]{3,2,1,0:T(8,128)(2,1)S(1)} %copy-done.1, bf16[2,16,64,384]{3,2,1,0:T(8,128)(2,1)S(1)} %collective-permute-done.1.pan.pan_b, ...), custom_call_target="tpu_custom_call" | custom-call | tf_op jit(solution)/shard_map/keep/pallas_call | solution.py:312
  21.9 3.2 %keep.4.keep_ref.rest_0_ = f32[2,256,512]{2,1,0:T(8,128)S(1)} custom-call(s32[2,48]{1,0:T(2,128)S(1)} %select_reduce_fusion.1.table.table_a, s32[2,48]{1,0:T(2,128)S(1)} %select_reduce_fusion.table.table_b, bf16[2,16,64,384]{3,2,1,0:T(8,128)(2,1)S(1)} %copy-done.1, bf16[2,16,64,384]{3,2,1,0:T(8,128)(2,1)S(1)} %collective-permute-done.1.pan.pan_b, ...), custom_call_target="tpu_custom_call" | custom-call | tf_op jit(solution)/shard_map/keep/pallas_call | solution.py:312
  25.1 3.7 %send.7 = s16[2,272,512]{2,1,0:T(8,128)(2,1)S(1)} custom-call(s32[2,48]{1,0:T(2,128)S(1)} %select_reduce_fusion.1.table.table_a, s32[2,48]{1,0:T(2,128)S(1)} %select_reduce_fusion.table.table_b, bf16[2,16,64,384]{3,2,1,0:T(8,128)(2,1)S(1)} %copy-done.1, bf16[2,16,64,384]{3,2,1,0:T(8,128)(2,1)S(1)} %collective-permute-done.1.pan.pan_b, ...), custom_call_target="tpu_custom_call" | custom-call | tf_op jit(solution)/shard_map/send/pallas_call | solution.py:312
  28.8 3.9 %send.6 = s16[2,272,512]{2,1,0:T(8,128)(2,1)S(1)} custom-call(s32[2,48]{1,0:T(2,128)S(1)} %select_reduce_fusion.1.table.table_a, s32[2,48]{1,0:T(2,128)S(1)} %select_reduce_fusion.table.table_b, bf16[2,16,64,384]{3,2,1,0:T(8,128)(2,1)S(1)} %copy-done.1, bf16[2,16,64,384]{3,2,1,0:T(8,128)(2,1)S(1)} %collective-permute-done.1.pan.pan_b, ...), custom_call_target="tpu_custom_call" | custom-call | tf_op jit(solution)/shard_map/send/pallas_call | solution.py:312
  32.7 0.0 collective-permute-done.4.rest_0_.rest_4_
  32.7 0.0 collective-permute-done.3.rest_0_.rest_1_
  32.7 1.1 %collective-permute-start.7 = (s16[2,272,512]{2,1,0:T(8,128)(2,1)S(1)}, s16[2,272,512]{2,1,0:T(8,128)(2,1)S(1)}, u32[]{:S(2)}, u32[]{:S(2)}) collective-permute-start(s16[2,272,512]{2,1,0:T(8,128)(2,1)S(1)} %send.7), channel_id=1, source_target_pairs={{0,16},{4,20},{8,24},{12,28},{16,0},{20,4},{24,8},{28,12},{1,17},{... | collective-permute-start | bytes 1671176 | tf_op jit(solution)/shard_map/ppermute | solution.py:266
  33.9 1.0 %collective-permute-start.5 = (s16[2,272,512]{2,1,0:T(8,128)(2,1)S(1)}, s16[2,272,512]{2,1,0:T(8,128)(2,1)S(1)}, u32[]{:S(2)}, u32[]{:S(2)}) collective-permute-start(s16[2,272,512]{2,1,0:T(8,128)(2,1)S(1)} %send.6), channel_id=1, source_target_pairs={{0,8},{4,12},{8,0},{12,4},{16,24},{20,28},{24,16},{28,20},{1,9},{5... | collective-permute-start | bytes 1671176 | tf_op jit(solution)/shard_map/ppermute | solution.py:266
  34.8 0.3 relay.7
  35.1 1.1 %collective-permute-start.13 = (s16[1,272,512]{2,1,0:T(8,128)(2,1)S(1)}, s16[1,272,512]{2,1,0:T(8,128)(2,1)S(1)}, u32[]{:S(2)}, u32[]{:S(2)}) collective-permute-start(s16[1,272,512]{2,1,0:T(8,128)(2,1)S(1)} %relay.7), channel_id=1, source_target_pairs={{0,8},{4,12},{8,0},{12,4},{16,24},{20,28},{24,16},{28,20},{1,9},{5... | collective-permute-start | bytes 835592 | tf_op jit(solution)/shard_map/ppermute | solution.py:266
  36.2 0.3 relay.6
  36.5 1.0 %collective-permute-start.12 = (s16[1,272,512]{2,1,0:T(8,128)(2,1)S(1)}, s16[1,272,512]{2,1,0:T(8,128)(2,1)S(1)}, u32[]{:S(2)}, u32[]{:S(2)}) collective-permute-start(s16[1,272,512]{2,1,0:T(8,128)(2,1)S(1)} %relay.6), channel_id=1, source_target_pairs={{0,16},{4,20},{8,24},{12,28},{16,0},{20,4},{24,8},{28,12},{1,17},{... | collective-permute-start | bytes 835592 | tf_op jit(solution)/shard_map/ppermute | solution.py:266
  37.6 3.0 %keep.7.keep_ref.rest_3_ = f32[2,256,512]{2,1,0:T(8,128)S(1)} custom-call(s32[2,48]{1,0:T(2,128)S(1)} %select_reduce_fusion.1.table.table_a, s32[2,48]{1,0:T(2,128)S(1)} %select_reduce_fusion.table.table_b, bf16[2,16,64,384]{3,2,1,0:T(8,128)(2,1)S(1)} %copy-done.1, bf16[2,16,64,384]{3,2,1,0:T(8,128)(2,1)S(1)} %collective-permute-done.1.pan.pan_b, ...), custom_call_target="tpu_custom_call" | custom-call | tf_op jit(solution)/shard_map/keep/pallas_call | solution.py:312
  40.5 3.2 %keep.6.keep_ref.rest_0_ = f32[2,256,512]{2,1,0:T(8,128)S(1)} custom-call(s32[2,48]{1,0:T(2,128)S(1)} %select_reduce_fusion.1.table.table_a, s32[2,48]{1,0:T(2,128)S(1)} %select_reduce_fusion.table.table_b, bf16[2,16,64,384]{3,2,1,0:T(8,128)(2,1)S(1)} %copy-done.1, bf16[2,16,64,384]{3,2,1,0:T(8,128)(2,1)S(1)} %collective-permute-done.1.pan.pan_b, ...), custom_call_target="tpu_custom_call" | custom-call | tf_op jit(solution)/shard_map/keep/pallas_call | solution.py:312
  43.7 4.6 %collective-permute-done.7.rest_0_.rest_4_ = s16[2,272,512]{2,1,0:T(8,128)(2,1)S(1)} collective-permute-done((s16[2,272,512]{2,1,0:T(8,128)(2,1)S(1)}, s16[2,272,512]{2,1,0:T(8,128)(2,1)S(1)}, u32[]{:S(2)}, u32[]{:S(2)}) %collective-permute-start.7) | collective-permute-done | bytes 557088 | tf_op jit(solution)/shard_map/ppermute | solution.py:266
  48.3 0.3 relay.5
  48.6 0.6 collective-permute-start.8
  49.2 0.0 collective-permute-done.5.rest_0_.rest_1_
  49.2 0.3 relay.4
  49.5 0.0 copy-start.3
  49.5 1.5 %collective-permute-start.6 = (s16[1,272,512]{2,1,0:T(8,128)(2,1)S(1)}, s16[1,272,512]{2,1,0:T(8,128)(2,1)S(1)}, u32[]{:S(2)}, u32[]{:S(2)}) collective-permute-start(s16[1,272,512]{2,1,0:T(8,128)(2,1)S(1)} %relay.4), channel_id=1, source_target_pairs={{0,16},{4,20},{8,24},{12,28},{16,0},{20,4},{24,8},{28,12},{1,17},{... | collective-permute-start | bytes 835592 | tf_op jit(solution)/shard_map/ppermute | solution.py:266
  51.1 4.1 %collective-permute-done.13.rest_5_ = s16[1,272,512]{2,1,0:T(8,128)(2,1)S(1)} collective-permute-done((s16[1,272,512]{2,1,0:T(8,128)(2,1)S(1)}, s16[1,272,512]{2,1,0:T(8,128)(2,1)S(1)}, u32[]{:S(2)}, u32[]{:S(2)}) %collective-permute-start.13) | collective-permute-done | bytes 278560 | tf_op jit(solution)/shard_map/ppermute | solution.py:266
  55.2 0.0 collective-permute-done.12.rest_2_
  55.2 0.4 cross.3
  55.5 1.6 %collective-permute-start.14 = (s16[2,272,128]{2,1,0:T(8,128)(2,1)S(1)}, s16[2,272,128]{2,1,0:T(8,128)(2,1)S(1)}, u32[]{:S(2)}, u32[]{:S(2)}) collective-permute-start(s16[2,272,128]{2,1,0:T(8,128)(2,1)S(1)} %get-tuple-element.30), channel_id=1, source_target_pairs={{0,1},{1,0},{2,3},{3,2},{4,5},{5,4},{6,7},{7,6},{8,9},{9,8},{10,11... | collective-permute-start | bytes 417800 | tf_op jit(solution)/shard_map/ppermute | solution.py:377
  57.1 1.2 %collective-permute-start.15 = (s16[2,272,128]{2,1,0:T(8,128)(2,1)S(1)}, s16[2,272,128]{2,1,0:T(8,128)(2,1)S(1)}, u32[]{:S(2)}, u32[]{:S(2)}) collective-permute-start(s16[2,272,128]{2,1,0:T(8,128)(2,1)S(1)} %get-tuple-element.31), channel_id=1, source_target_pairs={{0,2},{1,3},{2,0},{3,1},{4,6},{5,7},{6,4},{7,5},{8,10},{9,11},{10,... | collective-permute-start | bytes 417800 | tf_op jit(solution)/shard_map/ppermute | solution.py:377
  58.3 1.7 %collective-permute-start.16 = (s16[2,272,128]{2,1,0:T(8,128)(2,1)S(1)}, s16[2,272,128]{2,1,0:T(8,128)(2,1)S(1)}, u32[]{:S(2)}, u32[]{:S(2)}) collective-permute-start(s16[2,272,128]{2,1,0:T(8,128)(2,1)S(1)} %get-tuple-element.32), channel_id=1, source_target_pairs={{0,3},{1,2},{2,1},{3,0},{4,7},{5,6},{6,5},{7,4},{8,11},{9,10},{10,... | collective-permute-start | bytes 417800 | tf_op jit(solution)/shard_map/ppermute | solution.py:377
  60.0 1.1 %collective-permute-done.8.rest_5_ = s16[1,272,512]{2,1,0:T(8,128)(2,1)S(1)} collective-permute-done((s16[1,272,512]{2,1,0:T(8,128)(2,1)S(1)}, s16[1,272,512]{2,1,0:T(8,128)(2,1)S(1)}, u32[]{:S(2)}, u32[]{:S(2)}) %collective-permute-start.8) | collective-permute-done | bytes 278560 | tf_op jit(solution)/shard_map/ppermute | solution.py:266
  61.1 0.0 collective-permute-done.6.rest_2_
  61.1 0.4 cross.2
  61.5 0.8 collective-permute-start.10
  62.3 1.1 %collective-permute-start.11 = (s16[2,272,128]{2,1,0:T(8,128)(2,1)S(1)}, s16[2,272,128]{2,1,0:T(8,128)(2,1)S(1)}, u32[]{:S(2)}, u32[]{:S(2)}) collective-permute-start(s16[2,272,128]{2,1,0:T(8,128)(2,1)S(1)} %get-tuple-element.29), channel_id=1, source_target_pairs={{0,3},{1,2},{2,1},{3,0},{4,7},{5,6},{6,5},{7,4},{8,11},{9,10},{10,... | collective-permute-start | bytes 417800 | tf_op jit(solution)/shard_map/ppermute | solution.py:377
  63.4 0.2 collective-permute-done.14.rest_0_
  63.6 1.4 %collective-permute-start.9 = (s16[2,272,128]{2,1,0:T(8,128)(2,1)S(1)}, s16[2,272,128]{2,1,0:T(8,128)(2,1)S(1)}, u32[]{:S(2)}, u32[]{:S(2)}) collective-permute-start(s16[2,272,128]{2,1,0:T(8,128)(2,1)S(1)} %get-tuple-element.27), channel_id=1, source_target_pairs={{0,1},{1,0},{2,3},{3,2},{4,5},{5,4},{6,7},{7,6},{8,9},{9,8},{10,11... | collective-permute-start | bytes 417800 | tf_op jit(solution)/shard_map/ppermute | solution.py:377
  65.1 0.1 pad_add_fusion.me_ref
  65.2 0.1 pad_maximum_fusion.wide_ref
  65.3 0.6 base.3.base_ref
  65.9 10.2 %collective-permute-done.15.rest_1_ = s16[2,272,128]{2,1,0:T(8,128)(2,1)S(1)} collective-permute-done((s16[2,272,128]{2,1,0:T(8,128)(2,1)S(1)}, s16[2,272,128]{2,1,0:T(8,128)(2,1)S(1)}, u32[]{:S(2)}, u32[]{:S(2)}) %collective-permute-start.15) | collective-permute-done | bytes 139296 | tf_op jit(solution)/shard_map/ppermute | solution.py:377
  76.2 0.0 collective-permute-done.16.rest_2_
  76.2 0.8 finish.2.rest_3_
  77.0 0.6 base.2.base_ref
  77.6 4.5 %collective-permute-done.10.rest_1_ = s16[2,272,128]{2,1,0:T(8,128)(2,1)S(1)} collective-permute-done((s16[2,272,128]{2,1,0:T(8,128)(2,1)S(1)}, s16[2,272,128]{2,1,0:T(8,128)(2,1)S(1)}, u32[]{:S(2)}, u32[]{:S(2)}) %collective-permute-start.10) | collective-permute-done | bytes 139296 | tf_op jit(solution)/shard_map/ppermute | solution.py:377
  82.1 0.0 collective-permute-done.11.rest_2_
  82.1 0.0 collective-permute-done.9.rest_0_
  82.1 0.8 finish.3
  (5 shorter events, 0.1 us)
Async XLA Ops:
  0.0 6.1 %collective-permute-start.1 = (bf16[2,16,64,384]{3,2,1,0:T(8,128)(2,1)}, bf16[2,16,64,384]{3,2,1,0:T(8,128)(2,1)S(1)}, u32[]{:S(2)}, u32[]{:S(2)}) collective-permute-start(bf16[2,16,64,384]{3,2,1,0:T(8,128)(2,1)} %pan_a.15), channel_id=1, source_target_pairs={{0,4},{4,0},{8,12},{12,8},{16,20},{20,16},{24,28},{28,24},{1,5},{5... | collective-permute-start | bytes 4718600 | tf_op jit(solution)/shard_map/ppermute | solution.py:266
  1.2 4.7 %collective-permute-start = (s32[2,16]{1,0:T(2,128)S(1)}, s32[2,16]{1,0:T(2,128)S(1)}, u32[]{:S(2)}, u32[]{:S(2)}) collective-permute-start(s32[2,16]{1,0:T(2,128)S(1)} %get-tuple-element.34), channel_id=1, source_target_pairs={{0,4},{4,0},{8,12},{12,8},{16,20},{20,16},{24,28},{28,24},{1,5},{5... | collective-permute-start | bytes 392 | tf_op jit(solution)/shard_map/ppermute | solution.py:266
  1.3 4.7 %collective-permute-start.2 = (f32[3,3,256]{2,1,0:T(4,128)}, f32[3,3,256]{2,1,0:T(4,128)S(1)}, u32[]{:S(2)}, u32[]{:S(2)}) collective-permute-start(f32[3,3,256]{2,1,0:T(4,128)} %cur.1), channel_id=1, source_target_pairs={{0,4},{4,0},{8,12},{12,8},{16,20},{20,16},{24,28},{28,24},{1,5},{5... | collective-permute-start | bytes 27656 | tf_op jit(solution)/shard_map/ppermute | solution.py:266
  1.9 1.4 %copy-start = (bf16[2,16,64,384]{3,2,1,0:T(8,128)(2,1)S(1)}, bf16[2,16,64,384]{3,2,1,0:T(8,128)(2,1)}, u32[]{:S(2)}) copy-start(bf16[2,16,64,384]{3,2,1,0:T(8,128)(2,1)} %pan_a.15) | copy-start | bytes 4718596
  3.3 0.7 copy-start.2
  5.9 1.9 %copy-start.1 = (bf16[2,16,64,384]{3,2,1,0:T(8,128)(2,1)S(1)}, bf16[2,16,64,384]{3,2,1,0:T(8,128)(2,1)}, u32[]{:S(2)}) copy-start(bf16[2,16,64,384]{3,2,1,0:T(8,128)(2,1)} %pan_a.15) | copy-start | bytes 4718596
  11.6 21.2 %collective-permute-start.4 = (s16[2,272,512]{2,1,0:T(8,128)(2,1)S(1)}, s16[2,272,512]{2,1,0:T(8,128)(2,1)S(1)}, u32[]{:S(2)}, u32[]{:S(2)}) collective-permute-start(s16[2,272,512]{2,1,0:T(8,128)(2,1)S(1)} %send.5), channel_id=1, source_target_pairs={{0,16},{4,20},{8,24},{12,28},{16,0},{20,4},{24,8},{28,12},{1,17},{... | collective-permute-start | bytes 1671176 | tf_op jit(solution)/shard_map/ppermute | solution.py:266
  18.3 14.4 %collective-permute-start.3 = (s16[2,272,512]{2,1,0:T(8,128)(2,1)S(1)}, s16[2,272,512]{2,1,0:T(8,128)(2,1)S(1)}, u32[]{:S(2)}, u32[]{:S(2)}) collective-permute-start(s16[2,272,512]{2,1,0:T(8,128)(2,1)S(1)} %send.4), channel_id=1, source_target_pairs={{0,8},{4,12},{8,0},{12,4},{16,24},{20,28},{24,16},{28,20},{1,9},{5... | collective-permute-start | bytes 1671176 | tf_op jit(solution)/shard_map/ppermute | solution.py:266
  32.7 15.6 %collective-permute-start.7 = (s16[2,272,512]{2,1,0:T(8,128)(2,1)S(1)}, s16[2,272,512]{2,1,0:T(8,128)(2,1)S(1)}, u32[]{:S(2)}, u32[]{:S(2)}) collective-permute-start(s16[2,272,512]{2,1,0:T(8,128)(2,1)S(1)} %send.7), channel_id=1, source_target_pairs={{0,16},{4,20},{8,24},{12,28},{16,0},{20,4},{24,8},{28,12},{1,17},{... | collective-permute-start | bytes 1671176 | tf_op jit(solution)/shard_map/ppermute | solution.py:266
  33.9 15.4 %collective-permute-start.5 = (s16[2,272,512]{2,1,0:T(8,128)(2,1)S(1)}, s16[2,272,512]{2,1,0:T(8,128)(2,1)S(1)}, u32[]{:S(2)}, u32[]{:S(2)}) collective-permute-start(s16[2,272,512]{2,1,0:T(8,128)(2,1)S(1)} %send.6), channel_id=1, source_target_pairs={{0,8},{4,12},{8,0},{12,4},{16,24},{20,28},{24,16},{28,20},{1,9},{5... | collective-permute-start | bytes 1671176 | tf_op jit(solution)/shard_map/ppermute | solution.py:266
  35.1 20.0 %collective-permute-start.13 = (s16[1,272,512]{2,1,0:T(8,128)(2,1)S(1)}, s16[1,272,512]{2,1,0:T(8,128)(2,1)S(1)}, u32[]{:S(2)}, u32[]{:S(2)}) collective-permute-start(s16[1,272,512]{2,1,0:T(8,128)(2,1)S(1)} %relay.7), channel_id=1, source_target_pairs={{0,8},{4,12},{8,0},{12,4},{16,24},{20,28},{24,16},{28,20},{1,9},{5... | collective-permute-start | bytes 835592 | tf_op jit(solution)/shard_map/ppermute | solution.py:266
  36.5 18.6 %collective-permute-start.12 = (s16[1,272,512]{2,1,0:T(8,128)(2,1)S(1)}, s16[1,272,512]{2,1,0:T(8,128)(2,1)S(1)}, u32[]{:S(2)}, u32[]{:S(2)}) collective-permute-start(s16[1,272,512]{2,1,0:T(8,128)(2,1)S(1)} %relay.6), channel_id=1, source_target_pairs={{0,16},{4,20},{8,24},{12,28},{16,0},{20,4},{24,8},{28,12},{1,17},{... | collective-permute-start | bytes 835592 | tf_op jit(solution)/shard_map/ppermute | solution.py:266
  48.6 12.5 %collective-permute-start.8 = (s16[1,272,512]{2,1,0:T(8,128)(2,1)S(1)}, s16[1,272,512]{2,1,0:T(8,128)(2,1)S(1)}, u32[]{:S(2)}, u32[]{:S(2)}) collective-permute-start(s16[1,272,512]{2,1,0:T(8,128)(2,1)S(1)} %relay.5), channel_id=1, source_target_pairs={{0,8},{4,12},{8,0},{12,4},{16,24},{20,28},{24,16},{28,20},{1,9},{5... | collective-permute-start | bytes 835592 | tf_op jit(solution)/shard_map/ppermute | solution.py:266
  49.5 15.6 %copy-start.3 = (f32[4,64,64]{2,1,0:T(8,128)S(1)}, f32[4,64,64]{2,1,0:T(8,128)}, u32[]{:S(2)}) copy-start(f32[4,64,64]{2,1,0:T(8,128)} %param.9) | copy-start | bytes 196612
  49.5 11.6 %collective-permute-start.6 = (s16[1,272,512]{2,1,0:T(8,128)(2,1)S(1)}, s16[1,272,512]{2,1,0:T(8,128)(2,1)S(1)}, u32[]{:S(2)}, u32[]{:S(2)}) collective-permute-start(s16[1,272,512]{2,1,0:T(8,128)(2,1)S(1)} %relay.4), channel_id=1, source_target_pairs={{0,16},{4,20},{8,24},{12,28},{16,0},{20,4},{24,8},{28,12},{1,17},{... | collective-permute-start | bytes 835592 | tf_op jit(solution)/shard_map/ppermute | solution.py:266
  55.5 8.1 %collective-permute-start.14 = (s16[2,272,128]{2,1,0:T(8,128)(2,1)S(1)}, s16[2,272,128]{2,1,0:T(8,128)(2,1)S(1)}, u32[]{:S(2)}, u32[]{:S(2)}) collective-permute-start(s16[2,272,128]{2,1,0:T(8,128)(2,1)S(1)} %get-tuple-element.30), channel_id=1, source_target_pairs={{0,1},{1,0},{2,3},{3,2},{4,5},{5,4},{6,7},{7,6},{8,9},{9,8},{10,11... | collective-permute-start | bytes 417800 | tf_op jit(solution)/shard_map/ppermute | solution.py:377
  57.1 19.1 %collective-permute-start.15 = (s16[2,272,128]{2,1,0:T(8,128)(2,1)S(1)}, s16[2,272,128]{2,1,0:T(8,128)(2,1)S(1)}, u32[]{:S(2)}, u32[]{:S(2)}) collective-permute-start(s16[2,272,128]{2,1,0:T(8,128)(2,1)S(1)} %get-tuple-element.31), channel_id=1, source_target_pairs={{0,2},{1,3},{2,0},{3,1},{4,6},{5,7},{6,4},{7,5},{8,10},{9,11},{10,... | collective-permute-start | bytes 417800 | tf_op jit(solution)/shard_map/ppermute | solution.py:377
  58.3 17.9 %collective-permute-start.16 = (s16[2,272,128]{2,1,0:T(8,128)(2,1)S(1)}, s16[2,272,128]{2,1,0:T(8,128)(2,1)S(1)}, u32[]{:S(2)}, u32[]{:S(2)}) collective-permute-start(s16[2,272,128]{2,1,0:T(8,128)(2,1)S(1)} %get-tuple-element.32), channel_id=1, source_target_pairs={{0,3},{1,2},{2,1},{3,0},{4,7},{5,6},{6,5},{7,4},{8,11},{9,10},{10,... | collective-permute-start | bytes 417800 | tf_op jit(solution)/shard_map/ppermute | solution.py:377
  61.5 20.6 %collective-permute-start.10 = (s16[2,272,128]{2,1,0:T(8,128)(2,1)S(1)}, s16[2,272,128]{2,1,0:T(8,128)(2,1)S(1)}, u32[]{:S(2)}, u32[]{:S(2)}) collective-permute-start(s16[2,272,128]{2,1,0:T(8,128)(2,1)S(1)} %get-tuple-element.28), channel_id=1, source_target_pairs={{0,2},{1,3},{2,0},{3,1},{4,6},{5,7},{6,4},{7,5},{8,10},{9,11},{10,... | collective-permute-start | bytes 417800 | tf_op jit(solution)/shard_map/ppermute | solution.py:377
  62.3 19.8 %collective-permute-start.11 = (s16[2,272,128]{2,1,0:T(8,128)(2,1)S(1)}, s16[2,272,128]{2,1,0:T(8,128)(2,1)S(1)}, u32[]{:S(2)}, u32[]{:S(2)}) collective-permute-start(s16[2,272,128]{2,1,0:T(8,128)(2,1)S(1)} %get-tuple-element.29), channel_id=1, source_target_pairs={{0,3},{1,2},{2,1},{3,0},{4,7},{5,6},{6,5},{7,4},{8,11},{9,10},{10,... | collective-permute-start | bytes 417800 | tf_op jit(solution)/shard_map/ppermute | solution.py:377
  63.6 18.5 %collective-permute-start.9 = (s16[2,272,128]{2,1,0:T(8,128)(2,1)S(1)}, s16[2,272,128]{2,1,0:T(8,128)(2,1)S(1)}, u32[]{:S(2)}, u32[]{:S(2)}) collective-permute-start(s16[2,272,128]{2,1,0:T(8,128)(2,1)S(1)} %get-tuple-element.27), channel_id=1, source_target_pairs={{0,1},{1,0},{2,3},{3,2},{4,5},{5,4},{6,7},{7,6},{8,9},{9,8},{10,11... | collective-permute-start | bytes 417800 | tf_op jit(solution)/shard_map/ppermute | solution.py:377
where the time goes:
time: 82.9 us
  Pallas kernels  36 us (43%)
  waiting for transfers between devices  24.8 us (30%)
  starting transfers between devices  18.6 us (22%)
  local copies, waits for them, and re-layouts  2.12 us (3%)
  other arithmetic  1.18 us (1%)
    pallas_call x8, Pallas kernels, piece_call(): pl.pallas_call(functools.partial(piece_kernel, plan), in_specs=[SMEM] * 2...  27.6 us
    ppermute x6, waiting for transfers between devices, body(): lax.ppermute(value, 'cam', [(i, i ^ pos + 1) for i in range(n_cam)])  14.9 us
    ppermute x11, starting transfers between devices, swap(): return lax.ppermute(value, 'lm', [(i, i ^ 1 << bit) for i in range(n_lm)])  10.8 us
    ppermute x11, waiting for transfers between devices, swap(): return lax.ppermute(value, 'lm', [(i, i ^ 1 << bit) for i in range(n_lm)])  9.81 us
    ppermute x6, starting transfers between devices, body(): lax.ppermute(value, 'cam', [(i, i ^ pos + 1) for i in range(n_cam)])  7.79 us
    pallas_call x2, Pallas kernels, form_call(): pl.pallas_call(functools.partial(form_kernel, total), in_specs=[SMEM, VME...  3.62 us
    unnamed x8, local copies, waits for them, and re-layouts  2.12 us
  transfers between devices with their start and end apart: 17, of which 6 were waited for; matrix products, arithmetic and copies ran while one was open for 1% of the time, Pallas kernels for 22%

commit v1 on v0

--- a/solution.py
+++ b/solution.py
@@ -75,110 +75,144 @@
     return sum(((index >> (bits - 1 - pos)) & 1) << bit for pos, bit in enumerate(order))
 
 
+def form_tile(total, table, tile, pan, cur, rows):
+    inverse = invert_rows(cur, tile * LMB)
+
+    def one_place(place, carry):
+        slot = table[tile, total + place]
+        lines = pl.ds(pl.multiple_of(place * CB, CB), CB)
+
+        @pl.when(slot >= 0)
+        def form():
+            wide = pan[tile, slot].astype(jnp.float32)
+            split = [wide[:, c * LMB : (c + 1) * LMB] for c in range(3)]
+            for q in range(3):
+                formed = (
+                    split[0] * inverse[0][q] + split[1] * inverse[1][q] + split[2] * inverse[2][q]
+                )
+                high = formed.astype(jnp.bfloat16)
+                low = (formed - high.astype(jnp.float32)).astype(jnp.bfloat16)
+                at = q * LMB
+                rows[tile, lines, at : at + LMB] = high
+                rows[tile, lines, WIDTH + at : WIDTH + at + LMB] = low
+
+        @pl.when(slot < 0)
+        def blank():
+            rows[tile, lines, :] = jnp.zeros((CB, 2 * WIDTH), jnp.bfloat16)
+
+        return carry
+
+    lax.fori_loop(0, rows.shape[1] // CB, one_place, 0)
+
+
+def form_own_kernel(total, table, pan_ref, cur_ref, rows, pan, cur, pan_sem, cur_sem):
+    tiles = rows.shape[0]
+    copies = [
+        pltpu.make_async_copy(pan_ref.at[tile], pan.at[tile], pan_sem.at[tile])
+        for tile in range(tiles)
+    ]
+    small = pltpu.make_async_copy(cur_ref, cur, cur_sem)
+    small.start()
+    for copy in copies:
+        copy.start()
+    small.wait()
+    for tile, copy in enumerate(copies):
+        copy.wait()
+        form_tile(total, table, tile, pan, cur, rows)
+
+
 def form_kernel(total, table, pan, cur, rows):
-    tiles, height, _ = rows.shape
-
-    def one_tile(tile, carry):
-        inverse = invert_rows(cur, pl.multiple_of(tile * LMB, LMB))
-
-        def one_place(place, carry):
-            slot = table[tile, total + place]
-            lines = pl.ds(pl.multiple_of(place * CB, CB), CB)
-
-            @pl.when(slot >= 0)
-            def form():
-                wide = pan[tile, slot].astype(jnp.float32)
-                split = [wide[:, c * LMB : (c + 1) * LMB] for c in range(3)]
-                for q in range(3):
-                    formed = (
-                        split[0] * inverse[0][q]
-                        + split[1] * inverse[1][q]
-                        + split[2] * inverse[2][q]
+    for tile in range(rows.shape[0]):
+        form_tile(total, table, tile, pan, cur, rows)
+
+
+def round_kernel(plan, table_a, table_b, pan_a, pan_b, rows_a, rows_b, *rest):
+    sending, bases, orders, total, row_blocks, halves, tiles, pairs = plan
+    outs, right, pair_at, acc = rest[:2], rest[2], rest[3], rest[4]
+    extent = row_blocks * CB
+    columns = pairs * LANES
+    for base, order, out in zip(bases, orders, outs):
+        acc[...] = jnp.zeros_like(acc)
+        spots = [spot_of(half + (halves if sending else 0), order) for half in range(halves)]
+        for table, pan, rows in ((table_a, pan_a, rows_a), (table_b, pan_b, rows_b)):
+
+            def one_tile(tile, carry):
+                used = [
+                    functools.reduce(
+                        jnp.maximum,
+                        [
+                            table[tile, total + spot * row_blocks + block]
+                            for block in range(row_blocks)
+                        ],
                     )
-                    high = formed.astype(jnp.bfloat16)
-                    low = (formed - high.astype(jnp.float32)).astype(jnp.bfloat16)
-                    at = q * LMB
-                    rows[tile, lines, at : at + LMB] = high
-                    rows[tile, lines, WIDTH + at : WIDTH + at + LMB] = low
-
-            @pl.when(slot < 0)
-            def blank():
-                rows[tile, lines, :] = jnp.zeros((CB, 2 * WIDTH), jnp.bfloat16)
-
-            return carry
-
-        return lax.fori_loop(0, height // CB, one_place, carry)
-
-    lax.fori_loop(0, tiles, one_tile, 0)
-
-
-def piece_kernel(plan, table_a, table_b, pan_a, pan_b, rows_a, rows_b, out, right, *scratch):
-    sending, base, order, total, row_blocks, halves, tiles, chunks = plan
-    acc = scratch[0] if sending else out
-    acc[...] = jnp.zeros_like(acc)
-    spots = [spot_of(half + (halves if sending else 0), order) for half in range(halves)]
-    extent = row_blocks * CB
-    for table, pan, rows in ((table_a, pan_a, rows_a), (table_b, pan_b, rows_b)):
-
-        def one_tile(tile, carry):
-            used = [
-                functools.reduce(
-                    jnp.maximum,
-                    [table[tile, total + spot * row_blocks + block] for block in range(row_blocks)],
-                )
-                for spot in spots
-            ]
-
-            @pl.when(functools.reduce(jnp.maximum, used) >= 0)
-            def some():
-                def one_chunk(chunk, carry):
-                    def one_place(place, carry):
-                        slot = table[tile, base + chunk * (CHUNK // CB) + place]
-                        lines = pl.ds(pl.multiple_of(place * CB, CB), CB)
-
-                        @pl.when(slot >= 0)
-                        def fill():
-                            panel = pan[tile, slot]
-                            right[lines, :WIDTH] = panel
-                            right[lines, WIDTH:] = panel
-
-                        @pl.when(slot < 0)
-                        def blank():
-                            right[lines, :] = jnp.zeros((CB, 2 * WIDTH), jnp.bfloat16)
+                    for spot in spots
+                ]
+
+                @pl.when(functools.reduce(jnp.maximum, used) >= 0)
+                def some():
+                    def one_pair(pair, count):
+                        slots = [table[tile, base + 2 * pair + side] for side in range(2)]
+                        live = jnp.maximum(slots[0], slots[1]) >= 0
+
+                        @pl.when(live)
+                        def stage():
+                            pair_at[count] = pair * LANES
+                            for side, slot in enumerate(slots):
+                                first = pl.multiple_of(count * LANES + side * CB, CB)
+                                lines = pl.ds(first, CB)
+
+                                @pl.when(slot >= 0)
+                                def fill():
+                                    panel = pan[tile, slot]
+                                    right[lines, :WIDTH] = panel
+                                    right[lines, WIDTH:] = panel
+
+                                @pl.when(slot < 0)
+                                def blank():
+                                    right[lines, :] = jnp.zeros((CB, 2 * WIDTH), jnp.bfloat16)
+
+                        return count + jnp.where(live, 1, 0)
+
+                    count = lax.fori_loop(0, pairs, one_pair, jnp.int32(0))
+                    pair_at[count] = columns
+
+                    def one_dot(double, carry):
+                        first = pl.multiple_of(double * 2 * LANES, 2 * LANES)
+                        for half, spot in enumerate(spots):
+
+                            @pl.when(used[half] >= 0)
+                            def add():
+                                result = lax.dot_general(
+                                    rows[tile, spot * extent : (spot + 1) * extent, :],
+                                    right[pl.ds(first, 2 * LANES), :],
+                                    (((1,), (1,)), ((), ())),
+                                    preferred_element_type=jnp.float32,
+                                )
+                                for side in range(2):
+                                    at = pl.multiple_of(pair_at[2 * double + side], LANES)
+                                    acc[half, :, pl.ds(at, LANES)] += result[
+                                        :, side * LANES : (side + 1) * LANES
+                                    ]
 
                         return carry
 
-                    lax.fori_loop(0, CHUNK // CB, one_place, 0)
-                    lanes = pl.ds(pl.multiple_of(chunk * CHUNK, CHUNK), CHUNK)
-                    for half, spot in enumerate(spots):
-
-                        @pl.when(used[half] >= 0)
-                        def add():
-                            acc[half, :, lanes] += lax.dot_general(
-                                rows[tile, spot * extent : (spot + 1) * extent, :],
-                                right[...],
-                                (((1,), (1,)), ((), ())),
-                                preferred_element_type=jnp.float32,
-                            )
-
-                    return carry
-
-                lax.fori_loop(0, chunks, one_chunk, 0)
-
-            return carry
-
-        lax.fori_loop(0, tiles, one_tile, 0)
-
-    if sending:
-
-        def code(start, carry):
+                    lax.fori_loop(0, (count + 1) // 2, one_dot, 0)
+
+                return carry
+
+            lax.fori_loop(0, tiles, one_tile, 0)
+
+        def store(start, carry):
             lanes = pl.ds(pl.multiple_of(start * LANES, LANES), LANES)
             for half in range(halves):
-                parts = [acc[half, pl.ds(block * CB, CB), lanes] for block in range(row_blocks)]
-                encode(out.at[half], lanes, parts)
+                if sending:
+                    parts = [acc[half, pl.ds(block * CB, CB), lanes] for block in range(row_blocks)]
+                    encode(out.at[half], lanes, parts)
+                else:
+                    out[half, :, lanes] = acc[half, :, lanes]
             return carry
 
-        lax.fori_loop(0, out.shape[2] // LANES, code, 0)
+        lax.fori_loop(0, pairs, store, 0)
 
 
 def relay_kernel(row_blocks, keep_ref, *rest):
@@ -281,49 +315,55 @@
         found = (spot[:, :, None] == places) | (line[:, :, None] == places)
         return jnp.max(jnp.where(found, slots, -1), axis=1)
 
-    def form_call(table, panels, curvature):
+    table_a, table_b = table_of(ids), table_of(ids_other)
+    formed = jax.ShapeDtypeStruct((tiles, chips * extent, 2 * WIDTH), jnp.bfloat16)
+    whole = pl.BlockSpec(memory_space=pltpu.HBM)
+    rows_a, pan_here = pl.pallas_call(
+        functools.partial(form_own_kernel, total),
+        in_specs=[SMEM, whole, whole],
+        out_specs=[VMEM, VMEM],
+        out_shape=[formed, jax.ShapeDtypeStruct(panels.shape, panels.dtype)],
+        scratch_shapes=[
+            pltpu.VMEM(curvature.shape, jnp.float32),
+            pltpu.SemaphoreType.DMA((tiles,)),
+            pltpu.SemaphoreType.DMA,
+        ],
+        compiler_params=PARAMS,
+        name="form_own",
+    )(table_a, panels, curvature)
+    rows_b = pl.pallas_call(
+        functools.partial(form_kernel, total),
+        in_specs=[SMEM, VMEM, VMEM],
+        out_specs=VMEM,
+        out_shape=formed,
+        compiler_params=PARAMS,
+        name="form_other",
+    )(table_b, pan_other, cur_other)
+
+    def round_call(sending, turn, tables):
+        height, kind = (coded, jnp.int16) if sending else (extent, jnp.float32)
+        bases = [(2 * turn + which) * n_cam * per for which in range(2)]
+        pairs = columns // LANES
+        plan = (sending, bases, orders, total, row_blocks, chips // 2, tiles, pairs)
         return pl.pallas_call(
-            functools.partial(form_kernel, total),
-            in_specs=[SMEM, VMEM, VMEM],
-            out_specs=VMEM,
-            out_shape=jax.ShapeDtypeStruct((tiles, chips * extent, 2 * WIDTH), jnp.bfloat16),
-            compiler_params=PARAMS,
-            name="form",
-        )(table, panels, curvature)
-
-    tables = (table_of(ids), table_of(ids_other))
-    rows = (
-        form_call(tables[0], panels, curvature),
-        form_call(tables[1], pan_other, cur_other),
-    )
-
-    def piece_call(sending, turn, which, tables):
-        height, kind = (coded, jnp.int16) if sending else (extent, jnp.float32)
-        plan = (
-            sending,
-            (2 * turn + which) * n_cam * per,
-            orders[which],
-            total,
-            row_blocks,
-            chips // 2,
-            tiles,
-            columns // CHUNK,
-        )
-        return pl.pallas_call(
-            functools.partial(piece_kernel, plan),
+            functools.partial(round_kernel, plan),
             in_specs=[SMEM] * 2 + [VMEM] * 4,
-            out_specs=VMEM,
-            out_shape=jax.ShapeDtypeStruct((chips // 2, height, columns), kind),
-            scratch_shapes=[pltpu.VMEM((CHUNK, 2 * WIDTH), jnp.bfloat16)]
-            + [pltpu.VMEM((chips // 2, extent, columns), jnp.float32)] * sending,
+            out_specs=[VMEM] * 2,
+            out_shape=[jax.ShapeDtypeStruct((chips // 2, height, columns), kind)] * 2,
+            scratch_shapes=[
+                pltpu.VMEM((columns + LANES, 2 * WIDTH), jnp.bfloat16),
+                pltpu.SMEM((pairs + 1,), jnp.int32),
+                pltpu.VMEM((chips // 2, extent, columns + LANES), jnp.float32),
+            ],
             compiler_params=PARAMS,
             name="send" if sending else "keep",
-        )(*tables, panels, pan_other, *rows)
-
+        )(*tables, pan_here, pan_other, rows_a, rows_b)
+
+    tables = (table_a, table_b)
     sends, keeps = [], []
     for turn in range(turns):
         for sending, made in ((True, sends), (False, keeps)):
-            made.append([piece_call(sending, turn, which, tables) for which in range(2)])
+            made.append(list(round_call(sending, turn, tables)))
             tables = lax.optimization_barrier((tables, made[-1]))[0]
 
     came = [[[], []] for _ in range(turns)]

time: 82.9 us -> 77.9 us (0.940)
  Pallas kernels: 36 us -> 18.5 us
  waiting for transfers between devices: 24.8 us -> 35.7 us
  starting transfers between devices: 18.6 us -> 20.6 us
    pallas_call x10 -> x6, Pallas kernels: 31.2 us -> 13.7 us  [the longest x4 10.6 us: round_call(): pl.pallas_call(functools.partial(round_kernel, plan), in_specs=[SMEM] * 2...]
    ppermute x11, waiting for transfers between devices: 9.81 us -> 22.4 us  [swap(): return lax.ppermute(value, 'lm', [(i, i ^ 1 << bit) for i in range(n_lm)])]
    ppermute x11, starting transfers between devices: 10.8 us -> 12.6 us  [swap(): return lax.ppermute(value, 'lm', [(i, i ^ 1 << bit) for i in range(n_lm)])]
    ppermute x6, waiting for transfers between devices: 14.9 us -> 13.3 us  [body(): lax.ppermute(value, 'cam', [(i, i ^ pos + 1) for i in range(n_cam)])]
    unnamed x8 -> x6, local copies, waits for them, and re-layouts: 2.12 us -> 2.11 us
  transfers between devices with their start and end apart: 17 -> 17, of which waited for: 6 -> 6; matrix products, arithmetic and copies ran while one was open for 1% -> 2% of each run, Pallas kernels for 22% -> 14%
where the time goes in v1:
time: 77.9 us; the launch traced here: 78.3 us
  waiting for transfers between devices  35.7 us (46%)
  starting transfers between devices  20.6 us (26%)
  Pallas kernels  18.5 us (24%)
  local copies, waits for them, and re-layouts  2.11 us (3%)
  other arithmetic  1.18 us (2%)
    ppermute x11, waiting for transfers between devices, swap(): return lax.ppermute(value, 'lm', [(i, i ^ 1 << bit) for i in range(n_lm)])  22.4 us
    ppermute x6, waiting for transfers between devices, body(): lax.ppermute(value, 'cam', [(i, i ^ pos + 1) for i in range(n_cam)])  13.3 us
    ppermute x11, starting transfers between devices, swap(): return lax.ppermute(value, 'lm', [(i, i ^ 1 << bit) for i in range(n_lm)])  12.6 us
    pallas_call x4, Pallas kernels, round_call(): pl.pallas_call(functools.partial(round_kernel, plan), in_specs=[SMEM] * 2...  10.6 us
    ppermute x6, starting transfers between devices, body(): lax.ppermute(value, 'cam', [(i, i ^ pos + 1) for i in range(n_cam)])  8.01 us
    unnamed x6, local copies, waits for them, and re-layouts  2.11 us
    pallas_call x1, Pallas kernels, body(): pl.pallas_call(functools.partial(form_own_kernel, total), in_specs=[SMEM,...  1.7 us
    pallas_call x2, Pallas kernels, body(): pl.pallas_call(functools.partial(finish_kernel, row_blocks, n_cam - 1), g...  1.64 us
  transfers between devices with their start and end apart: 17, of which 6 were waited for; matrix products, arithmetic and copies ran while one was open for 2% of the time, Pallas kernels for 14%

profile of v1, /device:TPU:0, one launch (start us, length us, event | category | flops | bytes accessed | tf_op | source)
XLA Modules:
  0.0 78.3 jit_solution(1945976938470348259)
XLA Ops:
  0.0 0.5 collective-permute-start.1
  0.5 0.8 fusion.3
  1.2 0.1 collective-permute-start
  1.3 0.5 collective-permute-start.2
  1.8 0.1 select_reduce_fusion.1.table.table_a
  1.9 0.0 copy-start
  1.9 1.4 %copy-done = bf16[2,16,64,384]{3,2,1,0:T(8,128)(2,1)S(1)} copy-done((bf16[2,16,64,384]{3,2,1,0:T(8,128)(2,1)S(1)}, bf16[2,16,64,384]{3,2,1,0:T(8,128)(2,1)}, u32[]{:S(2)}) %copy-start) | copy-done | bytes 1572888
  3.3 0.0 copy-start.1
  3.3 0.7 copy-done.1
  4.0 1.7 %form_own.1 = (bf16[2,1024,768]{2,1,0:T(8,128)(2,1)S(1)}, bf16[2,16,64,384]{3,2,1,0:T(8,128)(2,1)S(1)}) custom-call(s32[2,48]{1,0:T(2,128)S(1)} %select_reduce_fusion.1.table.table_a, bf16[2,16,64,384]{3,2,1,0:T(8,128)(2,1)S(1)} %copy-done, f32[3,3,256]{2,1,0:T(4,128)S(1)} %copy-done.1), custom_call_target="tpu_custom_call" | custom-call | tf_op jit(solution)/shard_map/form_own/pallas_call | solution.py:321
  5.7 0.0 collective-permute-done
  5.8 0.1 select_reduce_fusion.table.table_b
  5.9 0.0 collective-permute-done.2.cur
  5.9 0.0 collective-permute-done.1.pan.pan_b
  5.9 1.4 %form_other.1.rows_b = bf16[2,1024,768]{2,1,0:T(8,128)(2,1)S(1)} custom-call(s32[2,48]{1,0:T(2,128)S(1)} %select_reduce_fusion.table.table_b, bf16[2,16,64,384]{3,2,1,0:T(8,128)(2,1)S(1)} %collective-permute-done.1.pan.pan_b, f32[3,3,256]{2,1,0:T(4,128)S(1)} %collective-permute-done.2.cur), custom_call_target="tpu_custom_call" | custom-call | tf_op jit(solution)/shard_map/form_other/pallas_call | solution.py:334
  7.3 3.2 %send.2 = (s16[2,272,512]{2,1,0:T(8,128)(2,1)S(1)}, s16[2,272,512]{2,1,0:T(8,128)(2,1)S(1)}) custom-call(s32[2,48]{1,0:T(2,128)S(1)} %select_reduce_fusion.1.table.table_a, s32[2,48]{1,0:T(2,128)S(1)} %select_reduce_fusion.table.table_b, bf16[2,16,64,384]{3,2,1,0:T(8,128)(2,1)S(1)} %get-tuple-element.29.pan_a, ...), custom_call_target="tpu_custom_call" | custom-call | tf_op jit(solution)/shard_map/send/pallas_call | solution.py:348
  10.6 5.6 %collective-permute-start.4 = (s16[2,272,512]{2,1,0:T(8,128)(2,1)S(1)}, s16[2,272,512]{2,1,0:T(8,128)(2,1)S(1)}, u32[]{:S(2)}, u32[]{:S(2)}) collective-permute-start(s16[2,272,512]{2,1,0:T(8,128)(2,1)S(1)} %get-tuple-element.32), channel_id=1, source_target_pairs={{0,16},{4,20},{8,24},{12,28},{16,0},{20,4},{24,8},{28,12},{1,17},{... | collective-permute-start | bytes 1671176 | tf_op jit(solution)/shard_map/ppermute | solution.py:300
  16.1 0.0 collective-permute-start.3
  16.1 2.9 %keep.2 = (f32[2,256,512]{2,1,0:T(8,128)S(1)}, f32[2,256,512]{2,1,0:T(8,128)S(1)}) custom-call(s32[2,48]{1,0:T(2,128)S(1)} %select_reduce_fusion.1.table.table_a, s32[2,48]{1,0:T(2,128)S(1)} %select_reduce_fusion.table.table_b, bf16[2,16,64,384]{3,2,1,0:T(8,128)(2,1)S(1)} %get-tuple-element.29.pan_a, ...), custom_call_target="tpu_custom_call" | custom-call | tf_op jit(solution)/shard_map/keep/pallas_call | solution.py:348
  19.1 2.2 %send.3 = (s16[2,272,512]{2,1,0:T(8,128)(2,1)S(1)}, s16[2,272,512]{2,1,0:T(8,128)(2,1)S(1)}) custom-call(s32[2,48]{1,0:T(2,128)S(1)} %select_reduce_fusion.1.table.table_a, s32[2,48]{1,0:T(2,128)S(1)} %select_reduce_fusion.table.table_b, bf16[2,16,64,384]{3,2,1,0:T(8,128)(2,1)S(1)} %get-tuple-element.29.pan_a, ...), custom_call_target="tpu_custom_call" | custom-call | tf_op jit(solution)/shard_map/send/pallas_call | solution.py:348
  21.3 8.2 %collective-permute-done.4.rest_0_.rest_4_ = s16[2,272,512]{2,1,0:T(8,128)(2,1)S(1)} collective-permute-done((s16[2,272,512]{2,1,0:T(8,128)(2,1)S(1)}, s16[2,272,512]{2,1,0:T(8,128)(2,1)S(1)}, u32[]{:S(2)}, u32[]{:S(2)}) %collective-permute-start.4) | collective-permute-done | bytes 557088 | tf_op jit(solution)/shard_map/ppermute | solution.py:300
  29.5 1.7 %collective-permute-done.3.rest_0_.rest_1_ = s16[2,272,512]{2,1,0:T(8,128)(2,1)S(1)} collective-permute-done((s16[2,272,512]{2,1,0:T(8,128)(2,1)S(1)}, s16[2,272,512]{2,1,0:T(8,128)(2,1)S(1)}, u32[]{:S(2)}, u32[]{:S(2)}) %collective-permute-start.3) | collective-permute-done | bytes 557088 | tf_op jit(solution)/shard_map/ppermute | solution.py:300
  31.2 0.4 collective-permute-start.7
  31.6 0.3 collective-permute-start.5
  31.9 0.3 relay.7
  32.1 1.8 %collective-permute-start.13 = (s16[1,272,512]{2,1,0:T(8,128)(2,1)S(1)}, s16[1,272,512]{2,1,0:T(8,128)(2,1)S(1)}, u32[]{:S(2)}, u32[]{:S(2)}) collective-permute-start(s16[1,272,512]{2,1,0:T(8,128)(2,1)S(1)} %relay.7), channel_id=1, source_target_pairs={{0,8},{4,12},{8,0},{12,4},{16,24},{20,28},{24,16},{28,20},{1,9},{5... | collective-permute-start | bytes 835592 | tf_op jit(solution)/shard_map/ppermute | solution.py:300
  33.9 0.3 relay.6
  34.2 1.7 %collective-permute-start.12 = (s16[1,272,512]{2,1,0:T(8,128)(2,1)S(1)}, s16[1,272,512]{2,1,0:T(8,128)(2,1)S(1)}, u32[]{:S(2)}, u32[]{:S(2)}) collective-permute-start(s16[1,272,512]{2,1,0:T(8,128)(2,1)S(1)} %relay.6), channel_id=1, source_target_pairs={{0,16},{4,20},{8,24},{12,28},{16,0},{20,4},{24,8},{28,12},{1,17},{... | collective-permute-start | bytes 835592 | tf_op jit(solution)/shard_map/ppermute | solution.py:300
  36.0 2.2 %keep.3 = (f32[2,256,512]{2,1,0:T(8,128)S(1)}, f32[2,256,512]{2,1,0:T(8,128)S(1)}) custom-call(s32[2,48]{1,0:T(2,128)S(1)} %select_reduce_fusion.1.table.table_a, s32[2,48]{1,0:T(2,128)S(1)} %select_reduce_fusion.table.table_b, bf16[2,16,64,384]{3,2,1,0:T(8,128)(2,1)S(1)} %get-tuple-element.29.pan_a, ...), custom_call_target="tpu_custom_call" | custom-call | tf_op jit(solution)/shard_map/keep/pallas_call | solution.py:348
  38.2 8.5 %collective-permute-done.7.rest_0_.rest_4_ = s16[2,272,512]{2,1,0:T(8,128)(2,1)S(1)} collective-permute-done((s16[2,272,512]{2,1,0:T(8,128)(2,1)S(1)}, s16[2,272,512]{2,1,0:T(8,128)(2,1)S(1)}, u32[]{:S(2)}, u32[]{:S(2)}) %collective-permute-start.7) | collective-permute-done | bytes 557088 | tf_op jit(solution)/shard_map/ppermute | solution.py:300
  46.7 0.3 relay.5
  47.0 0.3 collective-permute-start.8
  47.3 0.0 collective-permute-done.5.rest_0_.rest_1_
  47.3 0.3 relay.4
  47.6 1.5 %collective-permute-start.6 = (s16[1,272,512]{2,1,0:T(8,128)(2,1)S(1)}, s16[1,272,512]{2,1,0:T(8,128)(2,1)S(1)}, u32[]{:S(2)}, u32[]{:S(2)}) collective-permute-start(s16[1,272,512]{2,1,0:T(8,128)(2,1)S(1)} %relay.4), channel_id=1, source_target_pairs={{0,16},{4,20},{8,24},{12,28},{16,0},{20,4},{24,8},{28,12},{1,17},{... | collective-permute-start | bytes 835592 | tf_op jit(solution)/shard_map/ppermute | solution.py:300
  49.1 3.9 %collective-permute-done.13.rest_5_ = s16[1,272,512]{2,1,0:T(8,128)(2,1)S(1)} collective-permute-done((s16[1,272,512]{2,1,0:T(8,128)(2,1)S(1)}, s16[1,272,512]{2,1,0:T(8,128)(2,1)S(1)}, u32[]{:S(2)}, u32[]{:S(2)}) %collective-permute-start.13) | collective-permute-done | bytes 278560 | tf_op jit(solution)/shard_map/ppermute | solution.py:300
  53.1 0.0 collective-permute-done.12.rest_2_
  53.1 0.4 cross.3
  53.5 1.5 %collective-permute-start.14 = (s16[2,272,128]{2,1,0:T(8,128)(2,1)S(1)}, s16[2,272,128]{2,1,0:T(8,128)(2,1)S(1)}, u32[]{:S(2)}, u32[]{:S(2)}) collective-permute-start(s16[2,272,128]{2,1,0:T(8,128)(2,1)S(1)} %get-tuple-element.50), channel_id=1, source_target_pairs={{0,1},{1,0},{2,3},{3,2},{4,5},{5,4},{6,7},{7,6},{8,9},{9,8},{10,11... | collective-permute-start | bytes 417800 | tf_op jit(solution)/shard_map/ppermute | solution.py:417
  55.0 1.6 %collective-permute-start.15 = (s16[2,272,128]{2,1,0:T(8,128)(2,1)S(1)}, s16[2,272,128]{2,1,0:T(8,128)(2,1)S(1)}, u32[]{:S(2)}, u32[]{:S(2)}) collective-permute-start(s16[2,272,128]{2,1,0:T(8,128)(2,1)S(1)} %get-tuple-element.51), channel_id=1, source_target_pairs={{0,2},{1,3},{2,0},{3,1},{4,6},{5,7},{6,4},{7,5},{8,10},{9,11},{10,... | collective-permute-start | bytes 417800 | tf_op jit(solution)/shard_map/ppermute | solution.py:417
  56.6 0.0 copy-start.2
  56.6 1.3 %collective-permute-start.16 = (s16[2,272,128]{2,1,0:T(8,128)(2,1)S(1)}, s16[2,272,128]{2,1,0:T(8,128)(2,1)S(1)}, u32[]{:S(2)}, u32[]{:S(2)}) collective-permute-start(s16[2,272,128]{2,1,0:T(8,128)(2,1)S(1)} %get-tuple-element.52), channel_id=1, source_target_pairs={{0,3},{1,2},{2,1},{3,0},{4,7},{5,6},{6,5},{7,4},{8,11},{9,10},{10,... | collective-permute-start | bytes 417800 | tf_op jit(solution)/shard_map/ppermute | solution.py:417
  57.9 0.0 collective-permute-done.8.rest_5_
  57.9 0.0 collective-permute-done.6.rest_2_
  57.9 0.4 cross.2
  58.3 1.0 %collective-permute-start.10 = (s16[2,272,128]{2,1,0:T(8,128)(2,1)S(1)}, s16[2,272,128]{2,1,0:T(8,128)(2,1)S(1)}, u32[]{:S(2)}, u32[]{:S(2)}) collective-permute-start(s16[2,272,128]{2,1,0:T(8,128)(2,1)S(1)} %get-tuple-element.48), channel_id=1, source_target_pairs={{0,2},{1,3},{2,0},{3,1},{4,6},{5,7},{6,4},{7,5},{8,10},{9,11},{10,... | collective-permute-start | bytes 417800 | tf_op jit(solution)/shard_map/ppermute | solution.py:417
  59.3 2.5 %collective-permute-start.11 = (s16[2,272,128]{2,1,0:T(8,128)(2,1)S(1)}, s16[2,272,128]{2,1,0:T(8,128)(2,1)S(1)}, u32[]{:S(2)}, u32[]{:S(2)}) collective-permute-start(s16[2,272,128]{2,1,0:T(8,128)(2,1)S(1)} %get-tuple-element.49), channel_id=1, source_target_pairs={{0,3},{1,2},{2,1},{3,0},{4,7},{5,6},{6,5},{7,4},{8,11},{9,10},{10,... | collective-permute-start | bytes 417800 | tf_op jit(solution)/shard_map/ppermute | solution.py:417
  61.8 0.0 collective-permute-done.14.rest_0_
  61.8 0.1 collective-permute-start.9
  61.9 0.1 pad_add_fusion.me_ref
  62.0 0.0 copy-done.2
  62.0 0.1 pad_maximum_fusion.wide_ref
  62.1 0.6 base.3.base_ref
  62.7 8.8 %collective-permute-done.15.rest_1_ = s16[2,272,128]{2,1,0:T(8,128)(2,1)S(1)} collective-permute-done((s16[2,272,128]{2,1,0:T(8,128)(2,1)S(1)}, s16[2,272,128]{2,1,0:T(8,128)(2,1)S(1)}, u32[]{:S(2)}, u32[]{:S(2)}) %collective-permute-start.15) | collective-permute-done | bytes 139296 | tf_op jit(solution)/shard_map/ppermute | solution.py:417
  71.5 0.0 collective-permute-done.16.rest_2_
  71.5 0.8 %finish.2.rest_3_ = f32[256,512]{1,0:T(8,128)} custom-call(f32[256,256]{1,0:T(8,128)S(1)} %base.3.base_ref, s16[2,272,128]{2,1,0:T(8,128)(2,1)S(1)} %collective-permute-done.14.rest_0_, s16[2,272,128]{2,1,0:T(8,128)(2,1)S(1)} %collective-permute-done.15.rest_1_, s16[2,272,128]{2,1,0:T(8,128)(2,1)S(1)} %collective-permute-done.16.rest_2_), custom_call_target="tpu_custom_call" | custom-call | tf_op jit(solution)/shard_map/finish/pallas_call | solution.py:430
  72.3 0.6 base.2.base_ref
  73.0 4.5 %collective-permute-done.10.rest_1_ = s16[2,272,128]{2,1,0:T(8,128)(2,1)S(1)} collective-permute-done((s16[2,272,128]{2,1,0:T(8,128)(2,1)S(1)}, s16[2,272,128]{2,1,0:T(8,128)(2,1)S(1)}, u32[]{:S(2)}, u32[]{:S(2)}) %collective-permute-start.10) | collective-permute-done | bytes 139296 | tf_op jit(solution)/shard_map/ppermute | solution.py:417
  77.5 0.0 collective-permute-done.11.rest_2_
  77.5 0.0 collective-permute-done.9.rest_0_
  77.5 0.8 %finish.3 = f32[256,512]{1,0:T(8,128)} custom-call(f32[256,256]{1,0:T(8,128)S(1)} %base.2.base_ref, s16[2,272,128]{2,1,0:T(8,128)(2,1)S(1)} %collective-permute-done.9.rest_0_, s16[2,272,128]{2,1,0:T(8,128)(2,1)S(1)} %collective-permute-done.10.rest_1_, s16[2,272,128]{2,1,0:T(8,128)(2,1)S(1)} %collective-permute-done.11.rest_2_, ...), custom_call_target="tpu_custom_call", output_to_operand_aliasing={{}: (4, {})} | custom-call | tf_op jit(solution)/shard_map/finish/pallas_call | solution.py:430
  (2 shorter events, 0.0 us)
Async XLA Ops:
  0.0 5.9 %collective-permute-start.1 = (bf16[2,16,64,384]{3,2,1,0:T(8,128)(2,1)}, bf16[2,16,64,384]{3,2,1,0:T(8,128)(2,1)S(1)}, u32[]{:S(2)}, u32[]{:S(2)}) collective-permute-start(bf16[2,16,64,384]{3,2,1,0:T(8,128)(2,1)} %pan_ref.1), channel_id=1, source_target_pairs={{0,4},{4,0},{8,12},{12,8},{16,20},{20,16},{24,28},{28,24},{1,5},{5... | collective-permute-start | bytes 4718600 | tf_op jit(solution)/shard_map/ppermute | solution.py:300
  1.2 4.5 %collective-permute-start = (s32[2,16]{1,0:T(2,128)S(1)}, s32[2,16]{1,0:T(2,128)S(1)}, u32[]{:S(2)}, u32[]{:S(2)}) collective-permute-start(s32[2,16]{1,0:T(2,128)S(1)} %get-tuple-element.54), channel_id=1, source_target_pairs={{0,4},{4,0},{8,12},{12,8},{16,20},{20,16},{24,28},{28,24},{1,5},{5... | collective-permute-start | bytes 392 | tf_op jit(solution)/shard_map/ppermute | solution.py:300
  1.3 4.5 %collective-permute-start.2 = (f32[3,3,256]{2,1,0:T(4,128)}, f32[3,3,256]{2,1,0:T(4,128)S(1)}, u32[]{:S(2)}, u32[]{:S(2)}) collective-permute-start(f32[3,3,256]{2,1,0:T(4,128)} %cur_ref.1), channel_id=1, source_target_pairs={{0,4},{4,0},{8,12},{12,8},{16,20},{20,16},{24,28},{28,24},{1,5},{5... | collective-permute-start | bytes 27656 | tf_op jit(solution)/shard_map/ppermute | solution.py:300
  1.9 1.4 %copy-start = (bf16[2,16,64,384]{3,2,1,0:T(8,128)(2,1)S(1)}, bf16[2,16,64,384]{3,2,1,0:T(8,128)(2,1)}, u32[]{:S(2)}) copy-start(bf16[2,16,64,384]{3,2,1,0:T(8,128)(2,1)} %pan_ref.1) | copy-start | bytes 4718596
  3.3 0.7 copy-start.1
  10.6 18.9 %collective-permute-start.4 = (s16[2,272,512]{2,1,0:T(8,128)(2,1)S(1)}, s16[2,272,512]{2,1,0:T(8,128)(2,1)S(1)}, u32[]{:S(2)}, u32[]{:S(2)}) collective-permute-start(s16[2,272,512]{2,1,0:T(8,128)(2,1)S(1)} %get-tuple-element.32), channel_id=1, source_target_pairs={{0,16},{4,20},{8,24},{12,28},{16,0},{20,4},{24,8},{28,12},{1,17},{... | collective-permute-start | bytes 1671176 | tf_op jit(solution)/shard_map/ppermute | solution.py:300
  16.1 15.1 %collective-permute-start.3 = (s16[2,272,512]{2,1,0:T(8,128)(2,1)S(1)}, s16[2,272,512]{2,1,0:T(8,128)(2,1)S(1)}, u32[]{:S(2)}, u32[]{:S(2)}) collective-permute-start(s16[2,272,512]{2,1,0:T(8,128)(2,1)S(1)} %get-tuple-element.31), channel_id=1, source_target_pairs={{0,8},{4,12},{8,0},{12,4},{16,24},{20,28},{24,16},{28,20},{1,9},{5... | collective-permute-start | bytes 1671176 | tf_op jit(solution)/shard_map/ppermute | solution.py:300
  31.2 15.5 %collective-permute-start.7 = (s16[2,272,512]{2,1,0:T(8,128)(2,1)S(1)}, s16[2,272,512]{2,1,0:T(8,128)(2,1)S(1)}, u32[]{:S(2)}, u32[]{:S(2)}) collective-permute-start(s16[2,272,512]{2,1,0:T(8,128)(2,1)S(1)} %get-tuple-element.46), channel_id=1, source_target_pairs={{0,16},{4,20},{8,24},{12,28},{16,0},{20,4},{24,8},{28,12},{1,17},{... | collective-permute-start | bytes 1671176 | tf_op jit(solution)/shard_map/ppermute | solution.py:300
  31.6 15.8 %collective-permute-start.5 = (s16[2,272,512]{2,1,0:T(8,128)(2,1)S(1)}, s16[2,272,512]{2,1,0:T(8,128)(2,1)S(1)}, u32[]{:S(2)}, u32[]{:S(2)}) collective-permute-start(s16[2,272,512]{2,1,0:T(8,128)(2,1)S(1)} %get-tuple-element.44), channel_id=1, source_target_pairs={{0,8},{4,12},{8,0},{12,4},{16,24},{20,28},{24,16},{28,20},{1,9},{5... | collective-permute-start | bytes 1671176 | tf_op jit(solution)/shard_map/ppermute | solution.py:300
  32.1 20.9 %collective-permute-start.13 = (s16[1,272,512]{2,1,0:T(8,128)(2,1)S(1)}, s16[1,272,512]{2,1,0:T(8,128)(2,1)S(1)}, u32[]{:S(2)}, u32[]{:S(2)}) collective-permute-start(s16[1,272,512]{2,1,0:T(8,128)(2,1)S(1)} %relay.7), channel_id=1, source_target_pairs={{0,8},{4,12},{8,0},{12,4},{16,24},{20,28},{24,16},{28,20},{1,9},{5... | collective-permute-start | bytes 835592 | tf_op jit(solution)/shard_map/ppermute | solution.py:300
  34.2 18.9 %collective-permute-start.12 = (s16[1,272,512]{2,1,0:T(8,128)(2,1)S(1)}, s16[1,272,512]{2,1,0:T(8,128)(2,1)S(1)}, u32[]{:S(2)}, u32[]{:S(2)}) collective-permute-start(s16[1,272,512]{2,1,0:T(8,128)(2,1)S(1)} %relay.6), channel_id=1, source_target_pairs={{0,16},{4,20},{8,24},{12,28},{16,0},{20,4},{24,8},{28,12},{1,17},{... | collective-permute-start | bytes 835592 | tf_op jit(solution)/shard_map/ppermute | solution.py:300
  47.0 10.9 %collective-permute-start.8 = (s16[1,272,512]{2,1,0:T(8,128)(2,1)S(1)}, s16[1,272,512]{2,1,0:T(8,128)(2,1)S(1)}, u32[]{:S(2)}, u32[]{:S(2)}) collective-permute-start(s16[1,272,512]{2,1,0:T(8,128)(2,1)S(1)} %relay.5), channel_id=1, source_target_pairs={{0,8},{4,12},{8,0},{12,4},{16,24},{20,28},{24,16},{28,20},{1,9},{5... | collective-permute-start | bytes 835592 | tf_op jit(solution)/shard_map/ppermute | solution.py:300
  47.6 10.3 %collective-permute-start.6 = (s16[1,272,512]{2,1,0:T(8,128)(2,1)S(1)}, s16[1,272,512]{2,1,0:T(8,128)(2,1)S(1)}, u32[]{:S(2)}, u32[]{:S(2)}) collective-permute-start(s16[1,272,512]{2,1,0:T(8,128)(2,1)S(1)} %relay.4), channel_id=1, source_target_pairs={{0,16},{4,20},{8,24},{12,28},{16,0},{20,4},{24,8},{28,12},{1,17},{... | collective-permute-start | bytes 835592 | tf_op jit(solution)/shard_map/ppermute | solution.py:300
  53.5 8.4 %collective-permute-start.14 = (s16[2,272,128]{2,1,0:T(8,128)(2,1)S(1)}, s16[2,272,128]{2,1,0:T(8,128)(2,1)S(1)}, u32[]{:S(2)}, u32[]{:S(2)}) collective-permute-start(s16[2,272,128]{2,1,0:T(8,128)(2,1)S(1)} %get-tuple-element.50), channel_id=1, source_target_pairs={{0,1},{1,0},{2,3},{3,2},{4,5},{5,4},{6,7},{7,6},{8,9},{9,8},{10,11... | collective-permute-start | bytes 417800 | tf_op jit(solution)/shard_map/ppermute | solution.py:417
  55.0 16.5 %collective-permute-start.15 = (s16[2,272,128]{2,1,0:T(8,128)(2,1)S(1)}, s16[2,272,128]{2,1,0:T(8,128)(2,1)S(1)}, u32[]{:S(2)}, u32[]{:S(2)}) collective-permute-start(s16[2,272,128]{2,1,0:T(8,128)(2,1)S(1)} %get-tuple-element.51), channel_id=1, source_target_pairs={{0,2},{1,3},{2,0},{3,1},{4,6},{5,7},{6,4},{7,5},{8,10},{9,11},{10,... | collective-permute-start | bytes 417800 | tf_op jit(solution)/shard_map/ppermute | solution.py:417
  56.6 5.3 %copy-start.2 = (f32[4,64,64]{2,1,0:T(8,128)S(1)}, f32[4,64,64]{2,1,0:T(8,128)}, u32[]{:S(2)}) copy-start(f32[4,64,64]{2,1,0:T(8,128)} %param.9) | copy-start | bytes 196612
  56.6 14.9 %collective-permute-start.16 = (s16[2,272,128]{2,1,0:T(8,128)(2,1)S(1)}, s16[2,272,128]{2,1,0:T(8,128)(2,1)S(1)}, u32[]{:S(2)}, u32[]{:S(2)}) collective-permute-start(s16[2,272,128]{2,1,0:T(8,128)(2,1)S(1)} %get-tuple-element.52), channel_id=1, source_target_pairs={{0,3},{1,2},{2,1},{3,0},{4,7},{5,6},{6,5},{7,4},{8,11},{9,10},{10,... | collective-permute-start | bytes 417800 | tf_op jit(solution)/shard_map/ppermute | solution.py:417
  58.3 19.2 %collective-permute-start.10 = (s16[2,272,128]{2,1,0:T(8,128)(2,1)S(1)}, s16[2,272,128]{2,1,0:T(8,128)(2,1)S(1)}, u32[]{:S(2)}, u32[]{:S(2)}) collective-permute-start(s16[2,272,128]{2,1,0:T(8,128)(2,1)S(1)} %get-tuple-element.48), channel_id=1, source_target_pairs={{0,2},{1,3},{2,0},{3,1},{4,6},{5,7},{6,4},{7,5},{8,10},{9,11},{10,... | collective-permute-start | bytes 417800 | tf_op jit(solution)/shard_map/ppermute | solution.py:417
  59.3 18.1 %collective-permute-start.11 = (s16[2,272,128]{2,1,0:T(8,128)(2,1)S(1)}, s16[2,272,128]{2,1,0:T(8,128)(2,1)S(1)}, u32[]{:S(2)}, u32[]{:S(2)}) collective-permute-start(s16[2,272,128]{2,1,0:T(8,128)(2,1)S(1)} %get-tuple-element.49), channel_id=1, source_target_pairs={{0,3},{1,2},{2,1},{3,0},{4,7},{5,6},{6,5},{7,4},{8,11},{9,10},{10,... | collective-permute-start | bytes 417800 | tf_op jit(solution)/shard_map/ppermute | solution.py:417
  61.8 15.7 %collective-permute-start.9 = (s16[2,272,128]{2,1,0:T(8,128)(2,1)S(1)}, s16[2,272,128]{2,1,0:T(8,128)(2,1)S(1)}, u32[]{:S(2)}, u32[]{:S(2)}) collective-permute-start(s16[2,272,128]{2,1,0:T(8,128)(2,1)S(1)} %get-tuple-element.47), channel_id=1, source_target_pairs={{0,1},{1,0},{2,3},{3,2},{4,5},{5,4},{6,7},{7,6},{8,9},{9,8},{10,11... | collective-permute-start | bytes 417800 | tf_op jit(solution)/shard_map/ppermute | solution.py:417

commit v2 on v1

--- a/solution.py
+++ b/solution.py
@@ -14,7 +14,6 @@
 WIDTH = 3 * LMB
 STRIP = 16
 LANES = 128
-CHUNK = 512
 VMEM = pl.BlockSpec(memory_space=pltpu.VMEM)
 SMEM = pl.BlockSpec(memory_space=pltpu.SMEM)
 PARAMS = pltpu.CompilerParams(vmem_limit_bytes=32 * 1024 * 1024)
@@ -39,35 +38,40 @@
 
 def encode(dst, lanes, parts):
     blocks = len(parts)
-    row = lax.broadcasted_iota(jnp.int32, (8, LANES), 0)
-    tops = jnp.full((8, LANES), 2.0**-100, jnp.float32)
+    row = lax.broadcasted_iota(jnp.int32, (STRIP, LANES), 0)
+    tops = jnp.full((STRIP, LANES), 2.0**-100, jnp.float32)
     for block, part in enumerate(parts):
-        top = jnp.max(jnp.abs(part), axis=0, keepdims=True)
+        top = jnp.max(jnp.abs(part()), axis=0, keepdims=True)
         tops = jnp.where(row == block, jnp.maximum(top, tops), tops)
     power = jnp.ceil(jnp.log2(tops) - 14.99)
     inverse = jnp.exp2(-power)
     for block, part in enumerate(parts):
-        coded = jnp.round(part * inverse[block : block + 1])
+        coded = jnp.floor(part() * inverse[block : block + 1] + 0.5)
         dst[pl.ds(block * CB, CB), lanes] = coded.astype(jnp.int32).astype(jnp.int16)
-    strip = jnp.concatenate([power, power], axis=0).astype(jnp.int32)
-    dst[pl.ds(blocks * CB, STRIP), lanes] = strip.astype(jnp.int16)
-
-
-def decode(src, lanes, blocks):
-    strip = src[pl.ds(blocks * CB, STRIP), lanes].astype(jnp.int32).astype(jnp.float32)
+    dst[pl.ds(blocks * CB, STRIP), lanes] = power.astype(jnp.int32).astype(jnp.int16)
+
+
+def decode(src, lanes, first, blocks):
+    below = src.shape[0] - STRIP
+    strip = src[pl.ds(below, STRIP), lanes].astype(jnp.int32).astype(jnp.float32)
     scale = jnp.exp2(strip)
     return [
         src[pl.ds(block * CB, CB), lanes].astype(jnp.int32).astype(jnp.float32)
         * scale[block : block + 1]
-        for block in range(blocks)
+        for block in range(first, first + blocks)
     ]
 
 
-def gathered(keep, came, lanes, blocks):
-    parts = [keep[pl.ds(block * CB, CB), lanes] for block in range(blocks)]
+def gathered(place, keep, came, lanes, blocks):
+    parts = [keep[place, pl.ds(block * CB, CB), lanes] for block in range(blocks)]
     for src in came:
-        parts = [part + other for part, other in zip(parts, decode(src, lanes, blocks))]
+        here = decode(src, lanes, place * blocks, blocks)
+        parts = [part + other for part, other in zip(parts, here)]
     return parts
+
+
+def given(values):
+    return [functools.partial(lambda value: value, value) for value in values]
 
 
 def spot_of(index, order):
@@ -75,37 +79,45 @@
     return sum(((index >> (bits - 1 - pos)) & 1) << bit for pos, bit in enumerate(order))
 
 
-def form_tile(total, table, tile, pan, cur, rows):
+def form_tile(plan, table, tile, pan, cur, rows):
+    total, row_blocks = plan
     inverse = invert_rows(cur, tile * LMB)
 
-    def one_place(place, carry):
-        slot = table[tile, total + place]
-        lines = pl.ds(pl.multiple_of(place * CB, CB), CB)
-
-        @pl.when(slot >= 0)
-        def form():
-            wide = pan[tile, slot].astype(jnp.float32)
-            split = [wide[:, c * LMB : (c + 1) * LMB] for c in range(3)]
-            for q in range(3):
-                formed = (
-                    split[0] * inverse[0][q] + split[1] * inverse[1][q] + split[2] * inverse[2][q]
-                )
-                high = formed.astype(jnp.bfloat16)
-                low = (formed - high.astype(jnp.float32)).astype(jnp.bfloat16)
-                at = q * LMB
-                rows[tile, lines, at : at + LMB] = high
-                rows[tile, lines, WIDTH + at : WIDTH + at + LMB] = low
-
-        @pl.when(slot < 0)
-        def blank():
-            rows[tile, lines, :] = jnp.zeros((CB, 2 * WIDTH), jnp.bfloat16)
+    def one_group(group, carry):
+        places = [group * row_blocks + block for block in range(row_blocks)]
+        slots = [table[tile, total + place] for place in places]
+
+        @pl.when(functools.reduce(jnp.maximum, slots) >= 0)
+        def some():
+            for place, slot in zip(places, slots):
+                lines = pl.ds(pl.multiple_of(place * CB, CB), CB)
+
+                @pl.when(slot >= 0)
+                def form():
+                    wide = pan[tile, slot].astype(jnp.float32)
+                    split = [wide[:, c * LMB : (c + 1) * LMB] for c in range(3)]
+                    for q in range(3):
+                        formed = (
+                            split[0] * inverse[0][q]
+                            + split[1] * inverse[1][q]
+                            + split[2] * inverse[2][q]
+                        )
+                        high = formed.astype(jnp.bfloat16)
+                        low = (formed - high.astype(jnp.float32)).astype(jnp.bfloat16)
+                        at = q * LMB
+                        rows[tile, lines, at : at + LMB] = high
+                        rows[tile, lines, WIDTH + at : WIDTH + at + LMB] = low
+
+                @pl.when(slot < 0)
+                def blank():
+                    rows[tile, lines, :] = jnp.zeros((CB, 2 * WIDTH), jnp.bfloat16)
 
         return carry
 
-    lax.fori_loop(0, rows.shape[1] // CB, one_place, 0)
-
-
-def form_own_kernel(total, table, pan_ref, cur_ref, rows, pan, cur, pan_sem, cur_sem):
+    lax.fori_loop(0, rows.shape[1] // (row_blocks * CB), one_group, 0)
+
+
+def form_own_kernel(plan, table, pan_ref, cur_ref, rows, pan, cur, pan_sem, cur_sem):
     tiles = rows.shape[0]
     copies = [
         pltpu.make_async_copy(pan_ref.at[tile], pan.at[tile], pan_sem.at[tile])
@@ -118,12 +130,12 @@
     small.wait()
     for tile, copy in enumerate(copies):
         copy.wait()
-        form_tile(total, table, tile, pan, cur, rows)
-
-
-def form_kernel(total, table, pan, cur, rows):
+        form_tile(plan, table, tile, pan, cur, rows)
+
+
+def form_kernel(plan, table, pan, cur, rows):
     for tile in range(rows.shape[0]):
-        form_tile(total, table, tile, pan, cur, rows)
+        form_tile(plan, table, tile, pan, cur, rows)
 
 
 def round_kernel(plan, table_a, table_b, pan_a, pan_b, rows_a, rows_b, *rest):
@@ -204,24 +216,33 @@
 
         def store(start, carry):
             lanes = pl.ds(pl.multiple_of(start * LANES, LANES), LANES)
-            for half in range(halves):
-                if sending:
-                    parts = [acc[half, pl.ds(block * CB, CB), lanes] for block in range(row_blocks)]
-                    encode(out.at[half], lanes, parts)
-                else:
+            if sending:
+                parts = [
+                    functools.partial(
+                        lambda half, block: acc[half, pl.ds(block * CB, CB), lanes], half, block
+                    )
+                    for half in range(halves)
+                    for block in range(row_blocks)
+                ]
+                encode(out, lanes, parts)
+            else:
+                for half in range(halves):
                     out[half, :, lanes] = acc[half, :, lanes]
             return carry
 
         lax.fori_loop(0, pairs, store, 0)
 
 
-def relay_kernel(row_blocks, keep_ref, *rest):
-    dst = rest[-1].at[0]
+def relay_kernel(plan, keep, *rest):
+    row_blocks, size = plan
+    dst = rest[-1]
 
     def code(start, carry):
         lanes = pl.ds(pl.multiple_of(start * LANES, LANES), LANES)
-        came = [ref.at[0] for ref in rest[:-1]]
-        encode(dst, lanes, gathered(keep_ref.at[0], came, lanes, row_blocks))
+        parts = []
+        for place in range(size // 2, size):
+            parts += given(gathered(place, keep, rest[:-1], lanes, row_blocks))
+        encode(dst, lanes, parts)
         return carry
 
     lax.fori_loop(0, dst.shape[1] // LANES, code, 0)
@@ -229,14 +250,14 @@
 
 def cross_kernel(row_blocks, group, arrays, *rest):
     dsts = rest[2 * arrays :]
-    for piece in range(2):
-        keep = rest[piece * arrays].at[0]
-        came = [ref.at[0] for ref in rest[piece * arrays + 1 : (piece + 1) * arrays]]
-        for other, dst in enumerate(dsts):
-            for start in range(0, group, LANES):
+    for other, dst in enumerate(dsts):
+        for start in range(0, group, LANES):
+            parts = []
+            for piece in range(2):
+                keep, *came = rest[piece * arrays : (piece + 1) * arrays]
                 lanes = pl.ds((other + 1) * group + start, LANES)
-                parts = gathered(keep, came, lanes, row_blocks)
-                encode(dst.at[piece], pl.ds(start, LANES), parts)
+                parts += given(gathered(0, keep, came, lanes, row_blocks))
+            encode(dst, pl.ds(start, LANES), parts)
 
 
 def base_kernel(plan, me_ref, wide_ref, *rest):
@@ -247,10 +268,9 @@
     first_col = me_ref[2] * col_blocks
     lane = lax.broadcasted_iota(jnp.int32, (CB, LANES), 1) // CB
     for piece in range(2):
-        keep = rest[piece * arrays].at[0]
-        came = [ref.at[0] for ref in rest[piece * arrays + 1 : (piece + 1) * arrays]]
+        keep, *came = rest[piece * arrays : (piece + 1) * arrays]
         for start in range(0, group, LANES):
-            parts = gathered(keep, came, pl.ds(start, LANES), row_blocks)
+            parts = gathered(0, keep, came, pl.ds(start, LANES), row_blocks)
             base = first_col + ((2 * turn + piece) * group + start) // CB
             for block in range(row_blocks):
                 wide = jnp.where(base + lane == first_row + block, wide_ref[block], 0.0)
@@ -263,11 +283,10 @@
     out_ref = rest[-1]
     group = out_ref.shape[1] // 2
     for piece in range(2):
-        came = [ref.at[piece] for ref in rest[:far]]
         for start in range(0, group, LANES):
             total = [0.0] * row_blocks
-            for src in came:
-                parts = decode(src, pl.ds(start, LANES), row_blocks)
+            for src in rest[:far]:
+                parts = decode(src, pl.ds(start, LANES), piece * row_blocks, row_blocks)
                 total = [left + right for left, right in zip(total, parts)]
             lanes = pl.ds(piece * group + start, LANES)
             for block in range(row_blocks):
@@ -288,7 +307,6 @@
     group = col_blocks * CB // pieces
     columns = group * n_cam
     total = row_blocks * n_lm
-    coded = extent + STRIP
     orders = [list(range(bits)), list(reversed(range(bits)))]
     lm, cam = lax.axis_index("lm"), lax.axis_index("cam")
     me = jnp.stack([lm // 2, lm % 2, cam]).astype(jnp.int32)
@@ -319,7 +337,7 @@
     formed = jax.ShapeDtypeStruct((tiles, chips * extent, 2 * WIDTH), jnp.bfloat16)
     whole = pl.BlockSpec(memory_space=pltpu.HBM)
     rows_a, pan_here = pl.pallas_call(
-        functools.partial(form_own_kernel, total),
+        functools.partial(form_own_kernel, (total, row_blocks)),
         in_specs=[SMEM, whole, whole],
         out_specs=[VMEM, VMEM],
         out_shape=[formed, jax.ShapeDtypeStruct(panels.shape, panels.dtype)],
@@ -332,7 +350,7 @@
         name="form_own",
     )(table_a, panels, curvature)
     rows_b = pl.pallas_call(
-        functools.partial(form_kernel, total),
+        functools.partial(form_kernel, (total, row_blocks)),
         in_specs=[SMEM, VMEM, VMEM],
         out_specs=VMEM,
         out_shape=formed,
@@ -341,7 +359,10 @@
     )(table_b, pan_other, cur_other)
 
     def round_call(sending, turn, tables):
-        height, kind = (coded, jnp.int16) if sending else (extent, jnp.float32)
+        if sending:
+            made = jax.ShapeDtypeStruct((chips // 2 * extent + STRIP, columns), jnp.int16)
+        else:
+            made = jax.ShapeDtypeStruct((chips // 2, extent, columns), jnp.float32)
         bases = [(2 * turn + which) * n_cam * per for which in range(2)]
         pairs = columns // LANES
         plan = (sending, bases, orders, total, row_blocks, chips // 2, tiles, pairs)
@@ -349,7 +370,7 @@
             functools.partial(round_kernel, plan),
             in_specs=[SMEM] * 2 + [VMEM] * 4,
             out_specs=[VMEM] * 2,
-            out_shape=[jax.ShapeDtypeStruct((chips // 2, height, columns), kind)] * 2,
+            out_shape=[made] * 2,
             scratch_shapes=[
                 pltpu.VMEM((columns + LANES, 2 * WIDTH), jnp.bfloat16),
                 pltpu.SMEM((pairs + 1,), jnp.int32),
@@ -370,8 +391,7 @@
     result = None
     for turn in range(turns):
         if turn:
-            first_came = [arrays[0] for arrays in came[turn - 1]]
-            sends[turn] = lax.optimization_barrier((sends[turn], first_came))[0]
+            sends[turn] = lax.optimization_barrier((sends[turn], crossed))[0]
         for stage in range(bits):
             for piece in range(2):
                 came[turn][piece].append(swap(sends[turn][piece], orders[piece][stage] + 1))
@@ -380,36 +400,22 @@
                 break
             for piece in range(2):
                 arrays = [keeps[turn][piece]] + came[turn][piece]
-
-                def later(half, block, size=size):
-                    return (size // 2 + half, 0, block)
-
                 sends[turn][piece] = pl.pallas_call(
-                    functools.partial(relay_kernel, row_blocks),
-                    grid=(size // 2, columns // CHUNK),
-                    in_specs=[pl.BlockSpec((1, extent, CHUNK), later)]
-                    + [pl.BlockSpec((1, coded, CHUNK), later)] * (len(arrays) - 1),
-                    out_specs=pl.BlockSpec((1, coded, CHUNK), lambda half, block: (half, 0, block)),
-                    out_shape=jax.ShapeDtypeStruct((size // 2, coded, columns), jnp.int16),
+                    functools.partial(relay_kernel, (row_blocks, size)),
+                    in_specs=[VMEM] * len(arrays),
+                    out_specs=VMEM,
+                    out_shape=jax.ShapeDtypeStruct((size // 2 * extent + STRIP, columns), jnp.int16),
                     compiler_params=PARAMS,
                     name="relay",
                 )(*arrays)
 
         near = [array for piece in range(2) for array in [keeps[turn][piece]] + came[turn][piece]]
         arrays = len(near) // 2
-
-        def first(width):
-            return [
-                pl.BlockSpec((1, coded if pos % arrays else extent, width), lambda step: (0, 0, 0))
-                for pos in range(2 * arrays)
-            ]
-
         crossed = pl.pallas_call(
             functools.partial(cross_kernel, row_blocks, group, arrays),
-            grid=(1,),
-            in_specs=first(columns),
-            out_specs=[pl.BlockSpec((2, coded, group), lambda step: (0, 0, 0))] * (n_cam - 1),
-            out_shape=[jax.ShapeDtypeStruct((2, coded, group), jnp.int16)] * (n_cam - 1),
+            in_specs=[VMEM] * len(near),
+            out_specs=[VMEM] * (n_cam - 1),
+            out_shape=[jax.ShapeDtypeStruct((2 * extent + STRIP, group), jnp.int16)] * (n_cam - 1),
             compiler_params=PARAMS,
             name="cross",
         )(*near)
@@ -419,9 +425,8 @@
         ]
         base = pl.pallas_call(
             functools.partial(base_kernel, (turn, row_blocks, col_blocks, arrays)),
-            grid=(1,),
-            in_specs=[SMEM, VMEM] + first(group),
-            out_specs=pl.BlockSpec((extent, 2 * group), lambda step: (0, 0)),
+            in_specs=[SMEM, VMEM] + [VMEM] * len(near),
+            out_specs=VMEM,
             out_shape=jax.ShapeDtypeStruct((extent, 2 * group), jnp.float32),
             compiler_params=PARAMS,
             name="base",

time: 77.9 us -> 81.7 us (1.049)
  waiting for transfers between devices: 35.7 us -> 25.1 us
  Pallas kernels: 18.5 us -> 27.2 us
  starting transfers between devices: 20.6 us -> 26.1 us
    pallas_call x4, Pallas kernels: 10.6 us -> 19.5 us  [round_call(): pl.pallas_call(functools.partial(round_kernel, plan), in_specs=[SMEM] * 2...]
    ppermute x11, waiting for transfers between devices: 22.4 us -> 14.1 us  [swap(): return lax.ppermute(value, 'lm', [(i, i ^ 1 << bit) for i in range(n_lm)])]
    ppermute x6, starting transfers between devices: 8.01 us -> 11.6 us  [body(): lax.ppermute(value, 'cam', [(i, i ^ pos + 1) for i in range(n_cam)])]
    ppermute x6, waiting for transfers between devices: 13.3 us -> 11 us  [body(): lax.ppermute(value, 'cam', [(i, i ^ pos + 1) for i in range(n_cam)])]
    ppermute x11, starting transfers between devices: 12.6 us -> 14.5 us  [swap(): return lax.ppermute(value, 'lm', [(i, i ^ 1 << bit) for i in range(n_lm)])]
  transfers between devices with their start and end apart: 17 -> 17, of which waited for: 6 -> 7; matrix products, arithmetic and copies ran while one was open for 2% -> 1% of each run, Pallas kernels for 14% -> 20%
where the time goes in v2:
time: 81.7 us; the launch traced here: 81.9 us
  Pallas kernels  27.2 us (33%)
  starting transfers between devices  26.1 us (32%)
  waiting for transfers between devices  25.1 us (31%)
  local copies, waits for them, and re-layouts  2.12 us (3%)
  other arithmetic  1.18 us (1%)
    pallas_call x4, Pallas kernels, round_call(): pl.pallas_call(functools.partial(round_kernel, plan), in_specs=[SMEM] * 2...  19.5 us
    ppermute x11, starting transfers between devices, swap(): return lax.ppermute(value, 'lm', [(i, i ^ 1 << bit) for i in range(n_lm)])  14.5 us
    ppermute x11, waiting for transfers between devices, swap(): return lax.ppermute(value, 'lm', [(i, i ^ 1 << bit) for i in range(n_lm)])  14.1 us
    ppermute x6, starting transfers between devices, body(): lax.ppermute(value, 'cam', [(i, i ^ pos + 1) for i in range(n_cam)])  11.6 us
    ppermute x6, waiting for transfers between devices, body(): lax.ppermute(value, 'cam', [(i, i ^ pos + 1) for i in range(n_cam)])  11 us
    unnamed x6, local copies, waits for them, and re-layouts  2.12 us
    pallas_call x2, Pallas kernels, body(): pl.pallas_call(functools.partial(finish_kernel, row_blocks, n_cam - 1), g...  1.64 us
  transfers between devices with their start and end apart: 17, of which 7 were waited for; matrix products, arithmetic and copies ran while one was open for 1% of the time, Pallas kernels for 20%

profile of v2, /device:TPU:0, one launch (start us, length us, event | category | flops | bytes accessed | tf_op | source)
XLA Modules:
  0.0 81.9 jit_solution(16511795220836339084)
XLA Ops:
  0.0 0.5 collective-permute-start.1
  0.5 0.8 fusion.3
  1.2 0.1 collective-permute-start
  1.3 0.5 collective-permute-start.2
  1.8 0.1 select_reduce_fusion.1.table.table_a
  1.9 0.0 copy-start
  1.9 1.4 %copy-done = bf16[2,16,64,384]{3,2,1,0:T(8,128)(2,1)S(1)} copy-done((bf16[2,16,64,384]{3,2,1,0:T(8,128)(2,1)S(1)}, bf16[2,16,64,384]{3,2,1,0:T(8,128)(2,1)}, u32[]{:S(2)}) %copy-start) | copy-done | bytes 1572888
  3.3 0.0 copy-start.1
  3.3 0.7 copy-done.1
  4.0 1.4 %form_own.1 = (bf16[2,1024,768]{2,1,0:T(8,128)(2,1)S(1)}, bf16[2,16,64,384]{3,2,1,0:T(8,128)(2,1)S(1)}) custom-call(s32[2,48]{1,0:T(2,128)S(1)} %select_reduce_fusion.1.table.table_a, bf16[2,16,64,384]{3,2,1,0:T(8,128)(2,1)S(1)} %copy-done, f32[3,3,256]{2,1,0:T(4,128)S(1)} %copy-done.1), custom_call_target="tpu_custom_call" | custom-call | tf_op jit(solution)/shard_map/form_own/pallas_call | solution.py:339
  5.5 0.0 collective-permute-done
  5.5 0.1 select_reduce_fusion.table.table_b
  5.6 0.0 collective-permute-done.2.cur
  5.6 0.0 collective-permute-done.1.pan.pan_b
  5.6 1.1 %form_other.1.rows_b = bf16[2,1024,768]{2,1,0:T(8,128)(2,1)S(1)} custom-call(s32[2,48]{1,0:T(2,128)S(1)} %select_reduce_fusion.table.table_b, bf16[2,16,64,384]{3,2,1,0:T(8,128)(2,1)S(1)} %collective-permute-done.1.pan.pan_b, f32[3,3,256]{2,1,0:T(4,128)S(1)} %collective-permute-done.2.cur), custom_call_target="tpu_custom_call" | custom-call | tf_op jit(solution)/shard_map/form_other/pallas_call | solution.py:352
  6.8 4.0 %send.2 = (s16[528,512]{1,0:T(8,128)(2,1)S(1)}, s16[528,512]{1,0:T(8,128)(2,1)S(1)}) custom-call(s32[2,48]{1,0:T(2,128)S(1)} %select_reduce_fusion.1.table.table_a, s32[2,48]{1,0:T(2,128)S(1)} %select_reduce_fusion.table.table_b, bf16[2,16,64,384]{3,2,1,0:T(8,128)(2,1)S(1)} %get-tuple-element.29.pan_a, ...), custom_call_target="tpu_custom_call" | custom-call | tf_op jit(solution)/shard_map/send/pallas_call | solution.py:369
  10.8 3.3 %collective-permute-start.5 = (s16[528,512]{1,0:T(8,128)(2,1)S(1)}, s16[528,512]{1,0:T(8,128)(2,1)S(1)}, u32[]{:S(2)}, u32[]{:S(2)}) collective-permute-start(s16[528,512]{1,0:T(8,128)(2,1)S(1)} %get-tuple-element.32), channel_id=1, source_target_pairs={{0,16},{4,20},{8,24},{12,28},{16,0},{20,4},{24,8},{28,12},{1,17},{... | collective-permute-start | bytes 1622024 | tf_op jit(solution)/shard_map/ppermute | solution.py:318
  14.0 1.7 %collective-permute-start.3 = (s16[528,512]{1,0:T(8,128)(2,1)S(1)}, s16[528,512]{1,0:T(8,128)(2,1)S(1)}, u32[]{:S(2)}, u32[]{:S(2)}) collective-permute-start(s16[528,512]{1,0:T(8,128)(2,1)S(1)} %get-tuple-element.31), channel_id=1, source_target_pairs={{0,8},{4,12},{8,0},{12,4},{16,24},{20,28},{24,16},{28,20},{1,9},{5... | collective-permute-start | bytes 1622024 | tf_op jit(solution)/shard_map/ppermute | solution.py:318
  15.7 5.1 %keep.2 = (f32[2,256,512]{2,1,0:T(8,128)S(1)}, f32[2,256,512]{2,1,0:T(8,128)S(1)}) custom-call(s32[2,48]{1,0:T(2,128)S(1)} %select_reduce_fusion.1.table.table_a, s32[2,48]{1,0:T(2,128)S(1)} %select_reduce_fusion.table.table_b, bf16[2,16,64,384]{3,2,1,0:T(8,128)(2,1)S(1)} %get-tuple-element.29.pan_a, ...), custom_call_target="tpu_custom_call" | custom-call | tf_op jit(solution)/shard_map/keep/pallas_call | solution.py:369
  20.8 6.2 %collective-permute-done.5.rest_0_.rest_4_ = s16[528,512]{1,0:T(8,128)(2,1)S(1)} collective-permute-done((s16[528,512]{1,0:T(8,128)(2,1)S(1)}, s16[528,512]{1,0:T(8,128)(2,1)S(1)}, u32[]{:S(2)}, u32[]{:S(2)}) %collective-permute-start.5) | collective-permute-done | bytes 540704 | tf_op jit(solution)/shard_map/ppermute | solution.py:318
  27.1 0.3 relay.5
  27.4 2.6 %collective-permute-start.6 = (s16[272,512]{1,0:T(8,128)(2,1)S(1)}, s16[272,512]{1,0:T(8,128)(2,1)S(1)}, u32[]{:S(2)}, u32[]{:S(2)}) collective-permute-start(s16[272,512]{1,0:T(8,128)(2,1)S(1)} %relay.5), channel_id=1, source_target_pairs={{0,8},{4,12},{8,0},{12,4},{16,24},{20,28},{24,16},{28,20},{1,9},{5... | collective-permute-start | bytes 835592 | tf_op jit(solution)/shard_map/ppermute | solution.py:318
  29.9 0.0 collective-permute-done.3.rest_0_.rest_1_
  29.9 0.3 relay.4
  30.3 1.3 %collective-permute-start.4 = (s16[272,512]{1,0:T(8,128)(2,1)S(1)}, s16[272,512]{1,0:T(8,128)(2,1)S(1)}, u32[]{:S(2)}, u32[]{:S(2)}) collective-permute-start(s16[272,512]{1,0:T(8,128)(2,1)S(1)} %relay.4), channel_id=1, source_target_pairs={{0,16},{4,20},{8,24},{12,28},{16,0},{20,4},{24,8},{28,12},{1,17},{... | collective-permute-start | bytes 835592 | tf_op jit(solution)/shard_map/ppermute | solution.py:318
  31.6 4.3 %send.3 = (s16[528,512]{1,0:T(8,128)(2,1)S(1)}, s16[528,512]{1,0:T(8,128)(2,1)S(1)}) custom-call(s32[2,48]{1,0:T(2,128)S(1)} %select_reduce_fusion.1.table.table_a, s32[2,48]{1,0:T(2,128)S(1)} %select_reduce_fusion.table.table_b, bf16[2,16,64,384]{3,2,1,0:T(8,128)(2,1)S(1)} %get-tuple-element.29.pan_a, ...), custom_call_target="tpu_custom_call" | custom-call | tf_op jit(solution)/shard_map/send/pallas_call | solution.py:369
  35.9 0.3 collective-permute-done.6.rest_5_
  36.2 2.1 %collective-permute-done.4.rest_2_ = s16[272,512]{1,0:T(8,128)(2,1)S(1)} collective-permute-done((s16[272,512]{1,0:T(8,128)(2,1)S(1)}, s16[272,512]{1,0:T(8,128)(2,1)S(1)}, u32[]{:S(2)}, u32[]{:S(2)}) %collective-permute-start.4) | collective-permute-done | bytes 278560 | tf_op jit(solution)/shard_map/ppermute | solution.py:318
  38.3 0.5 cross.2
  38.8 1.2 %collective-permute-start.7 = (s16[528,512]{1,0:T(8,128)(2,1)S(1)}, s16[528,512]{1,0:T(8,128)(2,1)S(1)}, u32[]{:S(2)}, u32[]{:S(2)}) collective-permute-start(s16[528,512]{1,0:T(8,128)(2,1)S(1)} %get-tuple-element.47), channel_id=1, source_target_pairs={{0,8},{4,12},{8,0},{12,4},{16,24},{20,28},{24,16},{28,20},{1,9},{5... | collective-permute-start | bytes 1622024 | tf_op jit(solution)/shard_map/ppermute | solution.py:318
  39.9 1.0 %collective-permute-start.9 = (s16[528,512]{1,0:T(8,128)(2,1)S(1)}, s16[528,512]{1,0:T(8,128)(2,1)S(1)}, u32[]{:S(2)}, u32[]{:S(2)}) collective-permute-start(s16[528,512]{1,0:T(8,128)(2,1)S(1)} %get-tuple-element.49), channel_id=1, source_target_pairs={{0,16},{4,20},{8,24},{12,28},{16,0},{20,4},{24,8},{28,12},{1,17},{... | collective-permute-start | bytes 1622024 | tf_op jit(solution)/shard_map/ppermute | solution.py:318
  40.9 6.1 %keep.3 = (f32[2,256,512]{2,1,0:T(8,128)S(1)}, f32[2,256,512]{2,1,0:T(8,128)S(1)}) custom-call(s32[2,48]{1,0:T(2,128)S(1)} %select_reduce_fusion.1.table.table_a, s32[2,48]{1,0:T(2,128)S(1)} %select_reduce_fusion.table.table_b, bf16[2,16,64,384]{3,2,1,0:T(8,128)(2,1)S(1)} %get-tuple-element.29.pan_a, ...), custom_call_target="tpu_custom_call" | custom-call | tf_op jit(solution)/shard_map/keep/pallas_call | solution.py:369
  47.0 4.8 %collective-permute-done.7.rest_0_.rest_1_ = s16[528,512]{1,0:T(8,128)(2,1)S(1)} collective-permute-done((s16[528,512]{1,0:T(8,128)(2,1)S(1)}, s16[528,512]{1,0:T(8,128)(2,1)S(1)}, u32[]{:S(2)}, u32[]{:S(2)}) %collective-permute-start.7) | collective-permute-done | bytes 540704 | tf_op jit(solution)/shard_map/ppermute | solution.py:318
  51.8 0.3 relay.6
  52.1 2.0 %collective-permute-start.8 = (s16[272,512]{1,0:T(8,128)(2,1)S(1)}, s16[272,512]{1,0:T(8,128)(2,1)S(1)}, u32[]{:S(2)}, u32[]{:S(2)}) collective-permute-start(s16[272,512]{1,0:T(8,128)(2,1)S(1)} %relay.6), channel_id=1, source_target_pairs={{0,16},{4,20},{8,24},{12,28},{16,0},{20,4},{24,8},{28,12},{1,17},{... | collective-permute-start | bytes 835592 | tf_op jit(solution)/shard_map/ppermute | solution.py:318
  54.1 0.0 collective-permute-done.9.rest_0_.rest_4_
  54.1 0.3 relay.7
  54.5 0.0 copy-start.2
  54.5 0.5 collective-permute-start.10
  55.0 0.1 collective-permute-start.14
  55.1 5.3 %collective-permute-start.15 = (s16[528,128]{1,0:T(8,128)(2,1)S(1)}, s16[528,128]{1,0:T(8,128)(2,1)S(1)}, u32[]{:S(2)}, u32[]{:S(2)}) collective-permute-start(s16[528,128]{1,0:T(8,128)(2,1)S(1)} %get-tuple-element.45), channel_id=1, source_target_pairs={{0,2},{1,3},{2,0},{3,1},{4,6},{5,7},{6,4},{7,5},{8,10},{9,11},{10,... | collective-permute-start | bytes 405512 | tf_op jit(solution)/shard_map/ppermute | solution.py:423
  60.4 0.0 collective-permute-start.16
  60.4 0.0 collective-permute-done.8.rest_2_
  60.4 0.7 collective-permute-done.10.rest_5_
  61.1 0.5 cross.3
  61.6 0.1 collective-permute-start.11
  61.7 5.1 %collective-permute-start.12 = (s16[528,128]{1,0:T(8,128)(2,1)S(1)}, s16[528,128]{1,0:T(8,128)(2,1)S(1)}, u32[]{:S(2)}, u32[]{:S(2)}) collective-permute-start(s16[528,128]{1,0:T(8,128)(2,1)S(1)} %get-tuple-element.51), channel_id=1, source_target_pairs={{0,2},{1,3},{2,0},{3,1},{4,6},{5,7},{6,4},{7,5},{8,10},{9,11},{10,... | collective-permute-start | bytes 405512 | tf_op jit(solution)/shard_map/ppermute | solution.py:423
  66.8 0.0 collective-permute-done.14.rest_0_
  66.8 1.0 %collective-permute-start.13 = (s16[528,128]{1,0:T(8,128)(2,1)S(1)}, s16[528,128]{1,0:T(8,128)(2,1)S(1)}, u32[]{:S(2)}, u32[]{:S(2)}) collective-permute-start(s16[528,128]{1,0:T(8,128)(2,1)S(1)} %get-tuple-element.52), channel_id=1, source_target_pairs={{0,3},{1,2},{2,1},{3,0},{4,7},{5,6},{6,5},{7,4},{8,11},{9,10},{10,... | collective-permute-start | bytes 405512 | tf_op jit(solution)/shard_map/ppermute | solution.py:423
  67.8 0.1 pad_add_fusion.me_ref
  67.9 0.0 copy-done.2
  67.9 0.1 pad_maximum_fusion.wide_ref
  68.0 0.6 base.3.base_ref
  68.6 1.5 %collective-permute-done.15.rest_1_ = s16[528,128]{1,0:T(8,128)(2,1)S(1)} collective-permute-done((s16[528,128]{1,0:T(8,128)(2,1)S(1)}, s16[528,128]{1,0:T(8,128)(2,1)S(1)}, u32[]{:S(2)}, u32[]{:S(2)}) %collective-permute-start.15) | collective-permute-done | bytes 135200 | tf_op jit(solution)/shard_map/ppermute | solution.py:423
  70.1 0.0 collective-permute-done.16.rest_2_
  70.1 0.8 %finish.2.rest_3_ = f32[256,512]{1,0:T(8,128)} custom-call(f32[256,256]{1,0:T(8,128)S(1)} %base.3.base_ref, s16[528,128]{1,0:T(8,128)(2,1)S(1)} %collective-permute-done.14.rest_0_, s16[528,128]{1,0:T(8,128)(2,1)S(1)} %collective-permute-done.15.rest_1_, s16[528,128]{1,0:T(8,128)(2,1)S(1)} %collective-permute-done.16.rest_2_), custom_call_target="tpu_custom_call" | custom-call | tf_op jit(solution)/shard_map/finish/pallas_call | solution.py:435
  70.9 0.6 base.2.base_ref
  71.6 0.0 collective-permute-done.11.rest_0_
  71.6 9.5 %collective-permute-done.12.rest_1_ = s16[528,128]{1,0:T(8,128)(2,1)S(1)} collective-permute-done((s16[528,128]{1,0:T(8,128)(2,1)S(1)}, s16[528,128]{1,0:T(8,128)(2,1)S(1)}, u32[]{:S(2)}, u32[]{:S(2)}) %collective-permute-start.12) | collective-permute-done | bytes 135200 | tf_op jit(solution)/shard_map/ppermute | solution.py:423
  81.1 0.0 collective-permute-done.13.rest_2_
  81.1 0.8 %finish.3 = f32[256,512]{1,0:T(8,128)} custom-call(f32[256,256]{1,0:T(8,128)S(1)} %base.2.base_ref, s16[528,128]{1,0:T(8,128)(2,1)S(1)} %collective-permute-done.11.rest_0_, s16[528,128]{1,0:T(8,128)(2,1)S(1)} %collective-permute-done.12.rest_1_, s16[528,128]{1,0:T(8,128)(2,1)S(1)} %collective-permute-done.13.rest_2_, ...), custom_call_target="tpu_custom_call", output_to_operand_aliasing={{}: (4, {})} | custom-call | tf_op jit(solution)/shard_map/finish/pallas_call | solution.py:435
  (2 shorter events, 0.0 us)
Async XLA Ops:
  0.0 5.6 %collective-permute-start.1 = (bf16[2,16,64,384]{3,2,1,0:T(8,128)(2,1)}, bf16[2,16,64,384]{3,2,1,0:T(8,128)(2,1)S(1)}, u32[]{:S(2)}, u32[]{:S(2)}) collective-permute-start(bf16[2,16,64,384]{3,2,1,0:T(8,128)(2,1)} %pan_ref.1), channel_id=1, source_target_pairs={{0,4},{4,0},{8,12},{12,8},{16,20},{20,16},{24,28},{28,24},{1,5},{5... | collective-permute-start | bytes 4718600 | tf_op jit(solution)/shard_map/ppermute | solution.py:318
  1.2 4.2 %collective-permute-start = (s32[2,16]{1,0:T(2,128)S(1)}, s32[2,16]{1,0:T(2,128)S(1)}, u32[]{:S(2)}, u32[]{:S(2)}) collective-permute-start(s32[2,16]{1,0:T(2,128)S(1)} %get-tuple-element.54), channel_id=1, source_target_pairs={{0,4},{4,0},{8,12},{12,8},{16,20},{20,16},{24,28},{28,24},{1,5},{5... | collective-permute-start | bytes 392 | tf_op jit(solution)/shard_map/ppermute | solution.py:318
  1.3 4.2 %collective-permute-start.2 = (f32[3,3,256]{2,1,0:T(4,128)}, f32[3,3,256]{2,1,0:T(4,128)S(1)}, u32[]{:S(2)}, u32[]{:S(2)}) collective-permute-start(f32[3,3,256]{2,1,0:T(4,128)} %cur_ref.1), channel_id=1, source_target_pairs={{0,4},{4,0},{8,12},{12,8},{16,20},{20,16},{24,28},{28,24},{1,5},{5... | collective-permute-start | bytes 27656 | tf_op jit(solution)/shard_map/ppermute | solution.py:318
  1.9 1.4 %copy-start = (bf16[2,16,64,384]{3,2,1,0:T(8,128)(2,1)S(1)}, bf16[2,16,64,384]{3,2,1,0:T(8,128)(2,1)}, u32[]{:S(2)}) copy-start(bf16[2,16,64,384]{3,2,1,0:T(8,128)(2,1)} %pan_ref.1) | copy-start | bytes 4718596
  3.3 0.7 copy-start.1
  10.8 16.3 %collective-permute-start.5 = (s16[528,512]{1,0:T(8,128)(2,1)S(1)}, s16[528,512]{1,0:T(8,128)(2,1)S(1)}, u32[]{:S(2)}, u32[]{:S(2)}) collective-permute-start(s16[528,512]{1,0:T(8,128)(2,1)S(1)} %get-tuple-element.32), channel_id=1, source_target_pairs={{0,16},{4,20},{8,24},{12,28},{16,0},{20,4},{24,8},{28,12},{1,17},{... | collective-permute-start | bytes 1622024 | tf_op jit(solution)/shard_map/ppermute | solution.py:318
  14.0 15.9 %collective-permute-start.3 = (s16[528,512]{1,0:T(8,128)(2,1)S(1)}, s16[528,512]{1,0:T(8,128)(2,1)S(1)}, u32[]{:S(2)}, u32[]{:S(2)}) collective-permute-start(s16[528,512]{1,0:T(8,128)(2,1)S(1)} %get-tuple-element.31), channel_id=1, source_target_pairs={{0,8},{4,12},{8,0},{12,4},{16,24},{20,28},{24,16},{28,20},{1,9},{5... | collective-permute-start | bytes 1622024 | tf_op jit(solution)/shard_map/ppermute | solution.py:318
  27.4 8.8 %collective-permute-start.6 = (s16[272,512]{1,0:T(8,128)(2,1)S(1)}, s16[272,512]{1,0:T(8,128)(2,1)S(1)}, u32[]{:S(2)}, u32[]{:S(2)}) collective-permute-start(s16[272,512]{1,0:T(8,128)(2,1)S(1)} %relay.5), channel_id=1, source_target_pairs={{0,8},{4,12},{8,0},{12,4},{16,24},{20,28},{24,16},{28,20},{1,9},{5... | collective-permute-start | bytes 835592 | tf_op jit(solution)/shard_map/ppermute | solution.py:318
  30.3 8.0 %collective-permute-start.4 = (s16[272,512]{1,0:T(8,128)(2,1)S(1)}, s16[272,512]{1,0:T(8,128)(2,1)S(1)}, u32[]{:S(2)}, u32[]{:S(2)}) collective-permute-start(s16[272,512]{1,0:T(8,128)(2,1)S(1)} %relay.4), channel_id=1, source_target_pairs={{0,16},{4,20},{8,24},{12,28},{16,0},{20,4},{24,8},{28,12},{1,17},{... | collective-permute-start | bytes 835592 | tf_op jit(solution)/shard_map/ppermute | solution.py:318
  38.8 13.0 %collective-permute-start.7 = (s16[528,512]{1,0:T(8,128)(2,1)S(1)}, s16[528,512]{1,0:T(8,128)(2,1)S(1)}, u32[]{:S(2)}, u32[]{:S(2)}) collective-permute-start(s16[528,512]{1,0:T(8,128)(2,1)S(1)} %get-tuple-element.47), channel_id=1, source_target_pairs={{0,8},{4,12},{8,0},{12,4},{16,24},{20,28},{24,16},{28,20},{1,9},{5... | collective-permute-start | bytes 1622024 | tf_op jit(solution)/shard_map/ppermute | solution.py:318
  39.9 14.2 %collective-permute-start.9 = (s16[528,512]{1,0:T(8,128)(2,1)S(1)}, s16[528,512]{1,0:T(8,128)(2,1)S(1)}, u32[]{:S(2)}, u32[]{:S(2)}) collective-permute-start(s16[528,512]{1,0:T(8,128)(2,1)S(1)} %get-tuple-element.49), channel_id=1, source_target_pairs={{0,16},{4,20},{8,24},{12,28},{16,0},{20,4},{24,8},{28,12},{1,17},{... | collective-permute-start | bytes 1622024 | tf_op jit(solution)/shard_map/ppermute | solution.py:318
  52.1 8.3 %collective-permute-start.8 = (s16[272,512]{1,0:T(8,128)(2,1)S(1)}, s16[272,512]{1,0:T(8,128)(2,1)S(1)}, u32[]{:S(2)}, u32[]{:S(2)}) collective-permute-start(s16[272,512]{1,0:T(8,128)(2,1)S(1)} %relay.6), channel_id=1, source_target_pairs={{0,16},{4,20},{8,24},{12,28},{16,0},{20,4},{24,8},{28,12},{1,17},{... | collective-permute-start | bytes 835592 | tf_op jit(solution)/shard_map/ppermute | solution.py:318
  54.5 13.4 %copy-start.2 = (f32[4,64,64]{2,1,0:T(8,128)S(1)}, f32[4,64,64]{2,1,0:T(8,128)}, u32[]{:S(2)}) copy-start(f32[4,64,64]{2,1,0:T(8,128)} %param.9) | copy-start | bytes 196612
  54.5 6.6 %collective-permute-start.10 = (s16[272,512]{1,0:T(8,128)(2,1)S(1)}, s16[272,512]{1,0:T(8,128)(2,1)S(1)}, u32[]{:S(2)}, u32[]{:S(2)}) collective-permute-start(s16[272,512]{1,0:T(8,128)(2,1)S(1)} %relay.7), channel_id=1, source_target_pairs={{0,8},{4,12},{8,0},{12,4},{16,24},{20,28},{24,16},{28,20},{1,9},{5... | collective-permute-start | bytes 835592 | tf_op jit(solution)/shard_map/ppermute | solution.py:318
  55.0 11.8 %collective-permute-start.14 = (s16[528,128]{1,0:T(8,128)(2,1)S(1)}, s16[528,128]{1,0:T(8,128)(2,1)S(1)}, u32[]{:S(2)}, u32[]{:S(2)}) collective-permute-start(s16[528,128]{1,0:T(8,128)(2,1)S(1)} %get-tuple-element.44), channel_id=1, source_target_pairs={{0,1},{1,0},{2,3},{3,2},{4,5},{5,4},{6,7},{7,6},{8,9},{9,8},{10,11... | collective-permute-start | bytes 405512 | tf_op jit(solution)/shard_map/ppermute | solution.py:423
  55.1 15.0 %collective-permute-start.15 = (s16[528,128]{1,0:T(8,128)(2,1)S(1)}, s16[528,128]{1,0:T(8,128)(2,1)S(1)}, u32[]{:S(2)}, u32[]{:S(2)}) collective-permute-start(s16[528,128]{1,0:T(8,128)(2,1)S(1)} %get-tuple-element.45), channel_id=1, source_target_pairs={{0,2},{1,3},{2,0},{3,1},{4,6},{5,7},{6,4},{7,5},{8,10},{9,11},{10,... | collective-permute-start | bytes 405512 | tf_op jit(solution)/shard_map/ppermute | solution.py:423
  60.4 9.8 %collective-permute-start.16 = (s16[528,128]{1,0:T(8,128)(2,1)S(1)}, s16[528,128]{1,0:T(8,128)(2,1)S(1)}, u32[]{:S(2)}, u32[]{:S(2)}) collective-permute-start(s16[528,128]{1,0:T(8,128)(2,1)S(1)} %get-tuple-element.46), channel_id=1, source_target_pairs={{0,3},{1,2},{2,1},{3,0},{4,7},{5,6},{6,5},{7,4},{8,11},{9,10},{10,... | collective-permute-start | bytes 405512 | tf_op jit(solution)/shard_map/ppermute | solution.py:423
  61.6 10.0 %collective-permute-start.11 = (s16[528,128]{1,0:T(8,128)(2,1)S(1)}, s16[528,128]{1,0:T(8,128)(2,1)S(1)}, u32[]{:S(2)}, u32[]{:S(2)}) collective-permute-start(s16[528,128]{1,0:T(8,128)(2,1)S(1)} %get-tuple-element.50), channel_id=1, source_target_pairs={{0,1},{1,0},{2,3},{3,2},{4,5},{5,4},{6,7},{7,6},{8,9},{9,8},{10,11... | collective-permute-start | bytes 405512 | tf_op jit(solution)/shard_map/ppermute | solution.py:423
  61.7 19.4 %collective-permute-start.12 = (s16[528,128]{1,0:T(8,128)(2,1)S(1)}, s16[528,128]{1,0:T(8,128)(2,1)S(1)}, u32[]{:S(2)}, u32[]{:S(2)}) collective-permute-start(s16[528,128]{1,0:T(8,128)(2,1)S(1)} %get-tuple-element.51), channel_id=1, source_target_pairs={{0,2},{1,3},{2,0},{3,1},{4,6},{5,7},{6,4},{7,5},{8,10},{9,11},{10,... | collective-permute-start | bytes 405512 | tf_op jit(solution)/shard_map/ppermute | solution.py:423
  66.8 14.3 %collective-permute-start.13 = (s16[528,128]{1,0:T(8,128)(2,1)S(1)}, s16[528,128]{1,0:T(8,128)(2,1)S(1)}, u32[]{:S(2)}, u32[]{:S(2)}) collective-permute-start(s16[528,128]{1,0:T(8,128)(2,1)S(1)} %get-tuple-element.52), channel_id=1, source_target_pairs={{0,3},{1,2},{2,1},{3,0},{4,7},{5,6},{6,5},{7,4},{8,11},{9,10},{10,... | collective-permute-start | bytes 405512 | tf_op jit(solution)/shard_map/ppermute | solution.py:423

commit v3 on v2

--- a/solution.py
+++ b/solution.py
@@ -14,6 +14,7 @@
 WIDTH = 3 * LMB
 STRIP = 16
 LANES = 128
+WIDE = 256
 VMEM = pl.BlockSpec(memory_space=pltpu.VMEM)
 SMEM = pl.BlockSpec(memory_space=pltpu.SMEM)
 PARAMS = pltpu.CompilerParams(vmem_limit_bytes=32 * 1024 * 1024)
@@ -38,8 +39,8 @@
 
 def encode(dst, lanes, parts):
     blocks = len(parts)
-    row = lax.broadcasted_iota(jnp.int32, (STRIP, LANES), 0)
-    tops = jnp.full((STRIP, LANES), 2.0**-100, jnp.float32)
+    row = lax.broadcasted_iota(jnp.int32, (STRIP, lanes.size), 0)
+    tops = jnp.full((STRIP, lanes.size), 2.0**-100, jnp.float32)
     for block, part in enumerate(parts):
         top = jnp.max(jnp.abs(part()), axis=0, keepdims=True)
         tops = jnp.where(row == block, jnp.maximum(top, tops), tops)
@@ -215,7 +216,7 @@
             lax.fori_loop(0, tiles, one_tile, 0)
 
         def store(start, carry):
-            lanes = pl.ds(pl.multiple_of(start * LANES, LANES), LANES)
+            lanes = pl.ds(pl.multiple_of(start * WIDE, WIDE), WIDE)
             if sending:
                 parts = [
                     functools.partial(
@@ -230,7 +231,7 @@
                     out[half, :, lanes] = acc[half, :, lanes]
             return carry
 
-        lax.fori_loop(0, pairs, store, 0)
+        lax.fori_loop(0, columns // WIDE, store, 0)
 
 
 def relay_kernel(plan, keep, *rest):
@@ -238,14 +239,14 @@
     dst = rest[-1]
 
     def code(start, carry):
-        lanes = pl.ds(pl.multiple_of(start * LANES, LANES), LANES)
+        lanes = pl.ds(pl.multiple_of(start * WIDE, WIDE), WIDE)
         parts = []
         for place in range(size // 2, size):
             parts += given(gathered(place, keep, rest[:-1], lanes, row_blocks))
         encode(dst, lanes, parts)
         return carry
 
-    lax.fori_loop(0, dst.shape[1] // LANES, code, 0)
+    lax.fori_loop(0, dst.shape[1] // WIDE, code, 0)
 
 
 def cross_kernel(row_blocks, group, arrays, *rest):
@@ -399,7 +400,10 @@
             if size == 1:
                 break
             for piece in range(2):
-                arrays = [keeps[turn][piece]] + came[turn][piece]
+                keep = keeps[turn][piece]
+                if turn:
+                    keep = lax.optimization_barrier((keep, far))[0]
+                arrays = [keep] + came[turn][piece]
                 sends[turn][piece] = pl.pallas_call(
                     functools.partial(relay_kernel, (row_blocks, size)),
                     in_specs=[VMEM] * len(arrays),

time: 81.7 us -> 77.9 us (0.953)
  Pallas kernels: 27.2 us -> 24.3 us
  starting transfers between devices: 26.1 us -> 24.9 us
    pallas_call x4, Pallas kernels: 19.5 us -> 16.8 us  [round_call(): pl.pallas_call(functools.partial(round_kernel, plan), in_specs=[SMEM] * 2...]
    ppermute x11, starting transfers between devices: 14.5 us -> 12.1 us  [swap(): return lax.ppermute(value, 'lm', [(i, i ^ 1 << bit) for i in range(n_lm)])]
    ppermute x6, starting transfers between devices: 11.6 us -> 12.8 us  [body(): lax.ppermute(value, 'cam', [(i, i ^ pos + 1) for i in range(n_cam)])]
    ppermute x11, waiting for transfers between devices: 14.1 us -> 15 us  [swap(): return lax.ppermute(value, 'lm', [(i, i ^ 1 << bit) for i in range(n_lm)])]
  transfers between devices with their start and end apart: 17 -> 17, of which waited for: 7 -> 8; matrix products, arithmetic and copies ran while one was open for 1% -> 2% of each run, Pallas kernels for 20% -> 17%
where the time goes in v3:
time: 77.9 us; the launch traced here: 77.8 us
  waiting for transfers between devices  25.1 us (32%)
  starting transfers between devices  24.9 us (32%)
  Pallas kernels  24.3 us (31%)
  local copies, waits for them, and re-layouts  2.12 us (3%)
  other arithmetic  1.18 us (2%)
    pallas_call x4, Pallas kernels, round_call(): pl.pallas_call(functools.partial(round_kernel, plan), in_specs=[SMEM] * 2...  16.8 us
    ppermute x11, waiting for transfers between devices, swap(): return lax.ppermute(value, 'lm', [(i, i ^ 1 << bit) for i in range(n_lm)])  15 us
    ppermute x6, starting transfers between devices, body(): lax.ppermute(value, 'cam', [(i, i ^ pos + 1) for i in range(n_cam)])  12.8 us
    ppermute x11, starting transfers between devices, swap(): return lax.ppermute(value, 'lm', [(i, i ^ 1 << bit) for i in range(n_lm)])  12.1 us
    ppermute x6, waiting for transfers between devices, body(): lax.ppermute(value, 'cam', [(i, i ^ pos + 1) for i in range(n_cam)])  10.1 us
    unnamed x6, local copies, waits for them, and re-layouts  2.12 us
    pallas_call x2, Pallas kernels, body(): pl.pallas_call(functools.partial(finish_kernel, row_blocks, n_cam - 1), g...  1.64 us
  transfers between devices with their start and end apart: 17, of which 8 were waited for; matrix products, arithmetic and copies ran while one was open for 2% of the time, Pallas kernels for 17%

profile of v3, /device:TPU:0, one launch (start us, length us, event | category | flops | bytes accessed | tf_op | source)
XLA Modules:
  0.0 77.8 jit_solution(308535825487611870)
XLA Ops:
  0.0 0.5 collective-permute-start.1
  0.5 0.8 fusion.3
  1.2 0.1 collective-permute-start
  1.3 0.5 collective-permute-start.2
  1.8 0.1 select_reduce_fusion.1.table.table_a
  1.9 0.0 copy-start
  1.9 1.4 %copy-done = bf16[2,16,64,384]{3,2,1,0:T(8,128)(2,1)S(1)} copy-done((bf16[2,16,64,384]{3,2,1,0:T(8,128)(2,1)S(1)}, bf16[2,16,64,384]{3,2,1,0:T(8,128)(2,1)}, u32[]{:S(2)}) %copy-start) | copy-done | bytes 1572888
  3.3 0.0 copy-start.1
  3.3 0.7 copy-done.1
  4.0 1.3 %form_own.1 = (bf16[2,1024,768]{2,1,0:T(8,128)(2,1)S(1)}, bf16[2,16,64,384]{3,2,1,0:T(8,128)(2,1)S(1)}) custom-call(s32[2,48]{1,0:T(2,128)S(1)} %select_reduce_fusion.1.table.table_a, bf16[2,16,64,384]{3,2,1,0:T(8,128)(2,1)S(1)} %copy-done, f32[3,3,256]{2,1,0:T(4,128)S(1)} %copy-done.1), custom_call_target="tpu_custom_call" | custom-call | tf_op jit(solution)/shard_map/form_own/pallas_call | solution.py:340
  5.4 0.0 collective-permute-done
  5.4 0.1 select_reduce_fusion.table.table_b
  5.5 0.0 collective-permute-done.2.cur
  5.5 0.0 collective-permute-done.1.pan.pan_b
  5.5 1.3 %form_other.1.rows_b = bf16[2,1024,768]{2,1,0:T(8,128)(2,1)S(1)} custom-call(s32[2,48]{1,0:T(2,128)S(1)} %select_reduce_fusion.table.table_b, bf16[2,16,64,384]{3,2,1,0:T(8,128)(2,1)S(1)} %collective-permute-done.1.pan.pan_b, f32[3,3,256]{2,1,0:T(4,128)S(1)} %collective-permute-done.2.cur), custom_call_target="tpu_custom_call" | custom-call | tf_op jit(solution)/shard_map/form_other/pallas_call | solution.py:353
  6.8 4.3 %send.2 = (s16[528,512]{1,0:T(8,128)(2,1)S(1)}, s16[528,512]{1,0:T(8,128)(2,1)S(1)}) custom-call(s32[2,48]{1,0:T(2,128)S(1)} %select_reduce_fusion.1.table.table_a, s32[2,48]{1,0:T(2,128)S(1)} %select_reduce_fusion.table.table_b, bf16[2,16,64,384]{3,2,1,0:T(8,128)(2,1)S(1)} %get-tuple-element.31.pan_a, ...), custom_call_target="tpu_custom_call" | custom-call | tf_op jit(solution)/shard_map/send/pallas_call | solution.py:370
  11.1 3.7 %collective-permute-start.5 = (s16[528,512]{1,0:T(8,128)(2,1)S(1)}, s16[528,512]{1,0:T(8,128)(2,1)S(1)}, u32[]{:S(2)}, u32[]{:S(2)}) collective-permute-start(s16[528,512]{1,0:T(8,128)(2,1)S(1)} %get-tuple-element.34), channel_id=1, source_target_pairs={{0,16},{4,20},{8,24},{12,28},{16,0},{20,4},{24,8},{28,12},{1,17},{... | collective-permute-start | bytes 1622024 | tf_op jit(solution)/shard_map/ppermute | solution.py:319
  14.8 0.3 collective-permute-start.3
  15.2 4.6 %keep.2 = (f32[2,256,512]{2,1,0:T(8,128)S(1)}, f32[2,256,512]{2,1,0:T(8,128)S(1)}) custom-call(s32[2,48]{1,0:T(2,128)S(1)} %select_reduce_fusion.1.table.table_a, s32[2,48]{1,0:T(2,128)S(1)} %select_reduce_fusion.table.table_b, bf16[2,16,64,384]{3,2,1,0:T(8,128)(2,1)S(1)} %get-tuple-element.31.pan_a, ...), custom_call_target="tpu_custom_call" | custom-call | tf_op jit(solution)/shard_map/keep/pallas_call | solution.py:370
  19.8 7.2 %collective-permute-done.5.rest_0_.rest_4_ = s16[528,512]{1,0:T(8,128)(2,1)S(1)} collective-permute-done((s16[528,512]{1,0:T(8,128)(2,1)S(1)}, s16[528,512]{1,0:T(8,128)(2,1)S(1)}, u32[]{:S(2)}, u32[]{:S(2)}) %collective-permute-start.5) | collective-permute-done | bytes 540704 | tf_op jit(solution)/shard_map/ppermute | solution.py:319
  27.0 0.2 relay.5
  27.2 1.3 %collective-permute-start.6 = (s16[272,512]{1,0:T(8,128)(2,1)S(1)}, s16[272,512]{1,0:T(8,128)(2,1)S(1)}, u32[]{:S(2)}, u32[]{:S(2)}) collective-permute-start(s16[272,512]{1,0:T(8,128)(2,1)S(1)} %relay.5), channel_id=1, source_target_pairs={{0,8},{4,12},{8,0},{12,4},{16,24},{20,28},{24,16},{28,20},{1,9},{5... | collective-permute-start | bytes 835592 | tf_op jit(solution)/shard_map/ppermute | solution.py:319
  28.5 0.0 collective-permute-done.3.rest_0_.rest_1_
  28.5 0.2 relay.4
  28.8 0.6 collective-permute-start.4
  29.4 3.8 %send.3 = (s16[528,512]{1,0:T(8,128)(2,1)S(1)}, s16[528,512]{1,0:T(8,128)(2,1)S(1)}) custom-call(s32[2,48]{1,0:T(2,128)S(1)} %select_reduce_fusion.1.table.table_a, s32[2,48]{1,0:T(2,128)S(1)} %select_reduce_fusion.table.table_b, bf16[2,16,64,384]{3,2,1,0:T(8,128)(2,1)S(1)} %get-tuple-element.31.pan_a, ...), custom_call_target="tpu_custom_call" | custom-call | tf_op jit(solution)/shard_map/send/pallas_call | solution.py:370
  33.2 1.7 %collective-permute-done.6.rest_5_ = s16[272,512]{1,0:T(8,128)(2,1)S(1)} collective-permute-done((s16[272,512]{1,0:T(8,128)(2,1)S(1)}, s16[272,512]{1,0:T(8,128)(2,1)S(1)}, u32[]{:S(2)}, u32[]{:S(2)}) %collective-permute-start.6) | collective-permute-done | bytes 278560 | tf_op jit(solution)/shard_map/ppermute | solution.py:319
  34.9 0.8 %collective-permute-done.4.rest_2_ = s16[272,512]{1,0:T(8,128)(2,1)S(1)} collective-permute-done((s16[272,512]{1,0:T(8,128)(2,1)S(1)}, s16[272,512]{1,0:T(8,128)(2,1)S(1)}, u32[]{:S(2)}, u32[]{:S(2)}) %collective-permute-start.4) | collective-permute-done | bytes 278560 | tf_op jit(solution)/shard_map/ppermute | solution.py:319
  35.8 0.5 cross.2
  36.2 1.3 %collective-permute-start.7 = (s16[528,512]{1,0:T(8,128)(2,1)S(1)}, s16[528,512]{1,0:T(8,128)(2,1)S(1)}, u32[]{:S(2)}, u32[]{:S(2)}) collective-permute-start(s16[528,512]{1,0:T(8,128)(2,1)S(1)} %get-tuple-element.49), channel_id=1, source_target_pairs={{0,8},{4,12},{8,0},{12,4},{16,24},{20,28},{24,16},{28,20},{1,9},{5... | collective-permute-start | bytes 1622024 | tf_op jit(solution)/shard_map/ppermute | solution.py:319
  37.5 1.4 %collective-permute-start.12 = (s16[528,512]{1,0:T(8,128)(2,1)S(1)}, s16[528,512]{1,0:T(8,128)(2,1)S(1)}, u32[]{:S(2)}, u32[]{:S(2)}) collective-permute-start(s16[528,512]{1,0:T(8,128)(2,1)S(1)} %get-tuple-element.52), channel_id=1, source_target_pairs={{0,16},{4,20},{8,24},{12,28},{16,0},{20,4},{24,8},{28,12},{1,17},{... | collective-permute-start | bytes 1622024 | tf_op jit(solution)/shard_map/ppermute | solution.py:319
  39.0 3.0 %collective-permute-start.8 = (s16[528,128]{1,0:T(8,128)(2,1)S(1)}, s16[528,128]{1,0:T(8,128)(2,1)S(1)}, u32[]{:S(2)}, u32[]{:S(2)}) collective-permute-start(s16[528,128]{1,0:T(8,128)(2,1)S(1)} %get-tuple-element.46), channel_id=1, source_target_pairs={{0,1},{1,0},{2,3},{3,2},{4,5},{5,4},{6,7},{7,6},{8,9},{9,8},{10,11... | collective-permute-start | bytes 405512 | tf_op jit(solution)/shard_map/ppermute | solution.py:427
  42.0 2.6 %collective-permute-start.9 = (s16[528,128]{1,0:T(8,128)(2,1)S(1)}, s16[528,128]{1,0:T(8,128)(2,1)S(1)}, u32[]{:S(2)}, u32[]{:S(2)}) collective-permute-start(s16[528,128]{1,0:T(8,128)(2,1)S(1)} %get-tuple-element.47), channel_id=1, source_target_pairs={{0,2},{1,3},{2,0},{3,1},{4,6},{5,7},{6,4},{7,5},{8,10},{9,11},{10,... | collective-permute-start | bytes 405512 | tf_op jit(solution)/shard_map/ppermute | solution.py:427
  44.5 1.4 %collective-permute-start.10 = (s16[528,128]{1,0:T(8,128)(2,1)S(1)}, s16[528,128]{1,0:T(8,128)(2,1)S(1)}, u32[]{:S(2)}, u32[]{:S(2)}) collective-permute-start(s16[528,128]{1,0:T(8,128)(2,1)S(1)} %get-tuple-element.48), channel_id=1, source_target_pairs={{0,3},{1,2},{2,1},{3,0},{4,7},{5,6},{6,5},{7,4},{8,11},{9,10},{10,... | collective-permute-start | bytes 405512 | tf_op jit(solution)/shard_map/ppermute | solution.py:427
  45.9 4.1 %keep.3 = (f32[2,256,512]{2,1,0:T(8,128)S(1)}, f32[2,256,512]{2,1,0:T(8,128)S(1)}) custom-call(s32[2,48]{1,0:T(2,128)S(1)} %select_reduce_fusion.1.table.table_a, s32[2,48]{1,0:T(2,128)S(1)} %select_reduce_fusion.table.table_b, bf16[2,16,64,384]{3,2,1,0:T(8,128)(2,1)S(1)} %get-tuple-element.31.pan_a, ...), custom_call_target="tpu_custom_call" | custom-call | tf_op jit(solution)/shard_map/keep/pallas_call | solution.py:370
  50.1 0.0 collective-permute-done.8.rest_0_
  50.1 4.3 %collective-permute-done.9.rest_1_ = s16[528,128]{1,0:T(8,128)(2,1)S(1)} collective-permute-done((s16[528,128]{1,0:T(8,128)(2,1)S(1)}, s16[528,128]{1,0:T(8,128)(2,1)S(1)}, u32[]{:S(2)}, u32[]{:S(2)}) %collective-permute-start.9) | collective-permute-done | bytes 135200 | tf_op jit(solution)/shard_map/ppermute | solution.py:427
  54.4 0.0 collective-permute-done.10.rest_2_
  54.4 0.0 collective-permute-done.7.rest_0_.rest_1_
  54.4 0.2 relay.6
  54.7 0.9 %collective-permute-start.11 = (s16[272,512]{1,0:T(8,128)(2,1)S(1)}, s16[272,512]{1,0:T(8,128)(2,1)S(1)}, u32[]{:S(2)}, u32[]{:S(2)}) collective-permute-start(s16[272,512]{1,0:T(8,128)(2,1)S(1)} %relay.6), channel_id=1, source_target_pairs={{0,16},{4,20},{8,24},{12,28},{16,0},{20,4},{24,8},{28,12},{1,17},{... | collective-permute-start | bytes 835592 | tf_op jit(solution)/shard_map/ppermute | solution.py:319
  55.6 0.0 collective-permute-done.12.rest_0_.rest_4_
  55.6 0.2 relay.7
  55.9 0.0 copy-start.2
  55.9 1.4 %collective-permute-start.13 = (s16[272,512]{1,0:T(8,128)(2,1)S(1)}, s16[272,512]{1,0:T(8,128)(2,1)S(1)}, u32[]{:S(2)}, u32[]{:S(2)}) collective-permute-start(s16[272,512]{1,0:T(8,128)(2,1)S(1)} %relay.7), channel_id=1, source_target_pairs={{0,8},{4,12},{8,0},{12,4},{16,24},{20,28},{24,16},{28,20},{1,9},{5... | collective-permute-start | bytes 835592 | tf_op jit(solution)/shard_map/ppermute | solution.py:319
  57.3 3.9 %collective-permute-done.11.rest_2_ = s16[272,512]{1,0:T(8,128)(2,1)S(1)} collective-permute-done((s16[272,512]{1,0:T(8,128)(2,1)S(1)}, s16[272,512]{1,0:T(8,128)(2,1)S(1)}, u32[]{:S(2)}, u32[]{:S(2)}) %collective-permute-start.11) | collective-permute-done | bytes 278560 | tf_op jit(solution)/shard_map/ppermute | solution.py:319
  61.3 1.2 %collective-permute-done.13.rest_5_ = s16[272,512]{1,0:T(8,128)(2,1)S(1)} collective-permute-done((s16[272,512]{1,0:T(8,128)(2,1)S(1)}, s16[272,512]{1,0:T(8,128)(2,1)S(1)}, u32[]{:S(2)}, u32[]{:S(2)}) %collective-permute-start.13) | collective-permute-done | bytes 278560 | tf_op jit(solution)/shard_map/ppermute | solution.py:319
  62.5 0.5 cross.3
  63.0 3.4 %collective-permute-start.14 = (s16[528,128]{1,0:T(8,128)(2,1)S(1)}, s16[528,128]{1,0:T(8,128)(2,1)S(1)}, u32[]{:S(2)}, u32[]{:S(2)}) collective-permute-start(s16[528,128]{1,0:T(8,128)(2,1)S(1)} %get-tuple-element.54), channel_id=1, source_target_pairs={{0,1},{1,0},{2,3},{3,2},{4,5},{5,4},{6,7},{7,6},{8,9},{9,8},{10,11... | collective-permute-start | bytes 405512 | tf_op jit(solution)/shard_map/ppermute | solution.py:427
  66.4 0.0 collective-permute-start.15
  66.4 2.4 %collective-permute-start.16 = (s16[528,128]{1,0:T(8,128)(2,1)S(1)}, s16[528,128]{1,0:T(8,128)(2,1)S(1)}, u32[]{:S(2)}, u32[]{:S(2)}) collective-permute-start(s16[528,128]{1,0:T(8,128)(2,1)S(1)} %get-tuple-element.56), channel_id=1, source_target_pairs={{0,3},{1,2},{2,1},{3,0},{4,7},{5,6},{6,5},{7,4},{8,11},{9,10},{10,... | collective-permute-start | bytes 405512 | tf_op jit(solution)/shard_map/ppermute | solution.py:427
  68.8 0.1 pad_add_fusion.me_ref
  68.9 0.0 copy-done.2
  68.9 0.1 pad_maximum_fusion.wide_ref
  69.0 0.6 base.3.base_ref
  69.6 0.8 %finish.2.rest_3_ = f32[256,512]{1,0:T(8,128)} custom-call(f32[256,256]{1,0:T(8,128)S(1)} %base.3.base_ref, s16[528,128]{1,0:T(8,128)(2,1)S(1)} %collective-permute-done.8.rest_0_, s16[528,128]{1,0:T(8,128)(2,1)S(1)} %collective-permute-done.9.rest_1_, s16[528,128]{1,0:T(8,128)(2,1)S(1)} %collective-permute-done.10.rest_2_), custom_call_target="tpu_custom_call" | custom-call | tf_op jit(solution)/shard_map/finish/pallas_call | solution.py:439
  70.5 0.6 base.2.base_ref
  71.1 1.1 %collective-permute-done.14.rest_0_ = s16[528,128]{1,0:T(8,128)(2,1)S(1)} collective-permute-done((s16[528,128]{1,0:T(8,128)(2,1)S(1)}, s16[528,128]{1,0:T(8,128)(2,1)S(1)}, u32[]{:S(2)}, u32[]{:S(2)}) %collective-permute-start.14) | collective-permute-done | bytes 135200 | tf_op jit(solution)/shard_map/ppermute | solution.py:427
  72.2 4.7 %collective-permute-done.15.rest_1_ = s16[528,128]{1,0:T(8,128)(2,1)S(1)} collective-permute-done((s16[528,128]{1,0:T(8,128)(2,1)S(1)}, s16[528,128]{1,0:T(8,128)(2,1)S(1)}, u32[]{:S(2)}, u32[]{:S(2)}) %collective-permute-start.15) | collective-permute-done | bytes 135200 | tf_op jit(solution)/shard_map/ppermute | solution.py:427
  76.9 0.0 collective-permute-done.16.rest_2_
  76.9 0.8 %finish.3 = f32[256,512]{1,0:T(8,128)} custom-call(f32[256,256]{1,0:T(8,128)S(1)} %base.2.base_ref, s16[528,128]{1,0:T(8,128)(2,1)S(1)} %collective-permute-done.14.rest_0_, s16[528,128]{1,0:T(8,128)(2,1)S(1)} %collective-permute-done.15.rest_1_, s16[528,128]{1,0:T(8,128)(2,1)S(1)} %collective-permute-done.16.rest_2_, ...), custom_call_target="tpu_custom_call", output_to_operand_aliasing={{}: (4, {})} | custom-call | tf_op jit(solution)/shard_map/finish/pallas_call | solution.py:439
  (2 shorter events, 0.0 us)
Async XLA Ops:
  0.0 5.5 %collective-permute-start.1 = (bf16[2,16,64,384]{3,2,1,0:T(8,128)(2,1)}, bf16[2,16,64,384]{3,2,1,0:T(8,128)(2,1)S(1)}, u32[]{:S(2)}, u32[]{:S(2)}) collective-permute-start(bf16[2,16,64,384]{3,2,1,0:T(8,128)(2,1)} %pan_ref.1), channel_id=1, source_target_pairs={{0,4},{4,0},{8,12},{12,8},{16,20},{20,16},{24,28},{28,24},{1,5},{5... | collective-permute-start | bytes 4718600 | tf_op jit(solution)/shard_map/ppermute | solution.py:319
  1.2 4.1 %collective-permute-start = (s32[2,16]{1,0:T(2,128)S(1)}, s32[2,16]{1,0:T(2,128)S(1)}, u32[]{:S(2)}, u32[]{:S(2)}) collective-permute-start(s32[2,16]{1,0:T(2,128)S(1)} %get-tuple-element.58), channel_id=1, source_target_pairs={{0,4},{4,0},{8,12},{12,8},{16,20},{20,16},{24,28},{28,24},{1,5},{5... | collective-permute-start | bytes 392 | tf_op jit(solution)/shard_map/ppermute | solution.py:319
  1.3 4.2 %collective-permute-start.2 = (f32[3,3,256]{2,1,0:T(4,128)}, f32[3,3,256]{2,1,0:T(4,128)S(1)}, u32[]{:S(2)}, u32[]{:S(2)}) collective-permute-start(f32[3,3,256]{2,1,0:T(4,128)} %cur_ref.1), channel_id=1, source_target_pairs={{0,4},{4,0},{8,12},{12,8},{16,20},{20,16},{24,28},{28,24},{1,5},{5... | collective-permute-start | bytes 27656 | tf_op jit(solution)/shard_map/ppermute | solution.py:319
  1.9 1.4 %copy-start = (bf16[2,16,64,384]{3,2,1,0:T(8,128)(2,1)S(1)}, bf16[2,16,64,384]{3,2,1,0:T(8,128)(2,1)}, u32[]{:S(2)}) copy-start(bf16[2,16,64,384]{3,2,1,0:T(8,128)(2,1)} %pan_ref.1) | copy-start | bytes 4718596
  3.3 0.7 copy-start.1
  11.1 15.8 %collective-permute-start.5 = (s16[528,512]{1,0:T(8,128)(2,1)S(1)}, s16[528,512]{1,0:T(8,128)(2,1)S(1)}, u32[]{:S(2)}, u32[]{:S(2)}) collective-permute-start(s16[528,512]{1,0:T(8,128)(2,1)S(1)} %get-tuple-element.34), channel_id=1, source_target_pairs={{0,16},{4,20},{8,24},{12,28},{16,0},{20,4},{24,8},{28,12},{1,17},{... | collective-permute-start | bytes 1622024 | tf_op jit(solution)/shard_map/ppermute | solution.py:319
  14.8 13.7 %collective-permute-start.3 = (s16[528,512]{1,0:T(8,128)(2,1)S(1)}, s16[528,512]{1,0:T(8,128)(2,1)S(1)}, u32[]{:S(2)}, u32[]{:S(2)}) collective-permute-start(s16[528,512]{1,0:T(8,128)(2,1)S(1)} %get-tuple-element.33), channel_id=1, source_target_pairs={{0,8},{4,12},{8,0},{12,4},{16,24},{20,28},{24,16},{28,20},{1,9},{5... | collective-permute-start | bytes 1622024 | tf_op jit(solution)/shard_map/ppermute | solution.py:319
  27.2 7.7 %collective-permute-start.6 = (s16[272,512]{1,0:T(8,128)(2,1)S(1)}, s16[272,512]{1,0:T(8,128)(2,1)S(1)}, u32[]{:S(2)}, u32[]{:S(2)}) collective-permute-start(s16[272,512]{1,0:T(8,128)(2,1)S(1)} %relay.5), channel_id=1, source_target_pairs={{0,8},{4,12},{8,0},{12,4},{16,24},{20,28},{24,16},{28,20},{1,9},{5... | collective-permute-start | bytes 835592 | tf_op jit(solution)/shard_map/ppermute | solution.py:319
  28.8 7.0 %collective-permute-start.4 = (s16[272,512]{1,0:T(8,128)(2,1)S(1)}, s16[272,512]{1,0:T(8,128)(2,1)S(1)}, u32[]{:S(2)}, u32[]{:S(2)}) collective-permute-start(s16[272,512]{1,0:T(8,128)(2,1)S(1)} %relay.4), channel_id=1, source_target_pairs={{0,16},{4,20},{8,24},{12,28},{16,0},{20,4},{24,8},{28,12},{1,17},{... | collective-permute-start | bytes 835592 | tf_op jit(solution)/shard_map/ppermute | solution.py:319
  36.2 18.2 %collective-permute-start.7 = (s16[528,512]{1,0:T(8,128)(2,1)S(1)}, s16[528,512]{1,0:T(8,128)(2,1)S(1)}, u32[]{:S(2)}, u32[]{:S(2)}) collective-permute-start(s16[528,512]{1,0:T(8,128)(2,1)S(1)} %get-tuple-element.49), channel_id=1, source_target_pairs={{0,8},{4,12},{8,0},{12,4},{16,24},{20,28},{24,16},{28,20},{1,9},{5... | collective-permute-start | bytes 1622024 | tf_op jit(solution)/shard_map/ppermute | solution.py:319
  37.5 18.1 %collective-permute-start.12 = (s16[528,512]{1,0:T(8,128)(2,1)S(1)}, s16[528,512]{1,0:T(8,128)(2,1)S(1)}, u32[]{:S(2)}, u32[]{:S(2)}) collective-permute-start(s16[528,512]{1,0:T(8,128)(2,1)S(1)} %get-tuple-element.52), channel_id=1, source_target_pairs={{0,16},{4,20},{8,24},{12,28},{16,0},{20,4},{24,8},{28,12},{1,17},{... | collective-permute-start | bytes 1622024 | tf_op jit(solution)/shard_map/ppermute | solution.py:319
  39.0 11.1 %collective-permute-start.8 = (s16[528,128]{1,0:T(8,128)(2,1)S(1)}, s16[528,128]{1,0:T(8,128)(2,1)S(1)}, u32[]{:S(2)}, u32[]{:S(2)}) collective-permute-start(s16[528,128]{1,0:T(8,128)(2,1)S(1)} %get-tuple-element.46), channel_id=1, source_target_pairs={{0,1},{1,0},{2,3},{3,2},{4,5},{5,4},{6,7},{7,6},{8,9},{9,8},{10,11... | collective-permute-start | bytes 405512 | tf_op jit(solution)/shard_map/ppermute | solution.py:427
  42.0 12.4 %collective-permute-start.9 = (s16[528,128]{1,0:T(8,128)(2,1)S(1)}, s16[528,128]{1,0:T(8,128)(2,1)S(1)}, u32[]{:S(2)}, u32[]{:S(2)}) collective-permute-start(s16[528,128]{1,0:T(8,128)(2,1)S(1)} %get-tuple-element.47), channel_id=1, source_target_pairs={{0,2},{1,3},{2,0},{3,1},{4,6},{5,7},{6,4},{7,5},{8,10},{9,11},{10,... | collective-permute-start | bytes 405512 | tf_op jit(solution)/shard_map/ppermute | solution.py:427
  44.5 9.9 %collective-permute-start.10 = (s16[528,128]{1,0:T(8,128)(2,1)S(1)}, s16[528,128]{1,0:T(8,128)(2,1)S(1)}, u32[]{:S(2)}, u32[]{:S(2)}) collective-permute-start(s16[528,128]{1,0:T(8,128)(2,1)S(1)} %get-tuple-element.48), channel_id=1, source_target_pairs={{0,3},{1,2},{2,1},{3,0},{4,7},{5,6},{6,5},{7,4},{8,11},{9,10},{10,... | collective-permute-start | bytes 405512 | tf_op jit(solution)/shard_map/ppermute | solution.py:427
  54.7 6.6 %collective-permute-start.11 = (s16[272,512]{1,0:T(8,128)(2,1)S(1)}, s16[272,512]{1,0:T(8,128)(2,1)S(1)}, u32[]{:S(2)}, u32[]{:S(2)}) collective-permute-start(s16[272,512]{1,0:T(8,128)(2,1)S(1)} %relay.6), channel_id=1, source_target_pairs={{0,16},{4,20},{8,24},{12,28},{16,0},{20,4},{24,8},{28,12},{1,17},{... | collective-permute-start | bytes 835592 | tf_op jit(solution)/shard_map/ppermute | solution.py:319
  55.9 13.0 %copy-start.2 = (f32[4,64,64]{2,1,0:T(8,128)S(1)}, f32[4,64,64]{2,1,0:T(8,128)}, u32[]{:S(2)}) copy-start(f32[4,64,64]{2,1,0:T(8,128)} %param.9) | copy-start | bytes 196612
  55.9 6.6 %collective-permute-start.13 = (s16[272,512]{1,0:T(8,128)(2,1)S(1)}, s16[272,512]{1,0:T(8,128)(2,1)S(1)}, u32[]{:S(2)}, u32[]{:S(2)}) collective-permute-start(s16[272,512]{1,0:T(8,128)(2,1)S(1)} %relay.7), channel_id=1, source_target_pairs={{0,8},{4,12},{8,0},{12,4},{16,24},{20,28},{24,16},{28,20},{1,9},{5... | collective-permute-start | bytes 835592 | tf_op jit(solution)/shard_map/ppermute | solution.py:319
  63.0 9.2 %collective-permute-start.14 = (s16[528,128]{1,0:T(8,128)(2,1)S(1)}, s16[528,128]{1,0:T(8,128)(2,1)S(1)}, u32[]{:S(2)}, u32[]{:S(2)}) collective-permute-start(s16[528,128]{1,0:T(8,128)(2,1)S(1)} %get-tuple-element.54), channel_id=1, source_target_pairs={{0,1},{1,0},{2,3},{3,2},{4,5},{5,4},{6,7},{7,6},{8,9},{9,8},{10,11... | collective-permute-start | bytes 405512 | tf_op jit(solution)/shard_map/ppermute | solution.py:427
  66.4 10.6 %collective-permute-start.15 = (s16[528,128]{1,0:T(8,128)(2,1)S(1)}, s16[528,128]{1,0:T(8,128)(2,1)S(1)}, u32[]{:S(2)}, u32[]{:S(2)}) collective-permute-start(s16[528,128]{1,0:T(8,128)(2,1)S(1)} %get-tuple-element.55), channel_id=1, source_target_pairs={{0,2},{1,3},{2,0},{3,1},{4,6},{5,7},{6,4},{7,5},{8,10},{9,11},{10,... | collective-permute-start | bytes 405512 | tf_op jit(solution)/shard_map/ppermute | solution.py:427
  66.4 10.6 %collective-permute-start.16 = (s16[528,128]{1,0:T(8,128)(2,1)S(1)}, s16[528,128]{1,0:T(8,128)(2,1)S(1)}, u32[]{:S(2)}, u32[]{:S(2)}) collective-permute-start(s16[528,128]{1,0:T(8,128)(2,1)S(1)} %get-tuple-element.56), channel_id=1, source_target_pairs={{0,3},{1,2},{2,1},{3,0},{4,7},{5,6},{6,5},{7,4},{8,11},{9,10},{10,... | collective-permute-start | bytes 405512 | tf_op jit(solution)/shard_map/ppermute | solution.py:427

commit v4 on v3

--- a/solution.py
+++ b/solution.py
@@ -252,6 +252,20 @@
 def cross_kernel(row_blocks, group, arrays, *rest):
     dsts = rest[2 * arrays :]
     for other, dst in enumerate(dsts):
+        for start in range(0, group, LANES):
+            parts = []
+            for piece in range(2):
+                keep, *came = rest[piece * arrays : (piece + 1) * arrays]
+                lanes = pl.ds((other + 1) * group + start, LANES)
+                parts += given(gathered(0, keep, came, lanes, row_blocks))
+            encode(dst, pl.ds(start, LANES), parts)
+
+
+def cross_all_kernel(row_blocks, group, arrays, me_ref, *rest):
+    out = rest[-1]
+    out[me_ref[2]] = jnp.zeros(out.shape[1:], jnp.int16)
+    for other in range(out.shape[0] - 1):
+        dst = out.at[me_ref[2] ^ (other + 1)]
         for start in range(0, group, LANES):
             parts = []
             for piece in range(2):
@@ -287,6 +301,22 @@
         for start in range(0, group, LANES):
             total = [0.0] * row_blocks
             for src in rest[:far]:
+                parts = decode(src, pl.ds(start, LANES), piece * row_blocks, row_blocks)
+                total = [left + right for left, right in zip(total, parts)]
+            lanes = pl.ds(piece * group + start, LANES)
+            for block in range(row_blocks):
+                lines = pl.ds(block * CB, CB)
+                out_ref[lines, lanes] = base_ref[lines, lanes] - total[block]
+
+
+def finish_all_kernel(row_blocks, me_ref, base_ref, all_ref, *rest):
+    far = [all_ref.at[me_ref[2] ^ (other + 1)] for other in range(all_ref.shape[0] - 1)]
+    out_ref = rest[-1]
+    group = out_ref.shape[1] // 2
+    for piece in range(2):
+        for start in range(0, group, LANES):
+            total = [0.0] * row_blocks
+            for src in far:
                 parts = decode(src, pl.ds(start, LANES), piece * row_blocks, row_blocks)
                 total = [left + right for left, right in zip(total, parts)]
             lanes = pl.ds(piece * group + start, LANES)
@@ -415,18 +445,31 @@
 
         near = [array for piece in range(2) for array in [keeps[turn][piece]] + came[turn][piece]]
         arrays = len(near) // 2
-        crossed = pl.pallas_call(
-            functools.partial(cross_kernel, row_blocks, group, arrays),
-            in_specs=[VMEM] * len(near),
-            out_specs=[VMEM] * (n_cam - 1),
-            out_shape=[jax.ShapeDtypeStruct((2 * extent + STRIP, group), jnp.int16)] * (n_cam - 1),
-            compiler_params=PARAMS,
-            name="cross",
-        )(*near)
-        far = [
-            lax.ppermute(value, "cam", [(i, i ^ (pos + 1)) for i in range(n_cam)])
-            for pos, value in enumerate(crossed)
-        ]
+        part = (2 * extent + STRIP, group)
+        last = turn == turns - 1
+        if last:
+            crossed = pl.pallas_call(
+                functools.partial(cross_all_kernel, row_blocks, group, arrays),
+                in_specs=[SMEM] + [VMEM] * len(near),
+                out_specs=VMEM,
+                out_shape=jax.ShapeDtypeStruct((n_cam, *part), jnp.int16),
+                compiler_params=PARAMS,
+                name="cross_all",
+            )(me, *near)
+            far = [lax.all_to_all(crossed, "cam", 0, 0, tiled=True)]
+        else:
+            crossed = pl.pallas_call(
+                functools.partial(cross_kernel, row_blocks, group, arrays),
+                in_specs=[VMEM] * len(near),
+                out_specs=[VMEM] * (n_cam - 1),
+                out_shape=[jax.ShapeDtypeStruct((2 * extent + STRIP, group), jnp.int16)] * (n_cam - 1),
+                compiler_params=PARAMS,
+                name="cross",
+            )(*near)
+            far = [
+                lax.ppermute(value, "cam", [(i, i ^ (pos + 1)) for i in range(n_cam)])
+                for pos, value in enumerate(crossed)
+            ]
         base = pl.pallas_call(
             functools.partial(base_kernel, (turn, row_blocks, col_blocks, arrays)),
             in_specs=[SMEM, VMEM] + [VMEM] * len(near),
@@ -437,15 +480,19 @@
         )(me, wide, *near)
         before = [] if result is None else [result]
         result = pl.pallas_call(
-            functools.partial(finish_kernel, row_blocks, n_cam - 1),
+            functools.partial(finish_all_kernel, row_blocks)
+            if last
+            else functools.partial(finish_kernel, row_blocks, n_cam - 1),
             grid=(1,),
-            in_specs=[VMEM] * n_cam + [pl.BlockSpec(memory_space=pl.ANY)] * len(before),
+            in_specs=[SMEM] * last
+            + [VMEM] * (1 + len(far))
+            + [pl.BlockSpec(memory_space=pl.ANY)] * len(before),
             out_specs=pl.BlockSpec((extent, 2 * group), lambda step, turn=turn: (0, turn)),
             out_shape=jax.ShapeDtypeStruct((extent, col_blocks * CB), jnp.float32),
-            input_output_aliases={n_cam: 0} if before else {},
+            input_output_aliases={1 + last + len(far): 0} if before else {},
             compiler_params=PARAMS,
             name="finish",
-        )(base, *far, *before)
+        )(*[me] * last, base, *far, *before)
     return result
 
 

time: 77.9 us -> 85.7 us (1.10)
  local copies, waits for them, and re-layouts: 2.12 us -> 6.74 us
  Pallas kernels: 24.3 us -> 28.6 us
  starting transfers between devices: 24.9 us -> 20.9 us
  waiting for transfers between devices: 25.1 us -> 27.7 us
    ppermute x6 -> x3, starting transfers between devices: 12.8 us -> 4.59 us  [body(): lax.ppermute(value, 'cam', [(i, i ^ pos + 1) for i in range(n_cam)])]
    all_to_all x0 -> x1, waiting for transfers between devices: none -> 7.84 us  [body(): far = [lax.all_to_all(crossed, 'cam', 0, 0, tiled=True)]]
    ppermute x6 -> x3, waiting for transfers between devices: 10.1 us -> 3.61 us  [body(): lax.ppermute(value, 'cam', [(i, i ^ pos + 1) for i in range(n_cam)])]
    unnamed x6 -> x56, local copies, waits for them, and re-layouts: 2.12 us -> 6.74 us
    all_to_all x0 -> x1, starting transfers between devices: none -> 4.3 us  [body(): far = [lax.all_to_all(crossed, 'cam', 0, 0, tiled=True)]]
    pallas_call x4, Pallas kernels: 16.8 us -> 19.4 us  [round_call(): pl.pallas_call(functools.partial(round_kernel, plan), in_specs=[SMEM] * 2...]
    pallas_call x2 -> x3, Pallas kernels: 1.64 us -> 3.7 us  [the longest x2 2.7 us: body(): pl.pallas_call(functools.partial(finish_all_kernel, row_blocks) if last e...]
    ppermute x11, waiting for transfers between devices: 15 us -> 16.2 us  [swap(): return lax.ppermute(value, 'lm', [(i, i ^ 1 << bit) for i in range(n_lm)])]
  transfers between devices with their start and end apart: 17 -> 15, of which waited for: 8 -> 7; matrix products, arithmetic and copies ran while one was open for 2% -> 1% of each run, Pallas kernels for 17% -> 18%
where the time goes in v4:
time: 85.7 us; the launch traced here: 85.4 us
  Pallas kernels  28.6 us (33%)
  waiting for transfers between devices  27.7 us (32%)
  starting transfers between devices  20.9 us (24%)
  local copies, waits for them, and re-layouts  6.74 us (8%)
  other arithmetic  1.18 us (1%)
    pallas_call x4, Pallas kernels, round_call(): pl.pallas_call(functools.partial(round_kernel, plan), in_specs=[SMEM] * 2...  19.4 us
    ppermute x11, waiting for transfers between devices, swap(): return lax.ppermute(value, 'lm', [(i, i ^ 1 << bit) for i in range(n_lm)])  16.2 us
    ppermute x11, starting transfers between devices, swap(): return lax.ppermute(value, 'lm', [(i, i ^ 1 << bit) for i in range(n_lm)])  12 us
    all_to_all x1, waiting for transfers between devices, body(): far = [lax.all_to_all(crossed, 'cam', 0, 0, tiled=True)]  7.84 us
    unnamed x56, local copies, waits for them, and re-layouts  6.74 us
    ppermute x3, starting transfers between devices, body(): lax.ppermute(value, 'cam', [(i, i ^ pos + 1) for i in range(n_cam)])  4.59 us
    all_to_all x1, starting transfers between devices, body(): far = [lax.all_to_all(crossed, 'cam', 0, 0, tiled=True)]  4.3 us
    ppermute x3, waiting for transfers between devices, body(): lax.ppermute(value, 'cam', [(i, i ^ pos + 1) for i in range(n_cam)])  3.61 us
  transfers between devices with their start and end apart: 15, of which 7 were waited for; matrix products, arithmetic and copies ran while one was open for 1% of the time, Pallas kernels for 18%

profile of v4, /device:TPU:0, one launch (start us, length us, event | category | flops | bytes accessed | tf_op | source)
XLA Modules:
  0.0 85.4 jit_solution(15056656074228914)
XLA Ops:
  0.0 0.5 collective-permute-start.1
  0.5 0.8 fusion.3
  1.2 0.1 collective-permute-start
  1.3 0.5 collective-permute-start.2
  1.8 0.1 select_reduce_fusion.1.table.table_a
  1.9 0.0 copy-start.13
  1.9 1.4 %copy-done.13 = bf16[2,16,64,384]{3,2,1,0:T(8,128)(2,1)S(1)} copy-done((bf16[2,16,64,384]{3,2,1,0:T(8,128)(2,1)S(1)}, bf16[2,16,64,384]{3,2,1,0:T(8,128)(2,1)}, u32[]{:S(2)}) %copy-start.13) | copy-done | bytes 1572888
  3.3 0.7 copy-done.26
  4.0 1.4 %form_own.1 = (bf16[2,1024,768]{2,1,0:T(8,128)(2,1)S(1)}, bf16[2,16,64,384]{3,2,1,0:T(8,128)(2,1)S(1)}) custom-call(s32[2,48]{1,0:T(2,128)S(1)} %select_reduce_fusion.1.table.table_a, bf16[2,16,64,384]{3,2,1,0:T(8,128)(2,1)S(1)} %copy-done.13, f32[3,3,256]{2,1,0:T(4,128)S(1)} %copy-done.26), custom_call_target="tpu_custom_call" | custom-call | tf_op jit(solution)/shard_map/form_own/pallas_call | solution.py:370
  5.5 0.0 collective-permute-done
  5.5 0.1 select_reduce_fusion.table.table_b
  5.6 0.0 collective-permute-done.2.cur
  5.6 0.0 collective-permute-done.1.pan.pan_b
  5.6 1.3 %form_other.1.rows_b = bf16[2,1024,768]{2,1,0:T(8,128)(2,1)S(1)} custom-call(s32[2,48]{1,0:T(2,128)S(1)} %select_reduce_fusion.table.table_b, bf16[2,16,64,384]{3,2,1,0:T(8,128)(2,1)S(1)} %collective-permute-done.1.pan.pan_b, f32[3,3,256]{2,1,0:T(4,128)S(1)} %collective-permute-done.2.cur), custom_call_target="tpu_custom_call" | custom-call | tf_op jit(solution)/shard_map/form_other/pallas_call | solution.py:383
  7.0 4.3 %send.2 = (s16[528,512]{1,0:T(8,128)(2,1)S(1)}, s16[528,512]{1,0:T(8,128)(2,1)S(1)}) custom-call(s32[2,48]{1,0:T(2,128)S(1)} %select_reduce_fusion.1.table.table_a, s32[2,48]{1,0:T(2,128)S(1)} %select_reduce_fusion.table.table_b, bf16[2,16,64,384]{3,2,1,0:T(8,128)(2,1)S(1)} %get-tuple-element.28.pan_a, ...), custom_call_target="tpu_custom_call" | custom-call | tf_op jit(solution)/shard_map/send/pallas_call | solution.py:400
  11.3 3.6 %collective-permute-start.5 = (s16[528,512]{1,0:T(8,128)(2,1)S(1)}, s16[528,512]{1,0:T(8,128)(2,1)S(1)}, u32[]{:S(2)}, u32[]{:S(2)}) collective-permute-start(s16[528,512]{1,0:T(8,128)(2,1)S(1)} %get-tuple-element.31), channel_id=1, source_target_pairs={{0,16},{4,20},{8,24},{12,28},{16,0},{20,4},{24,8},{28,12},{1,17},{... | collective-permute-start | bytes 1622024 | tf_op jit(solution)/shard_map/ppermute | solution.py:349
  14.9 0.4 collective-permute-start.3
  15.3 5.4 %keep.2 = (f32[2,256,512]{2,1,0:T(8,128)S(1)}, f32[2,256,512]{2,1,0:T(8,128)S(1)}) custom-call(s32[2,48]{1,0:T(2,128)S(1)} %select_reduce_fusion.1.table.table_a, s32[2,48]{1,0:T(2,128)S(1)} %select_reduce_fusion.table.table_b, bf16[2,16,64,384]{3,2,1,0:T(8,128)(2,1)S(1)} %get-tuple-element.28.pan_a, ...), custom_call_target="tpu_custom_call" | custom-call | tf_op jit(solution)/shard_map/keep/pallas_call | solution.py:400
  20.7 7.2 %collective-permute-done.5.rest_0_.rest_4_ = s16[528,512]{1,0:T(8,128)(2,1)S(1)} collective-permute-done((s16[528,512]{1,0:T(8,128)(2,1)S(1)}, s16[528,512]{1,0:T(8,128)(2,1)S(1)}, u32[]{:S(2)}, u32[]{:S(2)}) %collective-permute-start.5) | collective-permute-done | bytes 540704 | tf_op jit(solution)/shard_map/ppermute | solution.py:349
  27.9 0.2 relay.5
  28.1 1.8 %collective-permute-start.6 = (s16[272,512]{1,0:T(8,128)(2,1)S(1)}, s16[272,512]{1,0:T(8,128)(2,1)S(1)}, u32[]{:S(2)}, u32[]{:S(2)}) collective-permute-start(s16[272,512]{1,0:T(8,128)(2,1)S(1)} %relay.5), channel_id=1, source_target_pairs={{0,8},{4,12},{8,0},{12,4},{16,24},{20,28},{24,16},{28,20},{1,9},{5... | collective-permute-start | bytes 835592 | tf_op jit(solution)/shard_map/ppermute | solution.py:349
  29.9 0.0 collective-permute-done.3.rest_0_.rest_1_
  29.9 0.2 relay.4
  30.2 0.4 collective-permute-start.4
  30.5 4.3 %send.3 = (s16[528,512]{1,0:T(8,128)(2,1)S(1)}, s16[528,512]{1,0:T(8,128)(2,1)S(1)}) custom-call(s32[2,48]{1,0:T(2,128)S(1)} %select_reduce_fusion.1.table.table_a, s32[2,48]{1,0:T(2,128)S(1)} %select_reduce_fusion.table.table_b, bf16[2,16,64,384]{3,2,1,0:T(8,128)(2,1)S(1)} %get-tuple-element.28.pan_a, ...), custom_call_target="tpu_custom_call" | custom-call | tf_op jit(solution)/shard_map/send/pallas_call | solution.py:400
  34.8 1.8 %collective-permute-done.6.rest_5_ = s16[272,512]{1,0:T(8,128)(2,1)S(1)} collective-permute-done((s16[272,512]{1,0:T(8,128)(2,1)S(1)}, s16[272,512]{1,0:T(8,128)(2,1)S(1)}, u32[]{:S(2)}, u32[]{:S(2)}) %collective-permute-start.6) | collective-permute-done | bytes 278560 | tf_op jit(solution)/shard_map/ppermute | solution.py:349
  36.7 1.2 %collective-permute-done.4.rest_2_ = s16[272,512]{1,0:T(8,128)(2,1)S(1)} collective-permute-done((s16[272,512]{1,0:T(8,128)(2,1)S(1)}, s16[272,512]{1,0:T(8,128)(2,1)S(1)}, u32[]{:S(2)}, u32[]{:S(2)}) %collective-permute-start.4) | collective-permute-done | bytes 278560 | tf_op jit(solution)/shard_map/ppermute | solution.py:349
  37.9 0.5 cross.1
  38.3 0.2 copy-done.14
  38.6 0.9 %collective-permute-start.7 = (s16[528,512]{1,0:T(8,128)(2,1)S(1)}, s16[528,512]{1,0:T(8,128)(2,1)S(1)}, u32[]{:S(2)}, u32[]{:S(2)}) collective-permute-start(s16[528,512]{1,0:T(8,128)(2,1)S(1)} %get-tuple-element.46), channel_id=1, source_target_pairs={{0,8},{4,12},{8,0},{12,4},{16,24},{20,28},{24,16},{28,20},{1,9},{5... | collective-permute-start | bytes 1622024 | tf_op jit(solution)/shard_map/ppermute | solution.py:349
  39.5 1.5 %collective-permute-start.12 = (s16[528,512]{1,0:T(8,128)(2,1)S(1)}, s16[528,512]{1,0:T(8,128)(2,1)S(1)}, u32[]{:S(2)}, u32[]{:S(2)}) collective-permute-start(s16[528,512]{1,0:T(8,128)(2,1)S(1)} %get-tuple-element.49), channel_id=1, source_target_pairs={{0,16},{4,20},{8,24},{12,28},{16,0},{20,4},{24,8},{28,12},{1,17},{... | collective-permute-start | bytes 1622024 | tf_op jit(solution)/shard_map/ppermute | solution.py:349
  41.0 2.2 %collective-permute-start.8 = (s16[528,128]{1,0:T(8,128)(2,1)S(1)}, s16[528,128]{1,0:T(8,128)(2,1)S(1)}, u32[]{:S(2)}, u32[]{:S(2)}) collective-permute-start(s16[528,128]{1,0:T(8,128)(2,1)S(1)} %get-tuple-element.43), channel_id=1, source_target_pairs={{0,1},{1,0},{2,3},{3,2},{4,5},{5,4},{6,7},{7,6},{8,9},{9,8},{10,11... | collective-permute-start | bytes 405512 | tf_op jit(solution)/shard_map/ppermute | solution.py:470
  43.2 0.2 collective-permute-start.9
  43.4 2.2 %collective-permute-start.10 = (s16[528,128]{1,0:T(8,128)(2,1)S(1)}, s16[528,128]{1,0:T(8,128)(2,1)S(1)}, u32[]{:S(2)}, u32[]{:S(2)}) collective-permute-start(s16[528,128]{1,0:T(8,128)(2,1)S(1)} %get-tuple-element.45), channel_id=1, source_target_pairs={{0,3},{1,2},{2,1},{3,0},{4,7},{5,6},{6,5},{7,4},{8,11},{9,10},{10,... | collective-permute-start | bytes 405512 | tf_op jit(solution)/shard_map/ppermute | solution.py:470
  45.6 5.4 %keep.3 = (f32[2,256,512]{2,1,0:T(8,128)S(1)}, f32[2,256,512]{2,1,0:T(8,128)S(1)}) custom-call(s32[2,48]{1,0:T(2,128)S(1)} %select_reduce_fusion.1.table.table_a, s32[2,48]{1,0:T(2,128)S(1)} %select_reduce_fusion.table.table_b, bf16[2,16,64,384]{3,2,1,0:T(8,128)(2,1)S(1)} %get-tuple-element.28.pan_a, ...), custom_call_target="tpu_custom_call" | custom-call | tf_op jit(solution)/shard_map/keep/pallas_call | solution.py:400
  51.0 0.0 collective-permute-done.8.rest_0_
  51.1 3.6 %collective-permute-done.9.rest_1_ = s16[528,128]{1,0:T(8,128)(2,1)S(1)} collective-permute-done((s16[528,128]{1,0:T(8,128)(2,1)S(1)}, s16[528,128]{1,0:T(8,128)(2,1)S(1)}, u32[]{:S(2)}, u32[]{:S(2)}) %collective-permute-start.9) | collective-permute-done | bytes 135200 | tf_op jit(solution)/shard_map/ppermute | solution.py:470
  54.7 0.0 collective-permute-done.10.rest_2_
  54.7 0.0 collective-permute-done.7.rest_0_.rest_1_
  54.7 0.2 relay.6
  55.0 1.9 %collective-permute-start.11 = (s16[272,512]{1,0:T(8,128)(2,1)S(1)}, s16[272,512]{1,0:T(8,128)(2,1)S(1)}, u32[]{:S(2)}, u32[]{:S(2)}) collective-permute-start(s16[272,512]{1,0:T(8,128)(2,1)S(1)} %relay.6), channel_id=1, source_target_pairs={{0,16},{4,20},{8,24},{12,28},{16,0},{20,4},{24,8},{28,12},{1,17},{... | collective-permute-start | bytes 835592 | tf_op jit(solution)/shard_map/ppermute | solution.py:349
  56.8 0.0 collective-permute-done.12.rest_0_.rest_4_
  56.8 0.2 relay.7
  57.1 0.5 collective-permute-start.13
  57.6 0.1 pad_add_fusion.me_ref
  57.7 3.9 %collective-permute-done.11.rest_2_ = s16[272,512]{1,0:T(8,128)(2,1)S(1)} collective-permute-done((s16[272,512]{1,0:T(8,128)(2,1)S(1)}, s16[272,512]{1,0:T(8,128)(2,1)S(1)}, u32[]{:S(2)}, u32[]{:S(2)}) %collective-permute-start.11) | collective-permute-done | bytes 278560 | tf_op jit(solution)/shard_map/ppermute | solution.py:349
  61.6 2.1 %collective-permute-done.13.rest_5_ = s16[272,512]{1,0:T(8,128)(2,1)S(1)} collective-permute-done((s16[272,512]{1,0:T(8,128)(2,1)S(1)}, s16[272,512]{1,0:T(8,128)(2,1)S(1)}, u32[]{:S(2)}, u32[]{:S(2)}) %collective-permute-start.13) | collective-permute-done | bytes 278560 | tf_op jit(solution)/shard_map/ppermute | solution.py:349
  63.7 1.0 %cross_all.1 = s16[4,528,128]{2,1,0:T(8,128)(2,1)S(1)} custom-call(s32[3]{0:T(128)S(1)} %pad_add_fusion.me_ref, f32[2,256,512]{2,1,0:T(8,128)S(1)} %get-tuple-element.47.keep.rest_0_, s16[528,512]{1,0:T(8,128)(2,1)S(1)} %collective-permute-done.7.rest_0_.rest_1_, s16[272,512]{1,0:T(8,128)(2,1)S(1)} %collective-permute-done.11.rest_2_, ...), custom_call_target="tpu_custom_call" | custom-call | tf_op jit(solution)/shard_map/cross_all/pallas_call | solution.py:451
  64.8 0.8 copy-done.12
  65.6 0.7 copy-done.16
  66.3 0.7 copy-done.18
  67.0 4.3 %all-to-all-start = ((s16[4,528,128]{2,1,0:T(8,128)(2,1)}), s16[4,528,128]{2,1,0:T(8,128)(2,1)}, u32[]{:S(2)}, u32[]{:S(2)}) async-start(s16[4,528,128]{2,1,0:T(8,128)(2,1)} %copy-done.12), calls=%async_computation | async-start | bytes 1081344 | tf_op jit(solution)/shard_map/all_to_all | solution.py:459
  71.3 0.1 pad_maximum_fusion.wide_ref
  71.5 1.0 %copy-done.7 = s16[528,512]{1,0:T(8,128)(2,1)S(1)} copy-done((s16[528,512]{1,0:T(8,128)(2,1)S(1)}, s16[528,512]{1,0:T(8,128)(2,1)}, u32[]{:S(2)}) %copy-start.7) | copy-done | bytes 540696
  72.6 0.6 base.3.base_ref
  73.2 0.2 copy-done.21
  73.4 0.1 copy-done.23
  73.5 0.1 copy-done.25
  73.5 0.8 finish.2.rest_0_
  74.4 0.0 copy-done.19
  74.4 0.7 copy-done.3
  75.1 0.6 base.2.base_ref
  75.7 7.8 %all-to-all-done.all_ref = s16[4,528,128]{2,1,0:T(8,128)(2,1)} async-done(((s16[4,528,128]{2,1,0:T(8,128)(2,1)}), s16[4,528,128]{2,1,0:T(8,128)(2,1)}, u32[]{:S(2)}, u32[]{:S(2)}) %all-to-all-start) | async-done | bytes 540704 | tf_op jit(solution)/shard_map/all_to_all | solution.py:459
  83.6 1.9 %finish.3 = f32[256,512]{1,0:T(8,128)} custom-call(s32[3]{0:T(128)S(1)} %pad_add_fusion.me_ref, f32[256,256]{1,0:T(8,128)S(1)} %base.2.base_ref, s16[4,528,128]{2,1,0:T(8,128)(2,1)} %all-to-all-done.all_ref, f32[256,512]{1,0:T(8,128)} %finish.2.rest_0_), custom_call_target="tpu_custom_call", output_to_operand_aliasing={{}: (3, {})} | custom-call | tf_op jit(solution)/shard_map/finish/pallas_call | solution.py:482
  (45 shorter events, 0.1 us)
Async XLA Ops:
  0.0 5.6 %collective-permute-start.1 = (bf16[2,16,64,384]{3,2,1,0:T(8,128)(2,1)}, bf16[2,16,64,384]{3,2,1,0:T(8,128)(2,1)S(1)}, u32[]{:S(2)}, u32[]{:S(2)}) collective-permute-start(bf16[2,16,64,384]{3,2,1,0:T(8,128)(2,1)} %pan_ref.1), channel_id=1, source_target_pairs={{0,4},{4,0},{8,12},{12,8},{16,20},{20,16},{24,28},{28,24},{1,5},{5... | collective-permute-start | bytes 4718600 | tf_op jit(solution)/shard_map/ppermute | solution.py:349
  1.2 4.3 %collective-permute-start = (s32[2,16]{1,0:T(2,128)S(1)}, s32[2,16]{1,0:T(2,128)S(1)}, u32[]{:S(2)}, u32[]{:S(2)}) collective-permute-start(s32[2,16]{1,0:T(2,128)S(1)} %get-tuple-element.52), channel_id=1, source_target_pairs={{0,4},{4,0},{8,12},{12,8},{16,20},{20,16},{24,28},{28,24},{1,5},{5... | collective-permute-start | bytes 392 | tf_op jit(solution)/shard_map/ppermute | solution.py:349
  1.3 4.3 %collective-permute-start.2 = (f32[3,3,256]{2,1,0:T(4,128)}, f32[3,3,256]{2,1,0:T(4,128)S(1)}, u32[]{:S(2)}, u32[]{:S(2)}) collective-permute-start(f32[3,3,256]{2,1,0:T(4,128)} %cur_ref.1), channel_id=1, source_target_pairs={{0,4},{4,0},{8,12},{12,8},{16,20},{20,16},{24,28},{28,24},{1,5},{5... | collective-permute-start | bytes 27656 | tf_op jit(solution)/shard_map/ppermute | solution.py:349
  1.9 1.4 %copy-start.13 = (bf16[2,16,64,384]{3,2,1,0:T(8,128)(2,1)S(1)}, bf16[2,16,64,384]{3,2,1,0:T(8,128)(2,1)}, u32[]{:S(2)}) copy-start(bf16[2,16,64,384]{3,2,1,0:T(8,128)(2,1)} %pan_ref.1) | copy-start | bytes 4718596
  3.3 0.7 copy-start.26
  11.3 16.6 %collective-permute-start.5 = (s16[528,512]{1,0:T(8,128)(2,1)S(1)}, s16[528,512]{1,0:T(8,128)(2,1)S(1)}, u32[]{:S(2)}, u32[]{:S(2)}) collective-permute-start(s16[528,512]{1,0:T(8,128)(2,1)S(1)} %get-tuple-element.31), channel_id=1, source_target_pairs={{0,16},{4,20},{8,24},{12,28},{16,0},{20,4},{24,8},{28,12},{1,17},{... | collective-permute-start | bytes 1622024 | tf_op jit(solution)/shard_map/ppermute | solution.py:349
  14.9 15.0 %collective-permute-start.3 = (s16[528,512]{1,0:T(8,128)(2,1)S(1)}, s16[528,512]{1,0:T(8,128)(2,1)S(1)}, u32[]{:S(2)}, u32[]{:S(2)}) collective-permute-start(s16[528,512]{1,0:T(8,128)(2,1)S(1)} %get-tuple-element.30), channel_id=1, source_target_pairs={{0,8},{4,12},{8,0},{12,4},{16,24},{20,28},{24,16},{28,20},{1,9},{5... | collective-permute-start | bytes 1622024 | tf_op jit(solution)/shard_map/ppermute | solution.py:349
  20.7 17.2 %copy-start = (f32[2,256,512]{2,1,0:T(8,128)}, f32[2,256,512]{2,1,0:T(8,128)S(1)}, u32[]{:S(2)}) copy-start(f32[2,256,512]{2,1,0:T(8,128)S(1)} %get-tuple-element.35.keep.rest_3_) | copy-start | bytes 3145732
  28.1 8.6 %collective-permute-start.6 = (s16[272,512]{1,0:T(8,128)(2,1)S(1)}, s16[272,512]{1,0:T(8,128)(2,1)S(1)}, u32[]{:S(2)}, u32[]{:S(2)}) collective-permute-start(s16[272,512]{1,0:T(8,128)(2,1)S(1)} %relay.5), channel_id=1, source_target_pairs={{0,8},{4,12},{8,0},{12,4},{16,24},{20,28},{24,16},{28,20},{1,9},{5... | collective-permute-start | bytes 835592 | tf_op jit(solution)/shard_map/ppermute | solution.py:349
  29.9 8.0 %copy-start.6 = (s16[528,512]{1,0:T(8,128)(2,1)}, s16[528,512]{1,0:T(8,128)(2,1)S(1)}, u32[]{:S(2)}) copy-start(s16[528,512]{1,0:T(8,128)(2,1)S(1)} %collective-permute-done.3.rest_0_.rest_1_) | copy-start | bytes 1622020
  30.2 7.7 %collective-permute-start.4 = (s16[272,512]{1,0:T(8,128)(2,1)S(1)}, s16[272,512]{1,0:T(8,128)(2,1)S(1)}, u32[]{:S(2)}, u32[]{:S(2)}) collective-permute-start(s16[272,512]{1,0:T(8,128)(2,1)S(1)} %relay.4), channel_id=1, source_target_pairs={{0,16},{4,20},{8,24},{12,28},{16,0},{20,4},{24,8},{28,12},{1,17},{... | collective-permute-start | bytes 835592 | tf_op jit(solution)/shard_map/ppermute | solution.py:349
  37.9 0.7 copy-start.14
  38.6 16.1 %collective-permute-start.7 = (s16[528,512]{1,0:T(8,128)(2,1)S(1)}, s16[528,512]{1,0:T(8,128)(2,1)S(1)}, u32[]{:S(2)}, u32[]{:S(2)}) collective-permute-start(s16[528,512]{1,0:T(8,128)(2,1)S(1)} %get-tuple-element.46), channel_id=1, source_target_pairs={{0,8},{4,12},{8,0},{12,4},{16,24},{20,28},{24,16},{28,20},{1,9},{5... | collective-permute-start | bytes 1622024 | tf_op jit(solution)/shard_map/ppermute | solution.py:349
  39.5 17.3 %collective-permute-start.12 = (s16[528,512]{1,0:T(8,128)(2,1)S(1)}, s16[528,512]{1,0:T(8,128)(2,1)S(1)}, u32[]{:S(2)}, u32[]{:S(2)}) collective-permute-start(s16[528,512]{1,0:T(8,128)(2,1)S(1)} %get-tuple-element.49), channel_id=1, source_target_pairs={{0,16},{4,20},{8,24},{12,28},{16,0},{20,4},{24,8},{28,12},{1,17},{... | collective-permute-start | bytes 1622024 | tf_op jit(solution)/shard_map/ppermute | solution.py:349
  41.0 10.0 %collective-permute-start.8 = (s16[528,128]{1,0:T(8,128)(2,1)S(1)}, s16[528,128]{1,0:T(8,128)(2,1)S(1)}, u32[]{:S(2)}, u32[]{:S(2)}) collective-permute-start(s16[528,128]{1,0:T(8,128)(2,1)S(1)} %get-tuple-element.43), channel_id=1, source_target_pairs={{0,1},{1,0},{2,3},{3,2},{4,5},{5,4},{6,7},{7,6},{8,9},{9,8},{10,11... | collective-permute-start | bytes 405512 | tf_op jit(solution)/shard_map/ppermute | solution.py:470
  43.2 11.4 %collective-permute-start.9 = (s16[528,128]{1,0:T(8,128)(2,1)S(1)}, s16[528,128]{1,0:T(8,128)(2,1)S(1)}, u32[]{:S(2)}, u32[]{:S(2)}) collective-permute-start(s16[528,128]{1,0:T(8,128)(2,1)S(1)} %get-tuple-element.44), channel_id=1, source_target_pairs={{0,2},{1,3},{2,0},{3,1},{4,6},{5,7},{6,4},{7,5},{8,10},{9,11},{10,... | collective-permute-start | bytes 405512 | tf_op jit(solution)/shard_map/ppermute | solution.py:470
  43.4 11.2 %collective-permute-start.10 = (s16[528,128]{1,0:T(8,128)(2,1)S(1)}, s16[528,128]{1,0:T(8,128)(2,1)S(1)}, u32[]{:S(2)}, u32[]{:S(2)}) collective-permute-start(s16[528,128]{1,0:T(8,128)(2,1)S(1)} %get-tuple-element.45), channel_id=1, source_target_pairs={{0,3},{1,2},{2,1},{3,0},{4,7},{5,6},{6,5},{7,4},{8,11},{9,10},{10,... | collective-permute-start | bytes 405512 | tf_op jit(solution)/shard_map/ppermute | solution.py:470
  51.0 12.7 %copy-start.2 = (f32[2,256,512]{2,1,0:T(8,128)}, f32[2,256,512]{2,1,0:T(8,128)S(1)}, u32[]{:S(2)}) copy-start(f32[2,256,512]{2,1,0:T(8,128)S(1)} %get-tuple-element.47.keep.rest_0_) | copy-start | bytes 3145732
  51.0 12.7 %copy-start.4 = (f32[2,256,512]{2,1,0:T(8,128)}, f32[2,256,512]{2,1,0:T(8,128)S(1)}, u32[]{:S(2)}) copy-start(f32[2,256,512]{2,1,0:T(8,128)S(1)} %get-tuple-element.50.keep.rest_3_) | copy-start | bytes 3145732
  51.1 6.0 %copy-start.20 = (s16[528,128]{1,0:T(8,128)(2,1)}, s16[528,128]{1,0:T(8,128)(2,1)S(1)}, u32[]{:S(2)}) copy-start(s16[528,128]{1,0:T(8,128)(2,1)S(1)} %collective-permute-done.8.rest_0_) | copy-start | bytes 405508
  54.7 2.4 %copy-start.22 = (s16[528,128]{1,0:T(8,128)(2,1)}, s16[528,128]{1,0:T(8,128)(2,1)S(1)}, u32[]{:S(2)}) copy-start(s16[528,128]{1,0:T(8,128)(2,1)S(1)} %collective-permute-done.9.rest_1_) | copy-start | bytes 405508
  54.7 2.4 %copy-start.24 = (s16[528,128]{1,0:T(8,128)(2,1)}, s16[528,128]{1,0:T(8,128)(2,1)S(1)}, u32[]{:S(2)}) copy-start(s16[528,128]{1,0:T(8,128)(2,1)S(1)} %collective-permute-done.10.rest_2_) | copy-start | bytes 405508
  54.7 9.0 %copy-start.8 = (s16[528,512]{1,0:T(8,128)(2,1)}, s16[528,512]{1,0:T(8,128)(2,1)S(1)}, u32[]{:S(2)}) copy-start(s16[528,512]{1,0:T(8,128)(2,1)S(1)} %collective-permute-done.7.rest_0_.rest_1_) | copy-start | bytes 1622020
  55.0 6.6 %collective-permute-start.11 = (s16[272,512]{1,0:T(8,128)(2,1)S(1)}, s16[272,512]{1,0:T(8,128)(2,1)S(1)}, u32[]{:S(2)}, u32[]{:S(2)}) collective-permute-start(s16[272,512]{1,0:T(8,128)(2,1)S(1)} %relay.6), channel_id=1, source_target_pairs={{0,16},{4,20},{8,24},{12,28},{16,0},{20,4},{24,8},{28,12},{1,17},{... | collective-permute-start | bytes 835592 | tf_op jit(solution)/shard_map/ppermute | solution.py:349
  56.8 6.9 %copy-start.10 = (s16[528,512]{1,0:T(8,128)(2,1)}, s16[528,512]{1,0:T(8,128)(2,1)S(1)}, u32[]{:S(2)}) copy-start(s16[528,512]{1,0:T(8,128)(2,1)S(1)} %collective-permute-done.12.rest_0_.rest_4_) | copy-start | bytes 1622020
  57.1 6.6 %collective-permute-start.13 = (s16[272,512]{1,0:T(8,128)(2,1)S(1)}, s16[272,512]{1,0:T(8,128)(2,1)S(1)}, u32[]{:S(2)}, u32[]{:S(2)}) collective-permute-start(s16[272,512]{1,0:T(8,128)(2,1)S(1)} %relay.7), channel_id=1, source_target_pairs={{0,8},{4,12},{8,0},{12,4},{16,24},{20,28},{24,16},{28,20},{1,9},{5... | collective-permute-start | bytes 835592 | tf_op jit(solution)/shard_map/ppermute | solution.py:349
  57.7 13.6 %copy-start.27 = (f32[4,64,64]{2,1,0:T(8,128)S(1)}, f32[4,64,64]{2,1,0:T(8,128)}, u32[]{:S(2)}) copy-start(f32[4,64,64]{2,1,0:T(8,128)} %param.9) | copy-start | bytes 196612
  57.7 13.7 %copy-start.15 = (s16[272,512]{1,0:T(8,128)(2,1)S(1)}, s16[272,512]{1,0:T(8,128)(2,1)}, u32[]{:S(2)}) copy-start(s16[272,512]{1,0:T(8,128)(2,1)} %copy-done.14) | copy-start | bytes 835588
  64.8 0.8 copy-start.12
  65.6 0.7 copy-start.16
  66.3 0.7 copy-start.18
  67.0 4.4 %copy-start.1 = (f32[2,256,512]{2,1,0:T(8,128)S(1)}, f32[2,256,512]{2,1,0:T(8,128)}, u32[]{:S(2)}) copy-start(f32[2,256,512]{2,1,0:T(8,128)} %copy-done) | copy-start | bytes 3145732
  67.0 16.5 %all-to-all-start = ((s16[4,528,128]{2,1,0:T(8,128)(2,1)}), s16[4,528,128]{2,1,0:T(8,128)(2,1)}, u32[]{:S(2)}, u32[]{:S(2)}) async-start(s16[4,528,128]{2,1,0:T(8,128)(2,1)} %copy-done.12), calls=%async_computation | async-start | bytes 1081344 | tf_op jit(solution)/shard_map/all_to_all | solution.py:459
  71.5 1.0 %copy-start.7 = (s16[528,512]{1,0:T(8,128)(2,1)S(1)}, s16[528,512]{1,0:T(8,128)(2,1)}, u32[]{:S(2)}) copy-start(s16[528,512]{1,0:T(8,128)(2,1)} %copy-done.6) | copy-start | bytes 1622020
  72.5 0.9 %copy-start.21 = (s16[528,128]{1,0:T(8,128)(2,1)S(1)}, s16[528,128]{1,0:T(8,128)(2,1)}, u32[]{:S(2)}) copy-start(s16[528,128]{1,0:T(8,128)(2,1)} %copy-done.20) | copy-start | bytes 405508
  72.5 1.0 %copy-start.23 = (s16[528,128]{1,0:T(8,128)(2,1)S(1)}, s16[528,128]{1,0:T(8,128)(2,1)}, u32[]{:S(2)}) copy-start(s16[528,128]{1,0:T(8,128)(2,1)} %copy-done.22) | copy-start | bytes 405508
  72.5 1.0 %copy-start.25 = (s16[528,128]{1,0:T(8,128)(2,1)S(1)}, s16[528,128]{1,0:T(8,128)(2,1)}, u32[]{:S(2)}) copy-start(s16[528,128]{1,0:T(8,128)(2,1)} %copy-done.24) | copy-start | bytes 405508
  72.5 1.9 %copy-start.5 = (f32[2,256,512]{2,1,0:T(8,128)S(1)}, f32[2,256,512]{2,1,0:T(8,128)}, u32[]{:S(2)}) copy-start(f32[2,256,512]{2,1,0:T(8,128)} %copy-done.4) | copy-start | bytes 3145732
  72.5 1.9 %copy-start.9 = (s16[528,512]{1,0:T(8,128)(2,1)S(1)}, s16[528,512]{1,0:T(8,128)(2,1)}, u32[]{:S(2)}) copy-start(s16[528,512]{1,0:T(8,128)(2,1)} %copy-done.8) | copy-start | bytes 1622020
  72.5 1.8 %copy-start.11 = (s16[528,512]{1,0:T(8,128)(2,1)S(1)}, s16[528,512]{1,0:T(8,128)(2,1)}, u32[]{:S(2)}) copy-start(s16[528,512]{1,0:T(8,128)(2,1)} %copy-done.10) | copy-start | bytes 1622020
  72.5 1.8 %copy-start.17 = (s16[272,512]{1,0:T(8,128)(2,1)S(1)}, s16[272,512]{1,0:T(8,128)(2,1)}, u32[]{:S(2)}) copy-start(s16[272,512]{1,0:T(8,128)(2,1)} %copy-done.16) | copy-start | bytes 835588
  72.6 1.8 %copy-start.19 = (s16[272,512]{1,0:T(8,128)(2,1)S(1)}, s16[272,512]{1,0:T(8,128)(2,1)}, u32[]{:S(2)}) copy-start(s16[272,512]{1,0:T(8,128)(2,1)} %copy-done.18) | copy-start | bytes 835588
  73.5 1.5 %copy-start.3 = (f32[2,256,512]{2,1,0:T(8,128)S(1)}, f32[2,256,512]{2,1,0:T(8,128)}, u32[]{:S(2)}) copy-start(f32[2,256,512]{2,1,0:T(8,128)} %copy-done.2) | copy-start | bytes 3145732

commit v5 on v3

--- a/solution.py
+++ b/solution.py
@@ -424,8 +424,8 @@
             name="cross",
         )(*near)
         far = [
-            lax.ppermute(value, "cam", [(i, i ^ (pos + 1)) for i in range(n_cam)])
-            for pos, value in enumerate(crossed)
+            lax.ppermute(crossed[pos], "cam", [(i, i ^ (pos + 1)) for i in range(n_cam)])
+            for pos in reversed(range(n_cam - 1))
         ]
         base = pl.pallas_call(
             functools.partial(base_kernel, (turn, row_blocks, col_blocks, arrays)),

time: 77.9 us -> 77.5 us (level)
  starting transfers between devices: 24.9 us -> 23.7 us
  waiting for transfers between devices: 25.1 us -> 26.3 us
    ppermute x6, starting transfers between devices: 12.8 us -> 10.9 us  [body(): lax.ppermute(crossed[pos], 'cam', [(i, i ^ pos + 1) for i in range(n_cam)])]
    ppermute x11, waiting for transfers between devices: 15 us -> 16 us  [swap(): return lax.ppermute(value, 'lm', [(i, i ^ 1 << bit) for i in range(n_lm)])]
  transfers between devices with their start and end apart: 17 -> 17, of which waited for: 8 -> 8; matrix products, arithmetic and copies ran while one was open for 2% -> 2% of each run, Pallas kernels for 17% -> 18%
where the time goes in v5:
time: 77.5 us; the launch traced here: 77.7 us
  waiting for transfers between devices  26.3 us (34%)
  Pallas kernels  24.2 us (31%)
  starting transfers between devices  23.7 us (31%)
  local copies, waits for them, and re-layouts  2.12 us (3%)
  other arithmetic  1.18 us (2%)
    pallas_call x4, Pallas kernels, round_call(): pl.pallas_call(functools.partial(round_kernel, plan), in_specs=[SMEM] * 2...  17 us
    ppermute x11, waiting for transfers between devices, swap(): return lax.ppermute(value, 'lm', [(i, i ^ 1 << bit) for i in range(n_lm)])  16 us
    ppermute x11, starting transfers between devices, swap(): return lax.ppermute(value, 'lm', [(i, i ^ 1 << bit) for i in range(n_lm)])  12.7 us
    ppermute x6, starting transfers between devices, body(): lax.ppermute(crossed[pos], 'cam', [(i, i ^ pos + 1) for i in range(n_cam)])  10.9 us
    ppermute x6, waiting for transfers between devices, body(): lax.ppermute(crossed[pos], 'cam', [(i, i ^ pos + 1) for i in range(n_cam)])  10.3 us
    unnamed x6, local copies, waits for them, and re-layouts  2.12 us
    pallas_call x2, Pallas kernels, body(): pl.pallas_call(functools.partial(finish_kernel, row_blocks, n_cam - 1), g...  1.64 us
  transfers between devices with their start and end apart: 17, of which 8 were waited for; matrix products, arithmetic and copies ran while one was open for 2% of the time, Pallas kernels for 18%

profile of v5, /device:TPU:0, one launch (start us, length us, event | category | flops | bytes accessed | tf_op | source)
XLA Modules:
  0.0 77.7 jit_solution(7112707119656981963)
XLA Ops:
  0.0 0.5 collective-permute-start.1
  0.5 0.8 fusion.3
  1.2 0.1 collective-permute-start
  1.3 0.5 collective-permute-start.2
  1.8 0.1 select_reduce_fusion.1.table.table_a
  1.9 0.0 copy-start
  1.9 1.4 %copy-done = bf16[2,16,64,384]{3,2,1,0:T(8,128)(2,1)S(1)} copy-done((bf16[2,16,64,384]{3,2,1,0:T(8,128)(2,1)S(1)}, bf16[2,16,64,384]{3,2,1,0:T(8,128)(2,1)}, u32[]{:S(2)}) %copy-start) | copy-done | bytes 1572888
  3.3 0.0 copy-start.1
  3.3 0.7 copy-done.1
  4.0 1.1 %form_own.1 = (bf16[2,1024,768]{2,1,0:T(8,128)(2,1)S(1)}, bf16[2,16,64,384]{3,2,1,0:T(8,128)(2,1)S(1)}) custom-call(s32[2,48]{1,0:T(2,128)S(1)} %select_reduce_fusion.1.table.table_a, bf16[2,16,64,384]{3,2,1,0:T(8,128)(2,1)S(1)} %copy-done, f32[3,3,256]{2,1,0:T(4,128)S(1)} %copy-done.1), custom_call_target="tpu_custom_call" | custom-call | tf_op jit(solution)/shard_map/form_own/pallas_call | solution.py:340
  5.1 0.0 collective-permute-done
  5.1 0.1 select_reduce_fusion.table.table_b
  5.2 0.0 collective-permute-done.2.cur
  5.2 0.0 collective-permute-done.1.pan.pan_b
  5.3 1.4 %form_other.1.rows_b = bf16[2,1024,768]{2,1,0:T(8,128)(2,1)S(1)} custom-call(s32[2,48]{1,0:T(2,128)S(1)} %select_reduce_fusion.table.table_b, bf16[2,16,64,384]{3,2,1,0:T(8,128)(2,1)S(1)} %collective-permute-done.1.pan.pan_b, f32[3,3,256]{2,1,0:T(4,128)S(1)} %collective-permute-done.2.cur), custom_call_target="tpu_custom_call" | custom-call | tf_op jit(solution)/shard_map/form_other/pallas_call | solution.py:353
  6.6 3.4 %send.2 = (s16[528,512]{1,0:T(8,128)(2,1)S(1)}, s16[528,512]{1,0:T(8,128)(2,1)S(1)}) custom-call(s32[2,48]{1,0:T(2,128)S(1)} %select_reduce_fusion.1.table.table_a, s32[2,48]{1,0:T(2,128)S(1)} %select_reduce_fusion.table.table_b, bf16[2,16,64,384]{3,2,1,0:T(8,128)(2,1)S(1)} %get-tuple-element.31.pan_a, ...), custom_call_target="tpu_custom_call" | custom-call | tf_op jit(solution)/shard_map/send/pallas_call | solution.py:370
  10.0 4.9 %collective-permute-start.5 = (s16[528,512]{1,0:T(8,128)(2,1)S(1)}, s16[528,512]{1,0:T(8,128)(2,1)S(1)}, u32[]{:S(2)}, u32[]{:S(2)}) collective-permute-start(s16[528,512]{1,0:T(8,128)(2,1)S(1)} %get-tuple-element.34), channel_id=1, source_target_pairs={{0,16},{4,20},{8,24},{12,28},{16,0},{20,4},{24,8},{28,12},{1,17},{... | collective-permute-start | bytes 1622024 | tf_op jit(solution)/shard_map/ppermute | solution.py:319
  15.0 0.0 collective-permute-start.3
  15.0 4.4 %keep.2 = (f32[2,256,512]{2,1,0:T(8,128)S(1)}, f32[2,256,512]{2,1,0:T(8,128)S(1)}) custom-call(s32[2,48]{1,0:T(2,128)S(1)} %select_reduce_fusion.1.table.table_a, s32[2,48]{1,0:T(2,128)S(1)} %select_reduce_fusion.table.table_b, bf16[2,16,64,384]{3,2,1,0:T(8,128)(2,1)S(1)} %get-tuple-element.31.pan_a, ...), custom_call_target="tpu_custom_call" | custom-call | tf_op jit(solution)/shard_map/keep/pallas_call | solution.py:370
  19.4 7.1 %collective-permute-done.5.rest_0_.rest_4_ = s16[528,512]{1,0:T(8,128)(2,1)S(1)} collective-permute-done((s16[528,512]{1,0:T(8,128)(2,1)S(1)}, s16[528,512]{1,0:T(8,128)(2,1)S(1)}, u32[]{:S(2)}, u32[]{:S(2)}) %collective-permute-start.5) | collective-permute-done | bytes 540704 | tf_op jit(solution)/shard_map/ppermute | solution.py:319
  26.5 0.2 relay.5
  26.7 1.7 %collective-permute-start.6 = (s16[272,512]{1,0:T(8,128)(2,1)S(1)}, s16[272,512]{1,0:T(8,128)(2,1)S(1)}, u32[]{:S(2)}, u32[]{:S(2)}) collective-permute-start(s16[272,512]{1,0:T(8,128)(2,1)S(1)} %relay.5), channel_id=1, source_target_pairs={{0,8},{4,12},{8,0},{12,4},{16,24},{20,28},{24,16},{28,20},{1,9},{5... | collective-permute-start | bytes 835592 | tf_op jit(solution)/shard_map/ppermute | solution.py:319
  28.4 0.0 collective-permute-done.3.rest_0_.rest_1_
  28.4 0.2 relay.4
  28.7 1.4 %collective-permute-start.4 = (s16[272,512]{1,0:T(8,128)(2,1)S(1)}, s16[272,512]{1,0:T(8,128)(2,1)S(1)}, u32[]{:S(2)}, u32[]{:S(2)}) collective-permute-start(s16[272,512]{1,0:T(8,128)(2,1)S(1)} %relay.4), channel_id=1, source_target_pairs={{0,16},{4,20},{8,24},{12,28},{16,0},{20,4},{24,8},{28,12},{1,17},{... | collective-permute-start | bytes 835592 | tf_op jit(solution)/shard_map/ppermute | solution.py:319
  30.1 3.7 %send.3 = (s16[528,512]{1,0:T(8,128)(2,1)S(1)}, s16[528,512]{1,0:T(8,128)(2,1)S(1)}) custom-call(s32[2,48]{1,0:T(2,128)S(1)} %select_reduce_fusion.1.table.table_a, s32[2,48]{1,0:T(2,128)S(1)} %select_reduce_fusion.table.table_b, bf16[2,16,64,384]{3,2,1,0:T(8,128)(2,1)S(1)} %get-tuple-element.31.pan_a, ...), custom_call_target="tpu_custom_call" | custom-call | tf_op jit(solution)/shard_map/send/pallas_call | solution.py:370
  33.8 1.7 %collective-permute-done.6.rest_5_ = s16[272,512]{1,0:T(8,128)(2,1)S(1)} collective-permute-done((s16[272,512]{1,0:T(8,128)(2,1)S(1)}, s16[272,512]{1,0:T(8,128)(2,1)S(1)}, u32[]{:S(2)}, u32[]{:S(2)}) %collective-permute-start.6) | collective-permute-done | bytes 278560 | tf_op jit(solution)/shard_map/ppermute | solution.py:319
  35.5 1.8 %collective-permute-done.4.rest_2_ = s16[272,512]{1,0:T(8,128)(2,1)S(1)} collective-permute-done((s16[272,512]{1,0:T(8,128)(2,1)S(1)}, s16[272,512]{1,0:T(8,128)(2,1)S(1)}, u32[]{:S(2)}, u32[]{:S(2)}) %collective-permute-start.4) | collective-permute-done | bytes 278560 | tf_op jit(solution)/shard_map/ppermute | solution.py:319
  37.3 0.5 cross.2
  37.8 0.4 collective-permute-start.7
  38.1 1.4 %collective-permute-start.12 = (s16[528,512]{1,0:T(8,128)(2,1)S(1)}, s16[528,512]{1,0:T(8,128)(2,1)S(1)}, u32[]{:S(2)}, u32[]{:S(2)}) collective-permute-start(s16[528,512]{1,0:T(8,128)(2,1)S(1)} %get-tuple-element.52), channel_id=1, source_target_pairs={{0,16},{4,20},{8,24},{12,28},{16,0},{20,4},{24,8},{28,12},{1,17},{... | collective-permute-start | bytes 1622024 | tf_op jit(solution)/shard_map/ppermute | solution.py:319
  39.6 2.4 %collective-permute-start.10 = (s16[528,128]{1,0:T(8,128)(2,1)S(1)}, s16[528,128]{1,0:T(8,128)(2,1)S(1)}, u32[]{:S(2)}, u32[]{:S(2)}) collective-permute-start(s16[528,128]{1,0:T(8,128)(2,1)S(1)} %get-tuple-element.46), channel_id=1, source_target_pairs={{0,1},{1,0},{2,3},{3,2},{4,5},{5,4},{6,7},{7,6},{8,9},{9,8},{10,11... | collective-permute-start | bytes 405512 | tf_op jit(solution)/shard_map/ppermute | solution.py:427
  42.0 2.6 %collective-permute-start.9 = (s16[528,128]{1,0:T(8,128)(2,1)S(1)}, s16[528,128]{1,0:T(8,128)(2,1)S(1)}, u32[]{:S(2)}, u32[]{:S(2)}) collective-permute-start(s16[528,128]{1,0:T(8,128)(2,1)S(1)} %get-tuple-element.47), channel_id=1, source_target_pairs={{0,2},{1,3},{2,0},{3,1},{4,6},{5,7},{6,4},{7,5},{8,10},{9,11},{10,... | collective-permute-start | bytes 405512 | tf_op jit(solution)/shard_map/ppermute | solution.py:427
  44.6 1.1 %collective-permute-start.8 = (s16[528,128]{1,0:T(8,128)(2,1)S(1)}, s16[528,128]{1,0:T(8,128)(2,1)S(1)}, u32[]{:S(2)}, u32[]{:S(2)}) collective-permute-start(s16[528,128]{1,0:T(8,128)(2,1)S(1)} %get-tuple-element.48), channel_id=1, source_target_pairs={{0,3},{1,2},{2,1},{3,0},{4,7},{5,6},{6,5},{7,4},{8,11},{9,10},{10,... | collective-permute-start | bytes 405512 | tf_op jit(solution)/shard_map/ppermute | solution.py:427
  45.7 5.4 %keep.3 = (f32[2,256,512]{2,1,0:T(8,128)S(1)}, f32[2,256,512]{2,1,0:T(8,128)S(1)}) custom-call(s32[2,48]{1,0:T(2,128)S(1)} %select_reduce_fusion.1.table.table_a, s32[2,48]{1,0:T(2,128)S(1)} %select_reduce_fusion.table.table_b, bf16[2,16,64,384]{3,2,1,0:T(8,128)(2,1)S(1)} %get-tuple-element.31.pan_a, ...), custom_call_target="tpu_custom_call" | custom-call | tf_op jit(solution)/shard_map/keep/pallas_call | solution.py:370
  51.1 0.0 collective-permute-done.10.rest_2_
  51.1 4.0 %collective-permute-done.9.rest_1_ = s16[528,128]{1,0:T(8,128)(2,1)S(1)} collective-permute-done((s16[528,128]{1,0:T(8,128)(2,1)S(1)}, s16[528,128]{1,0:T(8,128)(2,1)S(1)}, u32[]{:S(2)}, u32[]{:S(2)}) %collective-permute-start.9) | collective-permute-done | bytes 135200 | tf_op jit(solution)/shard_map/ppermute | solution.py:427
  55.1 0.0 collective-permute-done.8.rest_0_
  55.1 0.0 collective-permute-done.7.rest_0_.rest_1_
  55.1 0.2 relay.6
  55.3 0.7 collective-permute-start.11
  56.1 0.0 collective-permute-done.12.rest_0_.rest_4_
  56.1 0.2 relay.7
  56.3 0.0 copy-start.2
  56.3 1.2 %collective-permute-start.13 = (s16[272,512]{1,0:T(8,128)(2,1)S(1)}, s16[272,512]{1,0:T(8,128)(2,1)S(1)}, u32[]{:S(2)}, u32[]{:S(2)}) collective-permute-start(s16[272,512]{1,0:T(8,128)(2,1)S(1)} %relay.7), channel_id=1, source_target_pairs={{0,8},{4,12},{8,0},{12,4},{16,24},{20,28},{24,16},{28,20},{1,9},{5... | collective-permute-start | bytes 835592 | tf_op jit(solution)/shard_map/ppermute | solution.py:319
  57.5 4.4 %collective-permute-done.11.rest_2_ = s16[272,512]{1,0:T(8,128)(2,1)S(1)} collective-permute-done((s16[272,512]{1,0:T(8,128)(2,1)S(1)}, s16[272,512]{1,0:T(8,128)(2,1)S(1)}, u32[]{:S(2)}, u32[]{:S(2)}) %collective-permute-start.11) | collective-permute-done | bytes 278560 | tf_op jit(solution)/shard_map/ppermute | solution.py:319
  62.0 1.0 %collective-permute-done.13.rest_5_ = s16[272,512]{1,0:T(8,128)(2,1)S(1)} collective-permute-done((s16[272,512]{1,0:T(8,128)(2,1)S(1)}, s16[272,512]{1,0:T(8,128)(2,1)S(1)}, u32[]{:S(2)}, u32[]{:S(2)}) %collective-permute-start.13) | collective-permute-done | bytes 278560 | tf_op jit(solution)/shard_map/ppermute | solution.py:319
  63.0 0.5 cross.3
  63.4 2.4 %collective-permute-start.14 = (s16[528,128]{1,0:T(8,128)(2,1)S(1)}, s16[528,128]{1,0:T(8,128)(2,1)S(1)}, u32[]{:S(2)}, u32[]{:S(2)}) collective-permute-start(s16[528,128]{1,0:T(8,128)(2,1)S(1)} %get-tuple-element.54), channel_id=1, source_target_pairs={{0,3},{1,2},{2,1},{3,0},{4,7},{5,6},{6,5},{7,4},{8,11},{9,10},{10,... | collective-permute-start | bytes 405512 | tf_op jit(solution)/shard_map/ppermute | solution.py:427
  65.8 1.9 %collective-permute-start.15 = (s16[528,128]{1,0:T(8,128)(2,1)S(1)}, s16[528,128]{1,0:T(8,128)(2,1)S(1)}, u32[]{:S(2)}, u32[]{:S(2)}) collective-permute-start(s16[528,128]{1,0:T(8,128)(2,1)S(1)} %get-tuple-element.55), channel_id=1, source_target_pairs={{0,2},{1,3},{2,0},{3,1},{4,6},{5,7},{6,4},{7,5},{8,10},{9,11},{10,... | collective-permute-start | bytes 405512 | tf_op jit(solution)/shard_map/ppermute | solution.py:427
  67.8 0.5 collective-permute-start.16
  68.3 0.1 pad_add_fusion.me_ref
  68.3 0.0 copy-done.2
  68.3 0.1 pad_maximum_fusion.wide_ref
  68.4 0.6 base.3.base_ref
  69.1 0.8 %finish.2.rest_3_ = f32[256,512]{1,0:T(8,128)} custom-call(f32[256,256]{1,0:T(8,128)S(1)} %base.3.base_ref, s16[528,128]{1,0:T(8,128)(2,1)S(1)} %collective-permute-done.8.rest_0_, s16[528,128]{1,0:T(8,128)(2,1)S(1)} %collective-permute-done.9.rest_1_, s16[528,128]{1,0:T(8,128)(2,1)S(1)} %collective-permute-done.10.rest_2_), custom_call_target="tpu_custom_call" | custom-call | tf_op jit(solution)/shard_map/finish/pallas_call | solution.py:439
  69.9 0.6 base.2.base_ref
  70.6 1.1 %collective-permute-done.14.rest_0_ = s16[528,128]{1,0:T(8,128)(2,1)S(1)} collective-permute-done((s16[528,128]{1,0:T(8,128)(2,1)S(1)}, s16[528,128]{1,0:T(8,128)(2,1)S(1)}, u32[]{:S(2)}, u32[]{:S(2)}) %collective-permute-start.14) | collective-permute-done | bytes 135200 | tf_op jit(solution)/shard_map/ppermute | solution.py:427
  71.6 5.2 %collective-permute-done.15.rest_1_ = s16[528,128]{1,0:T(8,128)(2,1)S(1)} collective-permute-done((s16[528,128]{1,0:T(8,128)(2,1)S(1)}, s16[528,128]{1,0:T(8,128)(2,1)S(1)}, u32[]{:S(2)}, u32[]{:S(2)}) %collective-permute-start.15) | collective-permute-done | bytes 135200 | tf_op jit(solution)/shard_map/ppermute | solution.py:427
  76.9 0.0 collective-permute-done.16.rest_2_
  76.9 0.8 %finish.3 = f32[256,512]{1,0:T(8,128)} custom-call(f32[256,256]{1,0:T(8,128)S(1)} %base.2.base_ref, s16[528,128]{1,0:T(8,128)(2,1)S(1)} %collective-permute-done.14.rest_0_, s16[528,128]{1,0:T(8,128)(2,1)S(1)} %collective-permute-done.15.rest_1_, s16[528,128]{1,0:T(8,128)(2,1)S(1)} %collective-permute-done.16.rest_2_, ...), custom_call_target="tpu_custom_call", output_to_operand_aliasing={{}: (4, {})} | custom-call | tf_op jit(solution)/shard_map/finish/pallas_call | solution.py:439
  (2 shorter events, 0.0 us)
Async XLA Ops:
  0.0 5.2 %collective-permute-start.1 = (bf16[2,16,64,384]{3,2,1,0:T(8,128)(2,1)}, bf16[2,16,64,384]{3,2,1,0:T(8,128)(2,1)S(1)}, u32[]{:S(2)}, u32[]{:S(2)}) collective-permute-start(bf16[2,16,64,384]{3,2,1,0:T(8,128)(2,1)} %pan_ref.1), channel_id=1, source_target_pairs={{0,4},{4,0},{8,12},{12,8},{16,20},{20,16},{24,28},{28,24},{1,5},{5... | collective-permute-start | bytes 4718600 | tf_op jit(solution)/shard_map/ppermute | solution.py:319
  1.2 3.9 %collective-permute-start = (s32[2,16]{1,0:T(2,128)S(1)}, s32[2,16]{1,0:T(2,128)S(1)}, u32[]{:S(2)}, u32[]{:S(2)}) collective-permute-start(s32[2,16]{1,0:T(2,128)S(1)} %get-tuple-element.58), channel_id=1, source_target_pairs={{0,4},{4,0},{8,12},{12,8},{16,20},{20,16},{24,28},{28,24},{1,5},{5... | collective-permute-start | bytes 392 | tf_op jit(solution)/shard_map/ppermute | solution.py:319
  1.3 3.9 %collective-permute-start.2 = (f32[3,3,256]{2,1,0:T(4,128)}, f32[3,3,256]{2,1,0:T(4,128)S(1)}, u32[]{:S(2)}, u32[]{:S(2)}) collective-permute-start(f32[3,3,256]{2,1,0:T(4,128)} %cur_ref.1), channel_id=1, source_target_pairs={{0,4},{4,0},{8,12},{12,8},{16,20},{20,16},{24,28},{28,24},{1,5},{5... | collective-permute-start | bytes 27656 | tf_op jit(solution)/shard_map/ppermute | solution.py:319
  1.9 1.4 %copy-start = (bf16[2,16,64,384]{3,2,1,0:T(8,128)(2,1)S(1)}, bf16[2,16,64,384]{3,2,1,0:T(8,128)(2,1)}, u32[]{:S(2)}) copy-start(bf16[2,16,64,384]{3,2,1,0:T(8,128)(2,1)} %pan_ref.1) | copy-start | bytes 4718596
  3.3 0.7 copy-start.1
  10.0 16.5 %collective-permute-start.5 = (s16[528,512]{1,0:T(8,128)(2,1)S(1)}, s16[528,512]{1,0:T(8,128)(2,1)S(1)}, u32[]{:S(2)}, u32[]{:S(2)}) collective-permute-start(s16[528,512]{1,0:T(8,128)(2,1)S(1)} %get-tuple-element.34), channel_id=1, source_target_pairs={{0,16},{4,20},{8,24},{12,28},{16,0},{20,4},{24,8},{28,12},{1,17},{... | collective-permute-start | bytes 1622024 | tf_op jit(solution)/shard_map/ppermute | solution.py:319
  15.0 13.4 %collective-permute-start.3 = (s16[528,512]{1,0:T(8,128)(2,1)S(1)}, s16[528,512]{1,0:T(8,128)(2,1)S(1)}, u32[]{:S(2)}, u32[]{:S(2)}) collective-permute-start(s16[528,512]{1,0:T(8,128)(2,1)S(1)} %get-tuple-element.33), channel_id=1, source_target_pairs={{0,8},{4,12},{8,0},{12,4},{16,24},{20,28},{24,16},{28,20},{1,9},{5... | collective-permute-start | bytes 1622024 | tf_op jit(solution)/shard_map/ppermute | solution.py:319
  26.7 8.8 %collective-permute-start.6 = (s16[272,512]{1,0:T(8,128)(2,1)S(1)}, s16[272,512]{1,0:T(8,128)(2,1)S(1)}, u32[]{:S(2)}, u32[]{:S(2)}) collective-permute-start(s16[272,512]{1,0:T(8,128)(2,1)S(1)} %relay.5), channel_id=1, source_target_pairs={{0,8},{4,12},{8,0},{12,4},{16,24},{20,28},{24,16},{28,20},{1,9},{5... | collective-permute-start | bytes 835592 | tf_op jit(solution)/shard_map/ppermute | solution.py:319
  28.7 8.6 %collective-permute-start.4 = (s16[272,512]{1,0:T(8,128)(2,1)S(1)}, s16[272,512]{1,0:T(8,128)(2,1)S(1)}, u32[]{:S(2)}, u32[]{:S(2)}) collective-permute-start(s16[272,512]{1,0:T(8,128)(2,1)S(1)} %relay.4), channel_id=1, source_target_pairs={{0,16},{4,20},{8,24},{12,28},{16,0},{20,4},{24,8},{28,12},{1,17},{... | collective-permute-start | bytes 835592 | tf_op jit(solution)/shard_map/ppermute | solution.py:319
  37.8 17.3 %collective-permute-start.7 = (s16[528,512]{1,0:T(8,128)(2,1)S(1)}, s16[528,512]{1,0:T(8,128)(2,1)S(1)}, u32[]{:S(2)}, u32[]{:S(2)}) collective-permute-start(s16[528,512]{1,0:T(8,128)(2,1)S(1)} %get-tuple-element.49), channel_id=1, source_target_pairs={{0,8},{4,12},{8,0},{12,4},{16,24},{20,28},{24,16},{28,20},{1,9},{5... | collective-permute-start | bytes 1622024 | tf_op jit(solution)/shard_map/ppermute | solution.py:319
  38.1 17.9 %collective-permute-start.12 = (s16[528,512]{1,0:T(8,128)(2,1)S(1)}, s16[528,512]{1,0:T(8,128)(2,1)S(1)}, u32[]{:S(2)}, u32[]{:S(2)}) collective-permute-start(s16[528,512]{1,0:T(8,128)(2,1)S(1)} %get-tuple-element.52), channel_id=1, source_target_pairs={{0,16},{4,20},{8,24},{12,28},{16,0},{20,4},{24,8},{28,12},{1,17},{... | collective-permute-start | bytes 1622024 | tf_op jit(solution)/shard_map/ppermute | solution.py:319
  39.6 11.6 %collective-permute-start.10 = (s16[528,128]{1,0:T(8,128)(2,1)S(1)}, s16[528,128]{1,0:T(8,128)(2,1)S(1)}, u32[]{:S(2)}, u32[]{:S(2)}) collective-permute-start(s16[528,128]{1,0:T(8,128)(2,1)S(1)} %get-tuple-element.46), channel_id=1, source_target_pairs={{0,1},{1,0},{2,3},{3,2},{4,5},{5,4},{6,7},{7,6},{8,9},{9,8},{10,11... | collective-permute-start | bytes 405512 | tf_op jit(solution)/shard_map/ppermute | solution.py:427
  42.0 13.1 %collective-permute-start.9 = (s16[528,128]{1,0:T(8,128)(2,1)S(1)}, s16[528,128]{1,0:T(8,128)(2,1)S(1)}, u32[]{:S(2)}, u32[]{:S(2)}) collective-permute-start(s16[528,128]{1,0:T(8,128)(2,1)S(1)} %get-tuple-element.47), channel_id=1, source_target_pairs={{0,2},{1,3},{2,0},{3,1},{4,6},{5,7},{6,4},{7,5},{8,10},{9,11},{10,... | collective-permute-start | bytes 405512 | tf_op jit(solution)/shard_map/ppermute | solution.py:427
  44.6 10.5 %collective-permute-start.8 = (s16[528,128]{1,0:T(8,128)(2,1)S(1)}, s16[528,128]{1,0:T(8,128)(2,1)S(1)}, u32[]{:S(2)}, u32[]{:S(2)}) collective-permute-start(s16[528,128]{1,0:T(8,128)(2,1)S(1)} %get-tuple-element.48), channel_id=1, source_target_pairs={{0,3},{1,2},{2,1},{3,0},{4,7},{5,6},{6,5},{7,4},{8,11},{9,10},{10,... | collective-permute-start | bytes 405512 | tf_op jit(solution)/shard_map/ppermute | solution.py:427
  55.3 6.6 %collective-permute-start.11 = (s16[272,512]{1,0:T(8,128)(2,1)S(1)}, s16[272,512]{1,0:T(8,128)(2,1)S(1)}, u32[]{:S(2)}, u32[]{:S(2)}) collective-permute-start(s16[272,512]{1,0:T(8,128)(2,1)S(1)} %relay.6), channel_id=1, source_target_pairs={{0,16},{4,20},{8,24},{12,28},{16,0},{20,4},{24,8},{28,12},{1,17},{... | collective-permute-start | bytes 835592 | tf_op jit(solution)/shard_map/ppermute | solution.py:319
  56.3 12.0 %copy-start.2 = (f32[4,64,64]{2,1,0:T(8,128)S(1)}, f32[4,64,64]{2,1,0:T(8,128)}, u32[]{:S(2)}) copy-start(f32[4,64,64]{2,1,0:T(8,128)} %param.9) | copy-start | bytes 196612
  56.3 6.6 %collective-permute-start.13 = (s16[272,512]{1,0:T(8,128)(2,1)S(1)}, s16[272,512]{1,0:T(8,128)(2,1)S(1)}, u32[]{:S(2)}, u32[]{:S(2)}) collective-permute-start(s16[272,512]{1,0:T(8,128)(2,1)S(1)} %relay.7), channel_id=1, source_target_pairs={{0,8},{4,12},{8,0},{12,4},{16,24},{20,28},{24,16},{28,20},{1,9},{5... | collective-permute-start | bytes 835592 | tf_op jit(solution)/shard_map/ppermute | solution.py:319
  63.4 8.2 %collective-permute-start.14 = (s16[528,128]{1,0:T(8,128)(2,1)S(1)}, s16[528,128]{1,0:T(8,128)(2,1)S(1)}, u32[]{:S(2)}, u32[]{:S(2)}) collective-permute-start(s16[528,128]{1,0:T(8,128)(2,1)S(1)} %get-tuple-element.54), channel_id=1, source_target_pairs={{0,3},{1,2},{2,1},{3,0},{4,7},{5,6},{6,5},{7,4},{8,11},{9,10},{10,... | collective-permute-start | bytes 405512 | tf_op jit(solution)/shard_map/ppermute | solution.py:427
  65.8 11.1 %collective-permute-start.15 = (s16[528,128]{1,0:T(8,128)(2,1)S(1)}, s16[528,128]{1,0:T(8,128)(2,1)S(1)}, u32[]{:S(2)}, u32[]{:S(2)}) collective-permute-start(s16[528,128]{1,0:T(8,128)(2,1)S(1)} %get-tuple-element.55), channel_id=1, source_target_pairs={{0,2},{1,3},{2,0},{3,1},{4,6},{5,7},{6,4},{7,5},{8,10},{9,11},{10,... | collective-permute-start | bytes 405512 | tf_op jit(solution)/shard_map/ppermute | solution.py:427
  67.8 9.1 %collective-permute-start.16 = (s16[528,128]{1,0:T(8,128)(2,1)S(1)}, s16[528,128]{1,0:T(8,128)(2,1)S(1)}, u32[]{:S(2)}, u32[]{:S(2)}) collective-permute-start(s16[528,128]{1,0:T(8,128)(2,1)S(1)} %get-tuple-element.56), channel_id=1, source_target_pairs={{0,1},{1,0},{2,3},{3,2},{4,5},{5,4},{6,7},{7,6},{8,9},{9,8},{10,11... | collective-permute-start | bytes 405512 | tf_op jit(solution)/shard_map/ppermute | solution.py:427

commit v6 on v3

--- a/solution.py
+++ b/solution.py
@@ -144,6 +144,7 @@
     outs, right, pair_at, acc = rest[:2], rest[2], rest[3], rest[4]
     extent = row_blocks * CB
     columns = pairs * LANES
+    slice_size = min(columns, 2 * WIDE)
     for base, order, out in zip(bases, orders, outs):
         acc[...] = jnp.zeros_like(acc)
         spots = [spot_of(half + (halves if sending else 0), order) for half in range(halves)]
@@ -216,7 +217,7 @@
             lax.fori_loop(0, tiles, one_tile, 0)
 
         def store(start, carry):
-            lanes = pl.ds(pl.multiple_of(start * WIDE, WIDE), WIDE)
+            lanes = pl.ds(pl.multiple_of(start * slice_size, slice_size), slice_size)
             if sending:
                 parts = [
                     functools.partial(
@@ -231,7 +232,7 @@
                     out[half, :, lanes] = acc[half, :, lanes]
             return carry
 
-        lax.fori_loop(0, columns // WIDE, store, 0)
+        lax.fori_loop(0, columns // slice_size, store, 0)
 
 
 def relay_kernel(plan, keep, *rest):

time: 77.9 us -> 76.9 us (0.987)
  starting transfers between devices: 24.9 us -> 28.6 us
  waiting for transfers between devices: 25.1 us -> 22.8 us
  Pallas kernels: 24.3 us -> 22.6 us
    ppermute x11, starting transfers between devices: 12.1 us -> 16.1 us  [swap(): return lax.ppermute(value, 'lm', [(i, i ^ 1 << bit) for i in range(n_lm)])]
    ppermute x11, waiting for transfers between devices: 15 us -> 11.5 us  [swap(): return lax.ppermute(value, 'lm', [(i, i ^ 1 << bit) for i in range(n_lm)])]
    pallas_call x4, Pallas kernels: 16.8 us -> 15.4 us  [round_call(): pl.pallas_call(functools.partial(round_kernel, plan), in_specs=[SMEM] * 2...]
    ppermute x6, waiting for transfers between devices: 10.1 us -> 11.3 us  [body(): lax.ppermute(value, 'cam', [(i, i ^ pos + 1) for i in range(n_cam)])]
  transfers between devices with their start and end apart: 17 -> 17, of which waited for: 8 -> 7; matrix products, arithmetic and copies ran while one was open for 2% -> 2% of each run, Pallas kernels for 17% -> 15%
where the time goes in v6:
time: 76.9 us; the launch traced here: 77.5 us
  starting transfers between devices  28.6 us (37%)
  waiting for transfers between devices  22.8 us (30%)
  Pallas kernels  22.6 us (29%)
  local copies, waits for them, and re-layouts  2.12 us (3%)
  other arithmetic  1.18 us (2%)
    ppermute x11, starting transfers between devices, swap(): return lax.ppermute(value, 'lm', [(i, i ^ 1 << bit) for i in range(n_lm)])  16.1 us
    pallas_call x4, Pallas kernels, round_call(): pl.pallas_call(functools.partial(round_kernel, plan), in_specs=[SMEM] * 2...  15.4 us
    ppermute x6, starting transfers between devices, body(): lax.ppermute(value, 'cam', [(i, i ^ pos + 1) for i in range(n_cam)])  12.5 us
    ppermute x11, waiting for transfers between devices, swap(): return lax.ppermute(value, 'lm', [(i, i ^ 1 << bit) for i in range(n_lm)])  11.5 us
    ppermute x6, waiting for transfers between devices, body(): lax.ppermute(value, 'cam', [(i, i ^ pos + 1) for i in range(n_cam)])  11.3 us
    unnamed x6, local copies, waits for them, and re-layouts  2.12 us
    pallas_call x2, Pallas kernels, body(): pl.pallas_call(functools.partial(finish_kernel, row_blocks, n_cam - 1), g...  1.64 us
  transfers between devices with their start and end apart: 17, of which 7 were waited for; matrix products, arithmetic and copies ran while one was open for 2% of the time, Pallas kernels for 15%

profile of v6, /device:TPU:0, one launch (start us, length us, event | category | flops | bytes accessed | tf_op | source)
XLA Modules:
  0.0 77.5 jit_solution(3239529250069308961)
XLA Ops:
  0.0 0.5 collective-permute-start.1
  0.5 0.8 fusion.3
  1.2 0.1 collective-permute-start
  1.3 0.5 collective-permute-start.2
  1.8 0.1 select_reduce_fusion.1.table.table_a
  1.9 0.0 copy-start
  1.9 1.4 %copy-done = bf16[2,16,64,384]{3,2,1,0:T(8,128)(2,1)S(1)} copy-done((bf16[2,16,64,384]{3,2,1,0:T(8,128)(2,1)S(1)}, bf16[2,16,64,384]{3,2,1,0:T(8,128)(2,1)}, u32[]{:S(2)}) %copy-start) | copy-done | bytes 1572888
  3.3 0.0 copy-start.1
  3.3 0.7 copy-done.1
  4.0 1.1 %form_own.1 = (bf16[2,1024,768]{2,1,0:T(8,128)(2,1)S(1)}, bf16[2,16,64,384]{3,2,1,0:T(8,128)(2,1)S(1)}) custom-call(s32[2,48]{1,0:T(2,128)S(1)} %select_reduce_fusion.1.table.table_a, bf16[2,16,64,384]{3,2,1,0:T(8,128)(2,1)S(1)} %copy-done, f32[3,3,256]{2,1,0:T(4,128)S(1)} %copy-done.1), custom_call_target="tpu_custom_call" | custom-call | tf_op jit(solution)/shard_map/form_own/pallas_call | solution.py:341
  5.2 0.0 collective-permute-done
  5.2 0.1 select_reduce_fusion.table.table_b
  5.3 0.0 collective-permute-done.2.cur
  5.3 0.0 collective-permute-done.1.pan.pan_b
  5.3 1.2 %form_other.1.rows_b = bf16[2,1024,768]{2,1,0:T(8,128)(2,1)S(1)} custom-call(s32[2,48]{1,0:T(2,128)S(1)} %select_reduce_fusion.table.table_b, bf16[2,16,64,384]{3,2,1,0:T(8,128)(2,1)S(1)} %collective-permute-done.1.pan.pan_b, f32[3,3,256]{2,1,0:T(4,128)S(1)} %collective-permute-done.2.cur), custom_call_target="tpu_custom_call" | custom-call | tf_op jit(solution)/shard_map/form_other/pallas_call | solution.py:354
  6.5 4.1 %send.2 = (s16[528,512]{1,0:T(8,128)(2,1)S(1)}, s16[528,512]{1,0:T(8,128)(2,1)S(1)}) custom-call(s32[2,48]{1,0:T(2,128)S(1)} %select_reduce_fusion.1.table.table_a, s32[2,48]{1,0:T(2,128)S(1)} %select_reduce_fusion.table.table_b, bf16[2,16,64,384]{3,2,1,0:T(8,128)(2,1)S(1)} %get-tuple-element.31.pan_a, ...), custom_call_target="tpu_custom_call" | custom-call | tf_op jit(solution)/shard_map/send/pallas_call | solution.py:371
  10.6 3.2 %collective-permute-start.5 = (s16[528,512]{1,0:T(8,128)(2,1)S(1)}, s16[528,512]{1,0:T(8,128)(2,1)S(1)}, u32[]{:S(2)}, u32[]{:S(2)}) collective-permute-start(s16[528,512]{1,0:T(8,128)(2,1)S(1)} %get-tuple-element.34), channel_id=1, source_target_pairs={{0,16},{4,20},{8,24},{12,28},{16,0},{20,4},{24,8},{28,12},{1,17},{... | collective-permute-start | bytes 1622024 | tf_op jit(solution)/shard_map/ppermute | solution.py:320
  13.8 3.1 %collective-permute-start.3 = (s16[528,512]{1,0:T(8,128)(2,1)S(1)}, s16[528,512]{1,0:T(8,128)(2,1)S(1)}, u32[]{:S(2)}, u32[]{:S(2)}) collective-permute-start(s16[528,512]{1,0:T(8,128)(2,1)S(1)} %get-tuple-element.33), channel_id=1, source_target_pairs={{0,8},{4,12},{8,0},{12,4},{16,24},{20,28},{24,16},{28,20},{1,9},{5... | collective-permute-start | bytes 1622024 | tf_op jit(solution)/shard_map/ppermute | solution.py:320
  16.9 3.6 %keep.2 = (f32[2,256,512]{2,1,0:T(8,128)S(1)}, f32[2,256,512]{2,1,0:T(8,128)S(1)}) custom-call(s32[2,48]{1,0:T(2,128)S(1)} %select_reduce_fusion.1.table.table_a, s32[2,48]{1,0:T(2,128)S(1)} %select_reduce_fusion.table.table_b, bf16[2,16,64,384]{3,2,1,0:T(8,128)(2,1)S(1)} %get-tuple-element.31.pan_a, ...), custom_call_target="tpu_custom_call" | custom-call | tf_op jit(solution)/shard_map/keep/pallas_call | solution.py:371
  20.5 5.3 %collective-permute-done.5.rest_0_.rest_4_ = s16[528,512]{1,0:T(8,128)(2,1)S(1)} collective-permute-done((s16[528,512]{1,0:T(8,128)(2,1)S(1)}, s16[528,512]{1,0:T(8,128)(2,1)S(1)}, u32[]{:S(2)}, u32[]{:S(2)}) %collective-permute-start.5) | collective-permute-done | bytes 540704 | tf_op jit(solution)/shard_map/ppermute | solution.py:320
  25.9 0.2 relay.5
  26.1 2.5 %collective-permute-start.6 = (s16[272,512]{1,0:T(8,128)(2,1)S(1)}, s16[272,512]{1,0:T(8,128)(2,1)S(1)}, u32[]{:S(2)}, u32[]{:S(2)}) collective-permute-start(s16[272,512]{1,0:T(8,128)(2,1)S(1)} %relay.5), channel_id=1, source_target_pairs={{0,8},{4,12},{8,0},{12,4},{16,24},{20,28},{24,16},{28,20},{1,9},{5... | collective-permute-start | bytes 835592 | tf_op jit(solution)/shard_map/ppermute | solution.py:320
  28.6 0.0 collective-permute-done.3.rest_0_.rest_1_
  28.6 0.2 relay.4
  28.9 1.6 %collective-permute-start.4 = (s16[272,512]{1,0:T(8,128)(2,1)S(1)}, s16[272,512]{1,0:T(8,128)(2,1)S(1)}, u32[]{:S(2)}, u32[]{:S(2)}) collective-permute-start(s16[272,512]{1,0:T(8,128)(2,1)S(1)} %relay.4), channel_id=1, source_target_pairs={{0,16},{4,20},{8,24},{12,28},{16,0},{20,4},{24,8},{28,12},{1,17},{... | collective-permute-start | bytes 835592 | tf_op jit(solution)/shard_map/ppermute | solution.py:320
  30.4 4.1 %send.3 = (s16[528,512]{1,0:T(8,128)(2,1)S(1)}, s16[528,512]{1,0:T(8,128)(2,1)S(1)}) custom-call(s32[2,48]{1,0:T(2,128)S(1)} %select_reduce_fusion.1.table.table_a, s32[2,48]{1,0:T(2,128)S(1)} %select_reduce_fusion.table.table_b, bf16[2,16,64,384]{3,2,1,0:T(8,128)(2,1)S(1)} %get-tuple-element.31.pan_a, ...), custom_call_target="tpu_custom_call" | custom-call | tf_op jit(solution)/shard_map/send/pallas_call | solution.py:371
  34.5 0.0 collective-permute-done.6.rest_5_
  34.5 1.0 %collective-permute-done.4.rest_2_ = s16[272,512]{1,0:T(8,128)(2,1)S(1)} collective-permute-done((s16[272,512]{1,0:T(8,128)(2,1)S(1)}, s16[272,512]{1,0:T(8,128)(2,1)S(1)}, u32[]{:S(2)}, u32[]{:S(2)}) %collective-permute-start.4) | collective-permute-done | bytes 278560 | tf_op jit(solution)/shard_map/ppermute | solution.py:320
  35.6 0.5 cross.2
  36.0 0.9 %collective-permute-start.7 = (s16[528,512]{1,0:T(8,128)(2,1)S(1)}, s16[528,512]{1,0:T(8,128)(2,1)S(1)}, u32[]{:S(2)}, u32[]{:S(2)}) collective-permute-start(s16[528,512]{1,0:T(8,128)(2,1)S(1)} %get-tuple-element.49), channel_id=1, source_target_pairs={{0,8},{4,12},{8,0},{12,4},{16,24},{20,28},{24,16},{28,20},{1,9},{5... | collective-permute-start | bytes 1622024 | tf_op jit(solution)/shard_map/ppermute | solution.py:320
  36.9 1.2 %collective-permute-start.12 = (s16[528,512]{1,0:T(8,128)(2,1)S(1)}, s16[528,512]{1,0:T(8,128)(2,1)S(1)}, u32[]{:S(2)}, u32[]{:S(2)}) collective-permute-start(s16[528,512]{1,0:T(8,128)(2,1)S(1)} %get-tuple-element.52), channel_id=1, source_target_pairs={{0,16},{4,20},{8,24},{12,28},{16,0},{20,4},{24,8},{28,12},{1,17},{... | collective-permute-start | bytes 1622024 | tf_op jit(solution)/shard_map/ppermute | solution.py:320
  38.1 4.3 %collective-permute-start.8 = (s16[528,128]{1,0:T(8,128)(2,1)S(1)}, s16[528,128]{1,0:T(8,128)(2,1)S(1)}, u32[]{:S(2)}, u32[]{:S(2)}) collective-permute-start(s16[528,128]{1,0:T(8,128)(2,1)S(1)} %get-tuple-element.46), channel_id=1, source_target_pairs={{0,1},{1,0},{2,3},{3,2},{4,5},{5,4},{6,7},{7,6},{8,9},{9,8},{10,11... | collective-permute-start | bytes 405512 | tf_op jit(solution)/shard_map/ppermute | solution.py:428
  42.4 3.2 %collective-permute-start.9 = (s16[528,128]{1,0:T(8,128)(2,1)S(1)}, s16[528,128]{1,0:T(8,128)(2,1)S(1)}, u32[]{:S(2)}, u32[]{:S(2)}) collective-permute-start(s16[528,128]{1,0:T(8,128)(2,1)S(1)} %get-tuple-element.47), channel_id=1, source_target_pairs={{0,2},{1,3},{2,0},{3,1},{4,6},{5,7},{6,4},{7,5},{8,10},{9,11},{10,... | collective-permute-start | bytes 405512 | tf_op jit(solution)/shard_map/ppermute | solution.py:428
  45.6 0.1 collective-permute-start.10
  45.7 3.6 %keep.3 = (f32[2,256,512]{2,1,0:T(8,128)S(1)}, f32[2,256,512]{2,1,0:T(8,128)S(1)}) custom-call(s32[2,48]{1,0:T(2,128)S(1)} %select_reduce_fusion.1.table.table_a, s32[2,48]{1,0:T(2,128)S(1)} %select_reduce_fusion.table.table_b, bf16[2,16,64,384]{3,2,1,0:T(8,128)(2,1)S(1)} %get-tuple-element.31.pan_a, ...), custom_call_target="tpu_custom_call" | custom-call | tf_op jit(solution)/shard_map/keep/pallas_call | solution.py:371
  49.3 0.0 collective-permute-done.8.rest_0_
  49.3 5.6 %collective-permute-done.9.rest_1_ = s16[528,128]{1,0:T(8,128)(2,1)S(1)} collective-permute-done((s16[528,128]{1,0:T(8,128)(2,1)S(1)}, s16[528,128]{1,0:T(8,128)(2,1)S(1)}, u32[]{:S(2)}, u32[]{:S(2)}) %collective-permute-start.9) | collective-permute-done | bytes 135200 | tf_op jit(solution)/shard_map/ppermute | solution.py:428
  54.9 0.0 collective-permute-done.10.rest_2_
  54.9 0.0 collective-permute-done.7.rest_0_.rest_1_
  54.9 0.2 relay.6
  55.1 1.1 %collective-permute-start.11 = (s16[272,512]{1,0:T(8,128)(2,1)S(1)}, s16[272,512]{1,0:T(8,128)(2,1)S(1)}, u32[]{:S(2)}, u32[]{:S(2)}) collective-permute-start(s16[272,512]{1,0:T(8,128)(2,1)S(1)} %relay.6), channel_id=1, source_target_pairs={{0,16},{4,20},{8,24},{12,28},{16,0},{20,4},{24,8},{28,12},{1,17},{... | collective-permute-start | bytes 835592 | tf_op jit(solution)/shard_map/ppermute | solution.py:320
  56.3 0.0 collective-permute-done.12.rest_0_.rest_4_
  56.3 0.2 relay.7
  56.6 0.0 copy-start.2
  56.6 1.5 %collective-permute-start.13 = (s16[272,512]{1,0:T(8,128)(2,1)S(1)}, s16[272,512]{1,0:T(8,128)(2,1)S(1)}, u32[]{:S(2)}, u32[]{:S(2)}) collective-permute-start(s16[272,512]{1,0:T(8,128)(2,1)S(1)} %relay.7), channel_id=1, source_target_pairs={{0,8},{4,12},{8,0},{12,4},{16,24},{20,28},{24,16},{28,20},{1,9},{5... | collective-permute-start | bytes 835592 | tf_op jit(solution)/shard_map/ppermute | solution.py:320
  58.0 3.7 %collective-permute-done.11.rest_2_ = s16[272,512]{1,0:T(8,128)(2,1)S(1)} collective-permute-done((s16[272,512]{1,0:T(8,128)(2,1)S(1)}, s16[272,512]{1,0:T(8,128)(2,1)S(1)}, u32[]{:S(2)}, u32[]{:S(2)}) %collective-permute-start.11) | collective-permute-done | bytes 278560 | tf_op jit(solution)/shard_map/ppermute | solution.py:320
  61.8 1.4 %collective-permute-done.13.rest_5_ = s16[272,512]{1,0:T(8,128)(2,1)S(1)} collective-permute-done((s16[272,512]{1,0:T(8,128)(2,1)S(1)}, s16[272,512]{1,0:T(8,128)(2,1)S(1)}, u32[]{:S(2)}, u32[]{:S(2)}) %collective-permute-start.13) | collective-permute-done | bytes 278560 | tf_op jit(solution)/shard_map/ppermute | solution.py:320
  63.2 0.5 cross.3
  63.7 2.5 %collective-permute-start.14 = (s16[528,128]{1,0:T(8,128)(2,1)S(1)}, s16[528,128]{1,0:T(8,128)(2,1)S(1)}, u32[]{:S(2)}, u32[]{:S(2)}) collective-permute-start(s16[528,128]{1,0:T(8,128)(2,1)S(1)} %get-tuple-element.54), channel_id=1, source_target_pairs={{0,1},{1,0},{2,3},{3,2},{4,5},{5,4},{6,7},{7,6},{8,9},{9,8},{10,11... | collective-permute-start | bytes 405512 | tf_op jit(solution)/shard_map/ppermute | solution.py:428
  66.2 0.7 collective-permute-start.15
  66.9 1.7 %collective-permute-start.16 = (s16[528,128]{1,0:T(8,128)(2,1)S(1)}, s16[528,128]{1,0:T(8,128)(2,1)S(1)}, u32[]{:S(2)}, u32[]{:S(2)}) collective-permute-start(s16[528,128]{1,0:T(8,128)(2,1)S(1)} %get-tuple-element.56), channel_id=1, source_target_pairs={{0,3},{1,2},{2,1},{3,0},{4,7},{5,6},{6,5},{7,4},{8,11},{9,10},{10,... | collective-permute-start | bytes 405512 | tf_op jit(solution)/shard_map/ppermute | solution.py:428
  68.6 0.1 pad_add_fusion.me_ref
  68.7 0.0 copy-done.2
  68.7 0.1 pad_maximum_fusion.wide_ref
  68.8 0.6 base.3.base_ref
  69.4 0.8 %finish.2.rest_3_ = f32[256,512]{1,0:T(8,128)} custom-call(f32[256,256]{1,0:T(8,128)S(1)} %base.3.base_ref, s16[528,128]{1,0:T(8,128)(2,1)S(1)} %collective-permute-done.8.rest_0_, s16[528,128]{1,0:T(8,128)(2,1)S(1)} %collective-permute-done.9.rest_1_, s16[528,128]{1,0:T(8,128)(2,1)S(1)} %collective-permute-done.10.rest_2_), custom_call_target="tpu_custom_call" | custom-call | tf_op jit(solution)/shard_map/finish/pallas_call | solution.py:440
  70.3 0.6 base.2.base_ref
  70.9 0.9 %collective-permute-done.14.rest_0_ = s16[528,128]{1,0:T(8,128)(2,1)S(1)} collective-permute-done((s16[528,128]{1,0:T(8,128)(2,1)S(1)}, s16[528,128]{1,0:T(8,128)(2,1)S(1)}, u32[]{:S(2)}, u32[]{:S(2)}) %collective-permute-start.14) | collective-permute-done | bytes 135200 | tf_op jit(solution)/shard_map/ppermute | solution.py:428
  71.8 4.8 %collective-permute-done.15.rest_1_ = s16[528,128]{1,0:T(8,128)(2,1)S(1)} collective-permute-done((s16[528,128]{1,0:T(8,128)(2,1)S(1)}, s16[528,128]{1,0:T(8,128)(2,1)S(1)}, u32[]{:S(2)}, u32[]{:S(2)}) %collective-permute-start.15) | collective-permute-done | bytes 135200 | tf_op jit(solution)/shard_map/ppermute | solution.py:428
  76.6 0.0 collective-permute-done.16.rest_2_
  76.6 0.8 %finish.3 = f32[256,512]{1,0:T(8,128)} custom-call(f32[256,256]{1,0:T(8,128)S(1)} %base.2.base_ref, s16[528,128]{1,0:T(8,128)(2,1)S(1)} %collective-permute-done.14.rest_0_, s16[528,128]{1,0:T(8,128)(2,1)S(1)} %collective-permute-done.15.rest_1_, s16[528,128]{1,0:T(8,128)(2,1)S(1)} %collective-permute-done.16.rest_2_, ...), custom_call_target="tpu_custom_call", output_to_operand_aliasing={{}: (4, {})} | custom-call | tf_op jit(solution)/shard_map/finish/pallas_call | solution.py:440
  (2 shorter events, 0.0 us)
Async XLA Ops:
  0.0 5.3 %collective-permute-start.1 = (bf16[2,16,64,384]{3,2,1,0:T(8,128)(2,1)}, bf16[2,16,64,384]{3,2,1,0:T(8,128)(2,1)S(1)}, u32[]{:S(2)}, u32[]{:S(2)}) collective-permute-start(bf16[2,16,64,384]{3,2,1,0:T(8,128)(2,1)} %pan_ref.1), channel_id=1, source_target_pairs={{0,4},{4,0},{8,12},{12,8},{16,20},{20,16},{24,28},{28,24},{1,5},{5... | collective-permute-start | bytes 4718600 | tf_op jit(solution)/shard_map/ppermute | solution.py:320
  1.2 4.0 %collective-permute-start = (s32[2,16]{1,0:T(2,128)S(1)}, s32[2,16]{1,0:T(2,128)S(1)}, u32[]{:S(2)}, u32[]{:S(2)}) collective-permute-start(s32[2,16]{1,0:T(2,128)S(1)} %get-tuple-element.58), channel_id=1, source_target_pairs={{0,4},{4,0},{8,12},{12,8},{16,20},{20,16},{24,28},{28,24},{1,5},{5... | collective-permute-start | bytes 392 | tf_op jit(solution)/shard_map/ppermute | solution.py:320
  1.3 4.0 %collective-permute-start.2 = (f32[3,3,256]{2,1,0:T(4,128)}, f32[3,3,256]{2,1,0:T(4,128)S(1)}, u32[]{:S(2)}, u32[]{:S(2)}) collective-permute-start(f32[3,3,256]{2,1,0:T(4,128)} %cur_ref.1), channel_id=1, source_target_pairs={{0,4},{4,0},{8,12},{12,8},{16,20},{20,16},{24,28},{28,24},{1,5},{5... | collective-permute-start | bytes 27656 | tf_op jit(solution)/shard_map/ppermute | solution.py:320
  1.9 1.4 %copy-start = (bf16[2,16,64,384]{3,2,1,0:T(8,128)(2,1)S(1)}, bf16[2,16,64,384]{3,2,1,0:T(8,128)(2,1)}, u32[]{:S(2)}) copy-start(bf16[2,16,64,384]{3,2,1,0:T(8,128)(2,1)} %pan_ref.1) | copy-start | bytes 4718596
  3.3 0.7 copy-start.1
  10.6 15.3 %collective-permute-start.5 = (s16[528,512]{1,0:T(8,128)(2,1)S(1)}, s16[528,512]{1,0:T(8,128)(2,1)S(1)}, u32[]{:S(2)}, u32[]{:S(2)}) collective-permute-start(s16[528,512]{1,0:T(8,128)(2,1)S(1)} %get-tuple-element.34), channel_id=1, source_target_pairs={{0,16},{4,20},{8,24},{12,28},{16,0},{20,4},{24,8},{28,12},{1,17},{... | collective-permute-start | bytes 1622024 | tf_op jit(solution)/shard_map/ppermute | solution.py:320
  13.8 14.8 %collective-permute-start.3 = (s16[528,512]{1,0:T(8,128)(2,1)S(1)}, s16[528,512]{1,0:T(8,128)(2,1)S(1)}, u32[]{:S(2)}, u32[]{:S(2)}) collective-permute-start(s16[528,512]{1,0:T(8,128)(2,1)S(1)} %get-tuple-element.33), channel_id=1, source_target_pairs={{0,8},{4,12},{8,0},{12,4},{16,24},{20,28},{24,16},{28,20},{1,9},{5... | collective-permute-start | bytes 1622024 | tf_op jit(solution)/shard_map/ppermute | solution.py:320
  26.1 8.4 %collective-permute-start.6 = (s16[272,512]{1,0:T(8,128)(2,1)S(1)}, s16[272,512]{1,0:T(8,128)(2,1)S(1)}, u32[]{:S(2)}, u32[]{:S(2)}) collective-permute-start(s16[272,512]{1,0:T(8,128)(2,1)S(1)} %relay.5), channel_id=1, source_target_pairs={{0,8},{4,12},{8,0},{12,4},{16,24},{20,28},{24,16},{28,20},{1,9},{5... | collective-permute-start | bytes 835592 | tf_op jit(solution)/shard_map/ppermute | solution.py:320
  28.9 6.7 %collective-permute-start.4 = (s16[272,512]{1,0:T(8,128)(2,1)S(1)}, s16[272,512]{1,0:T(8,128)(2,1)S(1)}, u32[]{:S(2)}, u32[]{:S(2)}) collective-permute-start(s16[272,512]{1,0:T(8,128)(2,1)S(1)} %relay.4), channel_id=1, source_target_pairs={{0,16},{4,20},{8,24},{12,28},{16,0},{20,4},{24,8},{28,12},{1,17},{... | collective-permute-start | bytes 835592 | tf_op jit(solution)/shard_map/ppermute | solution.py:320
  36.0 18.9 %collective-permute-start.7 = (s16[528,512]{1,0:T(8,128)(2,1)S(1)}, s16[528,512]{1,0:T(8,128)(2,1)S(1)}, u32[]{:S(2)}, u32[]{:S(2)}) collective-permute-start(s16[528,512]{1,0:T(8,128)(2,1)S(1)} %get-tuple-element.49), channel_id=1, source_target_pairs={{0,8},{4,12},{8,0},{12,4},{16,24},{20,28},{24,16},{28,20},{1,9},{5... | collective-permute-start | bytes 1622024 | tf_op jit(solution)/shard_map/ppermute | solution.py:320
  36.9 19.4 %collective-permute-start.12 = (s16[528,512]{1,0:T(8,128)(2,1)S(1)}, s16[528,512]{1,0:T(8,128)(2,1)S(1)}, u32[]{:S(2)}, u32[]{:S(2)}) collective-permute-start(s16[528,512]{1,0:T(8,128)(2,1)S(1)} %get-tuple-element.52), channel_id=1, source_target_pairs={{0,16},{4,20},{8,24},{12,28},{16,0},{20,4},{24,8},{28,12},{1,17},{... | collective-permute-start | bytes 1622024 | tf_op jit(solution)/shard_map/ppermute | solution.py:320
  38.1 11.2 %collective-permute-start.8 = (s16[528,128]{1,0:T(8,128)(2,1)S(1)}, s16[528,128]{1,0:T(8,128)(2,1)S(1)}, u32[]{:S(2)}, u32[]{:S(2)}) collective-permute-start(s16[528,128]{1,0:T(8,128)(2,1)S(1)} %get-tuple-element.46), channel_id=1, source_target_pairs={{0,1},{1,0},{2,3},{3,2},{4,5},{5,4},{6,7},{7,6},{8,9},{9,8},{10,11... | collective-permute-start | bytes 405512 | tf_op jit(solution)/shard_map/ppermute | solution.py:428
  42.4 12.5 %collective-permute-start.9 = (s16[528,128]{1,0:T(8,128)(2,1)S(1)}, s16[528,128]{1,0:T(8,128)(2,1)S(1)}, u32[]{:S(2)}, u32[]{:S(2)}) collective-permute-start(s16[528,128]{1,0:T(8,128)(2,1)S(1)} %get-tuple-element.47), channel_id=1, source_target_pairs={{0,2},{1,3},{2,0},{3,1},{4,6},{5,7},{6,4},{7,5},{8,10},{9,11},{10,... | collective-permute-start | bytes 405512 | tf_op jit(solution)/shard_map/ppermute | solution.py:428
  45.6 9.3 %collective-permute-start.10 = (s16[528,128]{1,0:T(8,128)(2,1)S(1)}, s16[528,128]{1,0:T(8,128)(2,1)S(1)}, u32[]{:S(2)}, u32[]{:S(2)}) collective-permute-start(s16[528,128]{1,0:T(8,128)(2,1)S(1)} %get-tuple-element.48), channel_id=1, source_target_pairs={{0,3},{1,2},{2,1},{3,0},{4,7},{5,6},{6,5},{7,4},{8,11},{9,10},{10,... | collective-permute-start | bytes 405512 | tf_op jit(solution)/shard_map/ppermute | solution.py:428
  55.1 6.6 %collective-permute-start.11 = (s16[272,512]{1,0:T(8,128)(2,1)S(1)}, s16[272,512]{1,0:T(8,128)(2,1)S(1)}, u32[]{:S(2)}, u32[]{:S(2)}) collective-permute-start(s16[272,512]{1,0:T(8,128)(2,1)S(1)} %relay.6), channel_id=1, source_target_pairs={{0,16},{4,20},{8,24},{12,28},{16,0},{20,4},{24,8},{28,12},{1,17},{... | collective-permute-start | bytes 835592 | tf_op jit(solution)/shard_map/ppermute | solution.py:320
  56.6 12.1 %copy-start.2 = (f32[4,64,64]{2,1,0:T(8,128)S(1)}, f32[4,64,64]{2,1,0:T(8,128)}, u32[]{:S(2)}) copy-start(f32[4,64,64]{2,1,0:T(8,128)} %param.9) | copy-start | bytes 196612
  56.6 6.6 %collective-permute-start.13 = (s16[272,512]{1,0:T(8,128)(2,1)S(1)}, s16[272,512]{1,0:T(8,128)(2,1)S(1)}, u32[]{:S(2)}, u32[]{:S(2)}) collective-permute-start(s16[272,512]{1,0:T(8,128)(2,1)S(1)} %relay.7), channel_id=1, source_target_pairs={{0,8},{4,12},{8,0},{12,4},{16,24},{20,28},{24,16},{28,20},{1,9},{5... | collective-permute-start | bytes 835592 | tf_op jit(solution)/shard_map/ppermute | solution.py:320
  63.7 8.2 %collective-permute-start.14 = (s16[528,128]{1,0:T(8,128)(2,1)S(1)}, s16[528,128]{1,0:T(8,128)(2,1)S(1)}, u32[]{:S(2)}, u32[]{:S(2)}) collective-permute-start(s16[528,128]{1,0:T(8,128)(2,1)S(1)} %get-tuple-element.54), channel_id=1, source_target_pairs={{0,1},{1,0},{2,3},{3,2},{4,5},{5,4},{6,7},{7,6},{8,9},{9,8},{10,11... | collective-permute-start | bytes 405512 | tf_op jit(solution)/shard_map/ppermute | solution.py:428
  66.2 10.5 %collective-permute-start.15 = (s16[528,128]{1,0:T(8,128)(2,1)S(1)}, s16[528,128]{1,0:T(8,128)(2,1)S(1)}, u32[]{:S(2)}, u32[]{:S(2)}) collective-permute-start(s16[528,128]{1,0:T(8,128)(2,1)S(1)} %get-tuple-element.55), channel_id=1, source_target_pairs={{0,2},{1,3},{2,0},{3,1},{4,6},{5,7},{6,4},{7,5},{8,10},{9,11},{10,... | collective-permute-start | bytes 405512 | tf_op jit(solution)/shard_map/ppermute | solution.py:428
  66.9 9.8 %collective-permute-start.16 = (s16[528,128]{1,0:T(8,128)(2,1)S(1)}, s16[528,128]{1,0:T(8,128)(2,1)S(1)}, u32[]{:S(2)}, u32[]{:S(2)}) collective-permute-start(s16[528,128]{1,0:T(8,128)(2,1)S(1)} %get-tuple-element.56), channel_id=1, source_target_pairs={{0,3},{1,2},{2,1},{3,0},{4,7},{5,6},{6,5},{7,4},{8,11},{9,10},{10,... | collective-permute-start | bytes 405512 | tf_op jit(solution)/shard_map/ppermute | solution.py:428

commit v7 on v3

--- a/solution.py
+++ b/solution.py
@@ -116,22 +116,6 @@
         return carry
 
     lax.fori_loop(0, rows.shape[1] // (row_blocks * CB), one_group, 0)
-
-
-def form_own_kernel(plan, table, pan_ref, cur_ref, rows, pan, cur, pan_sem, cur_sem):
-    tiles = rows.shape[0]
-    copies = [
-        pltpu.make_async_copy(pan_ref.at[tile], pan.at[tile], pan_sem.at[tile])
-        for tile in range(tiles)
-    ]
-    small = pltpu.make_async_copy(cur_ref, cur, cur_sem)
-    small.start()
-    for copy in copies:
-        copy.start()
-    small.wait()
-    for tile, copy in enumerate(copies):
-        copy.wait()
-        form_tile(plan, table, tile, pan, cur, rows)
 
 
 def form_kernel(plan, table, pan, cur, rows):
@@ -336,28 +320,18 @@
 
     table_a, table_b = table_of(ids), table_of(ids_other)
     formed = jax.ShapeDtypeStruct((tiles, chips * extent, 2 * WIDTH), jnp.bfloat16)
-    whole = pl.BlockSpec(memory_space=pltpu.HBM)
-    rows_a, pan_here = pl.pallas_call(
-        functools.partial(form_own_kernel, (total, row_blocks)),
-        in_specs=[SMEM, whole, whole],
-        out_specs=[VMEM, VMEM],
-        out_shape=[formed, jax.ShapeDtypeStruct(panels.shape, panels.dtype)],
-        scratch_shapes=[
-            pltpu.VMEM(curvature.shape, jnp.float32),
-            pltpu.SemaphoreType.DMA((tiles,)),
-            pltpu.SemaphoreType.DMA,
-        ],
-        compiler_params=PARAMS,
-        name="form_own",
-    )(table_a, panels, curvature)
-    rows_b = pl.pallas_call(
-        functools.partial(form_kernel, (total, row_blocks)),
-        in_specs=[SMEM, VMEM, VMEM],
-        out_specs=VMEM,
-        out_shape=formed,
-        compiler_params=PARAMS,
-        name="form_other",
-    )(table_b, pan_other, cur_other)
+    def form_call(table, pan, cur):
+        return pl.pallas_call(
+            functools.partial(form_kernel, (total, row_blocks)),
+            in_specs=[SMEM, VMEM, VMEM],
+            out_specs=VMEM,
+            out_shape=formed,
+            compiler_params=PARAMS,
+            name="form",
+        )(table, pan, cur)
+
+    rows_a = form_call(table_a, panels, curvature)
+    rows_b = form_call(table_b, pan_other, cur_other)
 
     def round_call(sending, turn, tables):
         if sending:
@@ -379,7 +353,7 @@
             ],
             compiler_params=PARAMS,
             name="send" if sending else "keep",
-        )(*tables, pan_here, pan_other, rows_a, rows_b)
+        )(*tables, panels, pan_other, rows_a, rows_b)
 
     tables = (table_a, table_b)
     sends, keeps = [], []

time: 77.9 us -> 76.9 us (0.987); the launches traced: 77.8 us -> 75.4 us
  starting transfers between devices: 24.9 us -> 20.9 us
  waiting for transfers between devices: 25.1 us -> 28.1 us
  Pallas kernels: 24.3 us -> 22.7 us
    ppermute x6, starting transfers between devices: 12.8 us -> 9.42 us  [body(): lax.ppermute(value, 'cam', [(i, i ^ pos + 1) for i in range(n_cam)])]
    ppermute x11, waiting for transfers between devices: 15 us -> 17.4 us  [swap(): return lax.ppermute(value, 'lm', [(i, i ^ 1 << bit) for i in range(n_lm)])]
    pallas_call x4, Pallas kernels: 16.8 us -> 15.6 us  [round_call(): pl.pallas_call(functools.partial(round_kernel, plan), in_specs=[SMEM] * 2...]
    unnamed x6 -> x8, local copies, waits for them, and re-layouts: 2.12 us -> 2.21 us
  transfers between devices with their start and end apart: 17 -> 17, of which waited for: 8 -> 8; matrix products, arithmetic and copies ran while one was open for 2% -> 2% of each run, Pallas kernels for 17% -> 14%
where the time goes in v7:
time: 76.9 us; the launch traced here: 75.4 us
  waiting for transfers between devices  28.1 us (37%)
  Pallas kernels  22.7 us (30%)
  starting transfers between devices  20.9 us (27%)
  local copies, waits for them, and re-layouts  2.21 us (3%)
  other arithmetic  1.18 us (2%)
    ppermute x11, waiting for transfers between devices, swap(): return lax.ppermute(value, 'lm', [(i, i ^ 1 << bit) for i in range(n_lm)])  17.4 us
    pallas_call x4, Pallas kernels, round_call(): pl.pallas_call(functools.partial(round_kernel, plan), in_specs=[SMEM] * 2...  15.6 us
    ppermute x11, starting transfers between devices, swap(): return lax.ppermute(value, 'lm', [(i, i ^ 1 << bit) for i in range(n_lm)])  11.5 us
    ppermute x6, waiting for transfers between devices, body(): lax.ppermute(value, 'cam', [(i, i ^ pos + 1) for i in range(n_cam)])  10.8 us
    ppermute x6, starting transfers between devices, body(): lax.ppermute(value, 'cam', [(i, i ^ pos + 1) for i in range(n_cam)])  9.42 us
    pallas_call x2, Pallas kernels, form_call(): pl.pallas_call(functools.partial(form_kernel, (total, row_blocks)), in_sp...  2.32 us
    unnamed x8, local copies, waits for them, and re-layouts  2.21 us
    pallas_call x2, Pallas kernels, body(): pl.pallas_call(functools.partial(finish_kernel, row_blocks, n_cam - 1), g...  1.64 us
  transfers between devices with their start and end apart: 17, of which 8 were waited for; matrix products, arithmetic and copies ran while one was open for 2% of the time, Pallas kernels for 14%

profile of v7, /device:TPU:0, one launch (start us, length us, event | category | flops | bytes accessed | tf_op | source)
XLA Modules:
  0.0 75.4 jit_solution(11492013780744410964)
XLA Ops:
  0.0 0.5 collective-permute-start.1
  0.5 0.8 %fusion.3 = (s32[2,16]{1,0:T(2,128)S(1)}, s32[2,16]{1,0:T(2,128)S(1)}) fusion(s32[]{:T(128)} %axis_index.25, s32[2,16]{1,0:T(2,128)} %param.7, s32[2]{0:T(128)} %param.8), kind=kLoop, calls=%fused_computation.51 | loop fusion | flops 1504 | bytes 396 | tf_op jit(solution)/shard_map/jit(_where)/select_n | solution.py:316
  1.2 0.1 collective-permute-start
  1.3 0.5 collective-permute-start.2
  1.8 0.1 select_reduce_fusion.1.table.table_a
  1.9 0.0 copy-start
  1.9 1.4 %copy-done = bf16[2,16,64,384]{3,2,1,0:T(8,128)(2,1)S(1)} copy-done((bf16[2,16,64,384]{3,2,1,0:T(8,128)(2,1)S(1)}, bf16[2,16,64,384]{3,2,1,0:T(8,128)(2,1)}, u32[]{:S(2)}) %copy-start) | copy-done | bytes 1572888
  3.3 0.0 copy-start.2
  3.3 0.7 copy-done.2
  4.0 1.2 %form.2.rows_a = bf16[2,1024,768]{2,1,0:T(8,128)(2,1)S(1)} custom-call(s32[2,48]{1,0:T(2,128)S(1)} %select_reduce_fusion.1.table.table_a, bf16[2,16,64,384]{3,2,1,0:T(8,128)(2,1)S(1)} %copy-done, f32[3,3,256]{2,1,0:T(4,128)S(1)} %copy-done.2), custom_call_target="tpu_custom_call" | custom-call | tf_op jit(solution)/shard_map/form/pallas_call | solution.py:324
  5.2 0.0 copy-start.1
  5.2 0.0 collective-permute-done
  5.3 0.1 select_reduce_fusion.table.table_b
  5.4 0.0 collective-permute-done.2.cur
  5.4 0.0 collective-permute-done.1.pan.pan_b
  5.4 1.1 %form.3.rows_b = bf16[2,1024,768]{2,1,0:T(8,128)(2,1)S(1)} custom-call(s32[2,48]{1,0:T(2,128)S(1)} %select_reduce_fusion.table.table_b, bf16[2,16,64,384]{3,2,1,0:T(8,128)(2,1)S(1)} %collective-permute-done.1.pan.pan_b, f32[3,3,256]{2,1,0:T(4,128)S(1)} %collective-permute-done.2.cur), custom_call_target="tpu_custom_call" | custom-call | tf_op jit(solution)/shard_map/form/pallas_call | solution.py:324
  6.5 0.1 copy-done.1
  6.6 4.6 %send.2 = (s16[528,512]{1,0:T(8,128)(2,1)S(1)}, s16[528,512]{1,0:T(8,128)(2,1)S(1)}) custom-call(s32[2,48]{1,0:T(2,128)S(1)} %select_reduce_fusion.1.table.table_a, s32[2,48]{1,0:T(2,128)S(1)} %select_reduce_fusion.table.table_b, bf16[2,16,64,384]{3,2,1,0:T(8,128)(2,1)S(1)} %copy-done.1, bf16[2,16,64,384]{3,2,1,0:T(8,128)(2,1)S(1)} %collective-permute-done.1.pan.pan_b, ...), custom_call_target="tpu_custom_call" | custom-call | tf_op jit(solution)/shard_map/send/pallas_call | solution.py:344
  11.2 2.5 %collective-permute-start.5 = (s16[528,512]{1,0:T(8,128)(2,1)S(1)}, s16[528,512]{1,0:T(8,128)(2,1)S(1)}, u32[]{:S(2)}, u32[]{:S(2)}) collective-permute-start(s16[528,512]{1,0:T(8,128)(2,1)S(1)} %get-tuple-element.30), channel_id=1, source_target_pairs={{0,16},{4,20},{8,24},{12,28},{16,0},{20,4},{24,8},{28,12},{1,17},{... | collective-permute-start | bytes 1622024 | tf_op jit(solution)/shard_map/ppermute | solution.py:303
  13.8 1.1 %collective-permute-start.3 = (s16[528,512]{1,0:T(8,128)(2,1)S(1)}, s16[528,512]{1,0:T(8,128)(2,1)S(1)}, u32[]{:S(2)}, u32[]{:S(2)}) collective-permute-start(s16[528,512]{1,0:T(8,128)(2,1)S(1)} %get-tuple-element.29), channel_id=1, source_target_pairs={{0,8},{4,12},{8,0},{12,4},{16,24},{20,28},{24,16},{28,20},{1,9},{5... | collective-permute-start | bytes 1622024 | tf_op jit(solution)/shard_map/ppermute | solution.py:303
  14.8 3.0 %keep.2 = (f32[2,256,512]{2,1,0:T(8,128)S(1)}, f32[2,256,512]{2,1,0:T(8,128)S(1)}) custom-call(s32[2,48]{1,0:T(2,128)S(1)} %select_reduce_fusion.1.table.table_a, s32[2,48]{1,0:T(2,128)S(1)} %select_reduce_fusion.table.table_b, bf16[2,16,64,384]{3,2,1,0:T(8,128)(2,1)S(1)} %copy-done.1, bf16[2,16,64,384]{3,2,1,0:T(8,128)(2,1)S(1)} %collective-permute-done.1.pan.pan_b, ...), custom_call_target="tpu_custom_call" | custom-call | tf_op jit(solution)/shard_map/keep/pallas_call | solution.py:344
  17.8 9.0 %collective-permute-done.5.rest_0_.rest_4_ = s16[528,512]{1,0:T(8,128)(2,1)S(1)} collective-permute-done((s16[528,512]{1,0:T(8,128)(2,1)S(1)}, s16[528,512]{1,0:T(8,128)(2,1)S(1)}, u32[]{:S(2)}, u32[]{:S(2)}) %collective-permute-start.5) | collective-permute-done | bytes 540704 | tf_op jit(solution)/shard_map/ppermute | solution.py:303
  26.8 0.2 relay.5
  27.1 1.9 %collective-permute-start.6 = (s16[272,512]{1,0:T(8,128)(2,1)S(1)}, s16[272,512]{1,0:T(8,128)(2,1)S(1)}, u32[]{:S(2)}, u32[]{:S(2)}) collective-permute-start(s16[272,512]{1,0:T(8,128)(2,1)S(1)} %relay.5), channel_id=1, source_target_pairs={{0,8},{4,12},{8,0},{12,4},{16,24},{20,28},{24,16},{28,20},{1,9},{5... | collective-permute-start | bytes 835592 | tf_op jit(solution)/shard_map/ppermute | solution.py:303
  29.0 0.0 collective-permute-done.3.rest_0_.rest_1_
  29.0 0.2 relay.4
  29.3 0.9 %collective-permute-start.4 = (s16[272,512]{1,0:T(8,128)(2,1)S(1)}, s16[272,512]{1,0:T(8,128)(2,1)S(1)}, u32[]{:S(2)}, u32[]{:S(2)}) collective-permute-start(s16[272,512]{1,0:T(8,128)(2,1)S(1)} %relay.4), channel_id=1, source_target_pairs={{0,16},{4,20},{8,24},{12,28},{16,0},{20,4},{24,8},{28,12},{1,17},{... | collective-permute-start | bytes 835592 | tf_op jit(solution)/shard_map/ppermute | solution.py:303
  30.2 4.6 %send.3 = (s16[528,512]{1,0:T(8,128)(2,1)S(1)}, s16[528,512]{1,0:T(8,128)(2,1)S(1)}) custom-call(s32[2,48]{1,0:T(2,128)S(1)} %select_reduce_fusion.1.table.table_a, s32[2,48]{1,0:T(2,128)S(1)} %select_reduce_fusion.table.table_b, bf16[2,16,64,384]{3,2,1,0:T(8,128)(2,1)S(1)} %copy-done.1, bf16[2,16,64,384]{3,2,1,0:T(8,128)(2,1)S(1)} %collective-permute-done.1.pan.pan_b, ...), custom_call_target="tpu_custom_call" | custom-call | tf_op jit(solution)/shard_map/send/pallas_call | solution.py:344
  34.8 1.1 %collective-permute-done.6.rest_5_ = s16[272,512]{1,0:T(8,128)(2,1)S(1)} collective-permute-done((s16[272,512]{1,0:T(8,128)(2,1)S(1)}, s16[272,512]{1,0:T(8,128)(2,1)S(1)}, u32[]{:S(2)}, u32[]{:S(2)}) %collective-permute-start.6) | collective-permute-done | bytes 278560 | tf_op jit(solution)/shard_map/ppermute | solution.py:303
  35.9 1.4 %collective-permute-done.4.rest_2_ = s16[272,512]{1,0:T(8,128)(2,1)S(1)} collective-permute-done((s16[272,512]{1,0:T(8,128)(2,1)S(1)}, s16[272,512]{1,0:T(8,128)(2,1)S(1)}, u32[]{:S(2)}, u32[]{:S(2)}) %collective-permute-start.4) | collective-permute-done | bytes 278560 | tf_op jit(solution)/shard_map/ppermute | solution.py:303
  37.3 0.5 cross.2
  37.7 1.6 %collective-permute-start.7 = (s16[528,512]{1,0:T(8,128)(2,1)S(1)}, s16[528,512]{1,0:T(8,128)(2,1)S(1)}, u32[]{:S(2)}, u32[]{:S(2)}) collective-permute-start(s16[528,512]{1,0:T(8,128)(2,1)S(1)} %get-tuple-element.45), channel_id=1, source_target_pairs={{0,8},{4,12},{8,0},{12,4},{16,24},{20,28},{24,16},{28,20},{1,9},{5... | collective-permute-start | bytes 1622024 | tf_op jit(solution)/shard_map/ppermute | solution.py:303
  39.3 0.6 collective-permute-start.12
  39.9 1.4 %collective-permute-start.8 = (s16[528,128]{1,0:T(8,128)(2,1)S(1)}, s16[528,128]{1,0:T(8,128)(2,1)S(1)}, u32[]{:S(2)}, u32[]{:S(2)}) collective-permute-start(s16[528,128]{1,0:T(8,128)(2,1)S(1)} %get-tuple-element.42), channel_id=1, source_target_pairs={{0,1},{1,0},{2,3},{3,2},{4,5},{5,4},{6,7},{7,6},{8,9},{9,8},{10,11... | collective-permute-start | bytes 405512 | tf_op jit(solution)/shard_map/ppermute | solution.py:401
  41.3 2.3 %collective-permute-start.9 = (s16[528,128]{1,0:T(8,128)(2,1)S(1)}, s16[528,128]{1,0:T(8,128)(2,1)S(1)}, u32[]{:S(2)}, u32[]{:S(2)}) collective-permute-start(s16[528,128]{1,0:T(8,128)(2,1)S(1)} %get-tuple-element.43), channel_id=1, source_target_pairs={{0,2},{1,3},{2,0},{3,1},{4,6},{5,7},{6,4},{7,5},{8,10},{9,11},{10,... | collective-permute-start | bytes 405512 | tf_op jit(solution)/shard_map/ppermute | solution.py:401
  43.6 0.7 collective-permute-start.10
  44.3 3.3 %keep.3 = (f32[2,256,512]{2,1,0:T(8,128)S(1)}, f32[2,256,512]{2,1,0:T(8,128)S(1)}) custom-call(s32[2,48]{1,0:T(2,128)S(1)} %select_reduce_fusion.1.table.table_a, s32[2,48]{1,0:T(2,128)S(1)} %select_reduce_fusion.table.table_b, bf16[2,16,64,384]{3,2,1,0:T(8,128)(2,1)S(1)} %copy-done.1, bf16[2,16,64,384]{3,2,1,0:T(8,128)(2,1)S(1)} %collective-permute-done.1.pan.pan_b, ...), custom_call_target="tpu_custom_call" | custom-call | tf_op jit(solution)/shard_map/keep/pallas_call | solution.py:344
  47.6 0.0 collective-permute-done.8.rest_0_
  47.6 5.2 %collective-permute-done.9.rest_1_ = s16[528,128]{1,0:T(8,128)(2,1)S(1)} collective-permute-done((s16[528,128]{1,0:T(8,128)(2,1)S(1)}, s16[528,128]{1,0:T(8,128)(2,1)S(1)}, u32[]{:S(2)}, u32[]{:S(2)}) %collective-permute-start.9) | collective-permute-done | bytes 135200 | tf_op jit(solution)/shard_map/ppermute | solution.py:401
  52.8 0.0 collective-permute-done.10.rest_2_
  52.8 0.0 collective-permute-done.7.rest_0_.rest_1_
  52.8 0.2 relay.6
  53.1 0.0 copy-start.3
  53.1 1.2 %collective-permute-start.11 = (s16[272,512]{1,0:T(8,128)(2,1)S(1)}, s16[272,512]{1,0:T(8,128)(2,1)S(1)}, u32[]{:S(2)}, u32[]{:S(2)}) collective-permute-start(s16[272,512]{1,0:T(8,128)(2,1)S(1)} %relay.6), channel_id=1, source_target_pairs={{0,16},{4,20},{8,24},{12,28},{16,0},{20,4},{24,8},{28,12},{1,17},{... | collective-permute-start | bytes 835592 | tf_op jit(solution)/shard_map/ppermute | solution.py:303
  54.3 0.0 collective-permute-done.12.rest_0_.rest_4_
  54.3 0.2 relay.7
  54.5 0.7 collective-permute-start.13
  55.3 4.4 %collective-permute-done.11.rest_2_ = s16[272,512]{1,0:T(8,128)(2,1)S(1)} collective-permute-done((s16[272,512]{1,0:T(8,128)(2,1)S(1)}, s16[272,512]{1,0:T(8,128)(2,1)S(1)}, u32[]{:S(2)}, u32[]{:S(2)}) %collective-permute-start.11) | collective-permute-done | bytes 278560 | tf_op jit(solution)/shard_map/ppermute | solution.py:303
  59.7 1.5 %collective-permute-done.13.rest_5_ = s16[272,512]{1,0:T(8,128)(2,1)S(1)} collective-permute-done((s16[272,512]{1,0:T(8,128)(2,1)S(1)}, s16[272,512]{1,0:T(8,128)(2,1)S(1)}, u32[]{:S(2)}, u32[]{:S(2)}) %collective-permute-start.13) | collective-permute-done | bytes 278560 | tf_op jit(solution)/shard_map/ppermute | solution.py:303
  61.2 0.5 cross.3
  61.6 2.6 %collective-permute-start.14 = (s16[528,128]{1,0:T(8,128)(2,1)S(1)}, s16[528,128]{1,0:T(8,128)(2,1)S(1)}, u32[]{:S(2)}, u32[]{:S(2)}) collective-permute-start(s16[528,128]{1,0:T(8,128)(2,1)S(1)} %get-tuple-element.50), channel_id=1, source_target_pairs={{0,1},{1,0},{2,3},{3,2},{4,5},{5,4},{6,7},{7,6},{8,9},{9,8},{10,11... | collective-permute-start | bytes 405512 | tf_op jit(solution)/shard_map/ppermute | solution.py:401
  64.2 0.0 collective-permute-start.15
  64.2 2.4 %collective-permute-start.16 = (s16[528,128]{1,0:T(8,128)(2,1)S(1)}, s16[528,128]{1,0:T(8,128)(2,1)S(1)}, u32[]{:S(2)}, u32[]{:S(2)}) collective-permute-start(s16[528,128]{1,0:T(8,128)(2,1)S(1)} %get-tuple-element.52), channel_id=1, source_target_pairs={{0,3},{1,2},{2,1},{3,0},{4,7},{5,6},{6,5},{7,4},{8,11},{9,10},{10,... | collective-permute-start | bytes 405512 | tf_op jit(solution)/shard_map/ppermute | solution.py:401
  66.7 0.1 pad_add_fusion.me_ref
  66.7 0.0 copy-done.3
  66.7 0.1 pad_maximum_fusion.wide_ref
  66.9 0.6 base.3.base_ref
  67.5 0.8 %finish.2.rest_3_ = f32[256,512]{1,0:T(8,128)} custom-call(f32[256,256]{1,0:T(8,128)S(1)} %base.3.base_ref, s16[528,128]{1,0:T(8,128)(2,1)S(1)} %collective-permute-done.8.rest_0_, s16[528,128]{1,0:T(8,128)(2,1)S(1)} %collective-permute-done.9.rest_1_, s16[528,128]{1,0:T(8,128)(2,1)S(1)} %collective-permute-done.10.rest_2_), custom_call_target="tpu_custom_call" | custom-call | tf_op jit(solution)/shard_map/finish/pallas_call | solution.py:413
  68.3 0.6 base.2.base_ref
  69.0 1.2 %collective-permute-done.14.rest_0_ = s16[528,128]{1,0:T(8,128)(2,1)S(1)} collective-permute-done((s16[528,128]{1,0:T(8,128)(2,1)S(1)}, s16[528,128]{1,0:T(8,128)(2,1)S(1)}, u32[]{:S(2)}, u32[]{:S(2)}) %collective-permute-start.14) | collective-permute-done | bytes 135200 | tf_op jit(solution)/shard_map/ppermute | solution.py:401
  70.1 4.4 %collective-permute-done.15.rest_1_ = s16[528,128]{1,0:T(8,128)(2,1)S(1)} collective-permute-done((s16[528,128]{1,0:T(8,128)(2,1)S(1)}, s16[528,128]{1,0:T(8,128)(2,1)S(1)}, u32[]{:S(2)}, u32[]{:S(2)}) %collective-permute-start.15) | collective-permute-done | bytes 135200 | tf_op jit(solution)/shard_map/ppermute | solution.py:401
  74.5 0.0 collective-permute-done.16.rest_2_
  74.6 0.8 %finish.3 = f32[256,512]{1,0:T(8,128)} custom-call(f32[256,256]{1,0:T(8,128)S(1)} %base.2.base_ref, s16[528,128]{1,0:T(8,128)(2,1)S(1)} %collective-permute-done.14.rest_0_, s16[528,128]{1,0:T(8,128)(2,1)S(1)} %collective-permute-done.15.rest_1_, s16[528,128]{1,0:T(8,128)(2,1)S(1)} %collective-permute-done.16.rest_2_, ...), custom_call_target="tpu_custom_call", output_to_operand_aliasing={{}: (4, {})} | custom-call | tf_op jit(solution)/shard_map/finish/pallas_call | solution.py:413
  (2 shorter events, 0.0 us)
Async XLA Ops:
  0.0 5.4 %collective-permute-start.1 = (bf16[2,16,64,384]{3,2,1,0:T(8,128)(2,1)}, bf16[2,16,64,384]{3,2,1,0:T(8,128)(2,1)S(1)}, u32[]{:S(2)}, u32[]{:S(2)}) collective-permute-start(bf16[2,16,64,384]{3,2,1,0:T(8,128)(2,1)} %pan_a.7), channel_id=1, source_target_pairs={{0,4},{4,0},{8,12},{12,8},{16,20},{20,16},{24,28},{28,24},{1,5},{5... | collective-permute-start | bytes 4718600 | tf_op jit(solution)/shard_map/ppermute | solution.py:303
  1.2 4.0 %collective-permute-start = (s32[2,16]{1,0:T(2,128)S(1)}, s32[2,16]{1,0:T(2,128)S(1)}, u32[]{:S(2)}, u32[]{:S(2)}) collective-permute-start(s32[2,16]{1,0:T(2,128)S(1)} %get-tuple-element.54), channel_id=1, source_target_pairs={{0,4},{4,0},{8,12},{12,8},{16,20},{20,16},{24,28},{28,24},{1,5},{5... | collective-permute-start | bytes 392 | tf_op jit(solution)/shard_map/ppermute | solution.py:303
  1.3 4.0 %collective-permute-start.2 = (f32[3,3,256]{2,1,0:T(4,128)}, f32[3,3,256]{2,1,0:T(4,128)S(1)}, u32[]{:S(2)}, u32[]{:S(2)}) collective-permute-start(f32[3,3,256]{2,1,0:T(4,128)} %cur.1), channel_id=1, source_target_pairs={{0,4},{4,0},{8,12},{12,8},{16,20},{20,16},{24,28},{28,24},{1,5},{5... | collective-permute-start | bytes 27656 | tf_op jit(solution)/shard_map/ppermute | solution.py:303
  1.9 1.4 %copy-start = (bf16[2,16,64,384]{3,2,1,0:T(8,128)(2,1)S(1)}, bf16[2,16,64,384]{3,2,1,0:T(8,128)(2,1)}, u32[]{:S(2)}) copy-start(bf16[2,16,64,384]{3,2,1,0:T(8,128)(2,1)} %pan_a.7) | copy-start | bytes 4718596
  3.3 0.7 copy-start.2
  5.2 1.4 %copy-start.1 = (bf16[2,16,64,384]{3,2,1,0:T(8,128)(2,1)S(1)}, bf16[2,16,64,384]{3,2,1,0:T(8,128)(2,1)}, u32[]{:S(2)}) copy-start(bf16[2,16,64,384]{3,2,1,0:T(8,128)(2,1)} %pan_a.7) | copy-start | bytes 4718596
  11.2 15.6 %collective-permute-start.5 = (s16[528,512]{1,0:T(8,128)(2,1)S(1)}, s16[528,512]{1,0:T(8,128)(2,1)S(1)}, u32[]{:S(2)}, u32[]{:S(2)}) collective-permute-start(s16[528,512]{1,0:T(8,128)(2,1)S(1)} %get-tuple-element.30), channel_id=1, source_target_pairs={{0,16},{4,20},{8,24},{12,28},{16,0},{20,4},{24,8},{28,12},{1,17},{... | collective-permute-start | bytes 1622024 | tf_op jit(solution)/shard_map/ppermute | solution.py:303
  13.8 15.3 %collective-permute-start.3 = (s16[528,512]{1,0:T(8,128)(2,1)S(1)}, s16[528,512]{1,0:T(8,128)(2,1)S(1)}, u32[]{:S(2)}, u32[]{:S(2)}) collective-permute-start(s16[528,512]{1,0:T(8,128)(2,1)S(1)} %get-tuple-element.29), channel_id=1, source_target_pairs={{0,8},{4,12},{8,0},{12,4},{16,24},{20,28},{24,16},{28,20},{1,9},{5... | collective-permute-start | bytes 1622024 | tf_op jit(solution)/shard_map/ppermute | solution.py:303
  27.1 8.8 %collective-permute-start.6 = (s16[272,512]{1,0:T(8,128)(2,1)S(1)}, s16[272,512]{1,0:T(8,128)(2,1)S(1)}, u32[]{:S(2)}, u32[]{:S(2)}) collective-permute-start(s16[272,512]{1,0:T(8,128)(2,1)S(1)} %relay.5), channel_id=1, source_target_pairs={{0,8},{4,12},{8,0},{12,4},{16,24},{20,28},{24,16},{28,20},{1,9},{5... | collective-permute-start | bytes 835592 | tf_op jit(solution)/shard_map/ppermute | solution.py:303
  29.3 8.0 %collective-permute-start.4 = (s16[272,512]{1,0:T(8,128)(2,1)S(1)}, s16[272,512]{1,0:T(8,128)(2,1)S(1)}, u32[]{:S(2)}, u32[]{:S(2)}) collective-permute-start(s16[272,512]{1,0:T(8,128)(2,1)S(1)} %relay.4), channel_id=1, source_target_pairs={{0,16},{4,20},{8,24},{12,28},{16,0},{20,4},{24,8},{28,12},{1,17},{... | collective-permute-start | bytes 835592 | tf_op jit(solution)/shard_map/ppermute | solution.py:303
  37.7 15.1 %collective-permute-start.7 = (s16[528,512]{1,0:T(8,128)(2,1)S(1)}, s16[528,512]{1,0:T(8,128)(2,1)S(1)}, u32[]{:S(2)}, u32[]{:S(2)}) collective-permute-start(s16[528,512]{1,0:T(8,128)(2,1)S(1)} %get-tuple-element.45), channel_id=1, source_target_pairs={{0,8},{4,12},{8,0},{12,4},{16,24},{20,28},{24,16},{28,20},{1,9},{5... | collective-permute-start | bytes 1622024 | tf_op jit(solution)/shard_map/ppermute | solution.py:303
  39.3 15.0 %collective-permute-start.12 = (s16[528,512]{1,0:T(8,128)(2,1)S(1)}, s16[528,512]{1,0:T(8,128)(2,1)S(1)}, u32[]{:S(2)}, u32[]{:S(2)}) collective-permute-start(s16[528,512]{1,0:T(8,128)(2,1)S(1)} %get-tuple-element.48), channel_id=1, source_target_pairs={{0,16},{4,20},{8,24},{12,28},{16,0},{20,4},{24,8},{28,12},{1,17},{... | collective-permute-start | bytes 1622024 | tf_op jit(solution)/shard_map/ppermute | solution.py:303
  39.9 7.7 %collective-permute-start.8 = (s16[528,128]{1,0:T(8,128)(2,1)S(1)}, s16[528,128]{1,0:T(8,128)(2,1)S(1)}, u32[]{:S(2)}, u32[]{:S(2)}) collective-permute-start(s16[528,128]{1,0:T(8,128)(2,1)S(1)} %get-tuple-element.42), channel_id=1, source_target_pairs={{0,1},{1,0},{2,3},{3,2},{4,5},{5,4},{6,7},{7,6},{8,9},{9,8},{10,11... | collective-permute-start | bytes 405512 | tf_op jit(solution)/shard_map/ppermute | solution.py:401
  41.3 11.5 %collective-permute-start.9 = (s16[528,128]{1,0:T(8,128)(2,1)S(1)}, s16[528,128]{1,0:T(8,128)(2,1)S(1)}, u32[]{:S(2)}, u32[]{:S(2)}) collective-permute-start(s16[528,128]{1,0:T(8,128)(2,1)S(1)} %get-tuple-element.43), channel_id=1, source_target_pairs={{0,2},{1,3},{2,0},{3,1},{4,6},{5,7},{6,4},{7,5},{8,10},{9,11},{10,... | collective-permute-start | bytes 405512 | tf_op jit(solution)/shard_map/ppermute | solution.py:401
  43.6 9.2 %collective-permute-start.10 = (s16[528,128]{1,0:T(8,128)(2,1)S(1)}, s16[528,128]{1,0:T(8,128)(2,1)S(1)}, u32[]{:S(2)}, u32[]{:S(2)}) collective-permute-start(s16[528,128]{1,0:T(8,128)(2,1)S(1)} %get-tuple-element.44), channel_id=1, source_target_pairs={{0,3},{1,2},{2,1},{3,0},{4,7},{5,6},{6,5},{7,4},{8,11},{9,10},{10,... | collective-permute-start | bytes 405512 | tf_op jit(solution)/shard_map/ppermute | solution.py:401
  53.1 13.7 %copy-start.3 = (f32[4,64,64]{2,1,0:T(8,128)S(1)}, f32[4,64,64]{2,1,0:T(8,128)}, u32[]{:S(2)}) copy-start(f32[4,64,64]{2,1,0:T(8,128)} %param.9) | copy-start | bytes 196612
  53.1 6.6 %collective-permute-start.11 = (s16[272,512]{1,0:T(8,128)(2,1)S(1)}, s16[272,512]{1,0:T(8,128)(2,1)S(1)}, u32[]{:S(2)}, u32[]{:S(2)}) collective-permute-start(s16[272,512]{1,0:T(8,128)(2,1)S(1)} %relay.6), channel_id=1, source_target_pairs={{0,16},{4,20},{8,24},{12,28},{16,0},{20,4},{24,8},{28,12},{1,17},{... | collective-permute-start | bytes 835592 | tf_op jit(solution)/shard_map/ppermute | solution.py:303
  54.5 6.6 %collective-permute-start.13 = (s16[272,512]{1,0:T(8,128)(2,1)S(1)}, s16[272,512]{1,0:T(8,128)(2,1)S(1)}, u32[]{:S(2)}, u32[]{:S(2)}) collective-permute-start(s16[272,512]{1,0:T(8,128)(2,1)S(1)} %relay.7), channel_id=1, source_target_pairs={{0,8},{4,12},{8,0},{12,4},{16,24},{20,28},{24,16},{28,20},{1,9},{5... | collective-permute-start | bytes 835592 | tf_op jit(solution)/shard_map/ppermute | solution.py:303
  61.6 8.5 %collective-permute-start.14 = (s16[528,128]{1,0:T(8,128)(2,1)S(1)}, s16[528,128]{1,0:T(8,128)(2,1)S(1)}, u32[]{:S(2)}, u32[]{:S(2)}) collective-permute-start(s16[528,128]{1,0:T(8,128)(2,1)S(1)} %get-tuple-element.50), channel_id=1, source_target_pairs={{0,1},{1,0},{2,3},{3,2},{4,5},{5,4},{6,7},{7,6},{8,9},{9,8},{10,11... | collective-permute-start | bytes 405512 | tf_op jit(solution)/shard_map/ppermute | solution.py:401
  64.2 10.3 %collective-permute-start.15 = (s16[528,128]{1,0:T(8,128)(2,1)S(1)}, s16[528,128]{1,0:T(8,128)(2,1)S(1)}, u32[]{:S(2)}, u32[]{:S(2)}) collective-permute-start(s16[528,128]{1,0:T(8,128)(2,1)S(1)} %get-tuple-element.51), channel_id=1, source_target_pairs={{0,2},{1,3},{2,0},{3,1},{4,6},{5,7},{6,4},{7,5},{8,10},{9,11},{10,... | collective-permute-start | bytes 405512 | tf_op jit(solution)/shard_map/ppermute | solution.py:401
  64.2 10.3 %collective-permute-start.16 = (s16[528,128]{1,0:T(8,128)(2,1)S(1)}, s16[528,128]{1,0:T(8,128)(2,1)S(1)}, u32[]{:S(2)}, u32[]{:S(2)}) collective-permute-start(s16[528,128]{1,0:T(8,128)(2,1)S(1)} %get-tuple-element.52), channel_id=1, source_target_pairs={{0,3},{1,2},{2,1},{3,0},{4,7},{5,6},{6,5},{7,4},{8,11},{9,10},{10,... | collective-permute-start | bytes 405512 | tf_op jit(solution)/shard_map/ppermute | solution.py:401
